TPU v7x, 32 devices: a whole 2x2x4 slice. The times are simulated.
32 devices in a mesh: parts: 2 (over x), gx: 16 (over z, y, core).
Axes of the slice: x: 2, y: 2, z: 4, core: 2. Of those that a mesh axis runs over, the one named last changes fastest.
Arguments:
- salt: float32 [16, 128, 256], P('parts', 'gx'), parts along dimension 0, may hold values from 0 to 1
- recharge: int32 [128, 512], P('gx', 'parts'), parts along dimension 1, may hold values 0 or 1
- conductivity: float32 [16, 64, 32], P('parts', 'gx'), parts along dimension 0, may hold values from 0.1 to 10
- codes: int32 [64, 64], P('gx', 'parts'), parts along dimension 1, may hold values from 0 to 2
Outputs:
- tendency: float32 [16, 128, 256], P('parts', 'gx'), parts along dimension 0
- head: float32 [16, 64, 32], P('parts', 'gx'), parts along dimension 0
There are 2 independent parts, one for each index of `parts`. A program takes and returns all parts, laid end to end along the dimension named above; each array names one. Nothing has to cross between parts.
Inputs may be any that keep to these rules, and one draw needn't show every extreme that they name: `codes`: 0 marks inland cells without a boundary, 1 sea cells, 2 river cells.
All inputs are finite; a program needn't handle non-finite values. Where the computation divides by a largest or mean magnitude, that divisor is 1e-20 or more. No bound on the sum of `recharge` on one device may be relied on, other than what follows from the above.
Results may differ from a plain program's by a relative error of at most 0.0003.
Values sent between devices are 32-bit elements; how exact they have to be, the bound alone decides.
No kernel may reach another device: no remote copies, remote signals or barrier semaphores. Data moves between devices by JAX's collectives and lax.ppermute only.
A program may use at most 128 MiB of HBM per device.

v0:
```python
import jax
import jax.numpy as jnp
from jax import lax
from jax.sharding import PartitionSpec as P

CYCLES = 2
SMOOTH = 2
COARSE_SWEEPS = 6


relax_weight = 0.8
vertical_ratio = 0.5
sea_penalty = 2.0
river_penalty = 0.5
river_head = 1.0
recharge_rate = 1.0
courant = 0.45
freshening = 1.0


def padded_2(array, sides, width):
    for axis, dim in sides:
        count, length = (lax.axis_size(axis), array.shape[dim])
        up = [(i, (i + 1) % count) for i in range(count - 1)]
        down = [(j, i) for i, j in up]
        last = lax.slice_in_dim(array, length - width, length, axis=dim)
        first = lax.slice_in_dim(array, 0, width, axis=dim)
        before = lax.ppermute(last, axis, up)
        after = lax.ppermute(first, axis, down)
        array = jnp.concatenate([before, array, after], axis=dim)
    return array


def harmonic(first, second):
    total = first + second
    return 2.0 * first * second / (total + jnp.where(total > 0, 0.0, 1.0))


def coefficients(padded, penalty, vertical_scale):
    inner = padded[:, 1:-1, :]
    y_low = harmonic(inner, padded[:, :-2, :])
    y_high = harmonic(inner, padded[:, 2:, :])
    x_face = harmonic(inner[:, :, :-1], inner[:, :, 1:])
    zero_col = jnp.zeros_like(inner[:, :, :1])
    x_low = jnp.concatenate([zero_col, x_face], axis=2)
    x_high = jnp.concatenate([x_face, zero_col], axis=2)
    z_face = vertical_scale * vertical_ratio * harmonic(inner[:-1], inner[1:])
    zero_layer = jnp.zeros_like(inner[:1])
    z_up = jnp.concatenate([zero_layer, z_face], axis=0)
    z_down = jnp.concatenate([z_face, zero_layer], axis=0)
    top_term = jnp.concatenate([penalty[None], jnp.zeros_like(inner[1:])], axis=0)
    diagonal = x_low + x_high + y_low + y_high + z_up + z_down + top_term
    return (x_low, x_high, y_low, y_high, z_up, z_down, diagonal)


def neighbors(padded):
    center = padded[:, 1:-1, :]
    zero_col = jnp.zeros_like(center[:, :, :1])
    west = jnp.concatenate([zero_col, center[:, :, :-1]], axis=2)
    east = jnp.concatenate([center[:, :, 1:], zero_col], axis=2)
    zero_layer = jnp.zeros_like(center[:1])
    upper = jnp.concatenate([zero_layer, center[:-1]], axis=0)
    lower = jnp.concatenate([center[1:], zero_layer], axis=0)
    return (center, west, east, padded[:, :-2, :], padded[:, 2:, :], upper, lower)


def apply_operator(padded, coeffs):
    center, west, east, south, north, upper, lower = neighbors(padded)
    x_low, x_high, y_low, y_high, z_up, z_down, diagonal = coeffs
    return (
        diagonal * center
        - x_low * west
        - x_high * east
        - y_low * south
        - y_high * north
        - z_up * upper
        - z_down * lower
    )


def relax(padded, coeffs, right_side):
    return (
        padded[:, 1:-1, :]
        + relax_weight * (right_side - apply_operator(padded, coeffs)) / coeffs[6]
    )


def block_mean(field):
    leading = field.shape[:-2]
    count_a, count_b = field.shape[-2:]
    grouped = field.reshape(leading + (count_a // 4, 4, count_b // 4, 4))
    return jnp.sum(grouped, axis=(-3, -1)) * 0.0625


def pair_sum(field):
    leading = field.shape[:-2]
    count_a, count_b = field.shape[-2:]
    grouped = field.reshape(leading + (count_a // 2, 2, count_b // 2, 2))
    return jnp.sum(grouped, axis=(-3, -1))


def upsample(field, factor):
    return jnp.repeat(jnp.repeat(field, factor, axis=-2), factor, axis=-1)


def minmod(first, second):
    return 0.5 * (jnp.sign(first) + jnp.sign(second)) * jnp.minimum(jnp.abs(first), jnp.abs(second))


def portion(field, start, stop, axis):
    return lax.slice_in_dim(field, start, stop, axis=axis)


def divergence(cells, speed, axis):
    length = cells.shape[axis]
    widths = [(0, 0)] * cells.ndim
    widths[axis] = (1, 1)
    padded = jnp.pad(cells, widths)
    steps_diff = portion(padded, 1, length + 2, axis) - portion(padded, 0, length + 1, axis)
    slope = minmod(portion(steps_diff, 0, length, axis), portion(steps_diff, 1, length + 1, axis))
    faces = 0.5 * (portion(speed, 0, length - 1, axis) + portion(speed, 1, length, axis))
    left = portion(cells, 0, length - 1, axis) + 0.5 * portion(slope, 0, length - 1, axis)
    right = portion(cells, 1, length, axis) - 0.5 * portion(slope, 1, length, axis)
    flux = jnp.pad(faces * jnp.where(faces > 0, left, right), widths)
    return portion(flux, 1, length + 1, axis) - portion(flux, 0, length, axis)


def divergence_x(extended, faces):
    steps_diff = extended[:, 1:] - extended[:, :-1]
    slope = minmod(steps_diff[:, :-1], steps_diff[:, 1:])
    cells = extended[:, 1:-1]
    left = cells[:, :-1] + 0.5 * slope[:, :-1]
    right = cells[:, 1:] - 0.5 * slope[:, 1:]
    flux = faces * jnp.where(faces > 0, left, right)
    return flux[:, 1:] - flux[:, :-1]


def velocities(padded, coeffs, above, below):
    center, west, east, south, north, upper, lower = neighbors(padded)
    x_low, x_high, y_low, y_high, z_up, z_down, diagonal = coeffs
    vel_x = 0.5 * (x_low * (west - center) + x_high * (center - east))
    vel_y = 0.5 * (y_low * (south - center) + y_high * (center - north))
    vel_z = 0.5 * (z_up * (upper - center + above) + z_down * (center - lower + below))
    return (vel_z, vel_x, vel_y)


def buoyancy_terms(salt_coarse):
    face_salt = 0.5 * (salt_coarse[:-1] + salt_coarse[1:])
    zero_layer = jnp.zeros_like(salt_coarse[:1])
    above = jnp.concatenate([zero_layer, face_salt], axis=0)
    below = jnp.concatenate([face_salt, zero_layer], axis=0)
    return (above, below)


def boundary_penalty(codes):
    return jnp.where(codes == 1, sea_penalty, 0.0) + jnp.where(codes == 2, river_penalty, 0.0)


def source_terms(coeffs, above, below, recharge_frac, codes):
    top_source = recharge_rate * recharge_frac + river_head * jnp.where(
        codes == 2, river_penalty, 0.0
    )
    surface = jnp.concatenate([top_source[None], jnp.zeros_like(above[1:])], axis=0)
    return coeffs[4] * above - coeffs[5] * below + surface


def local(salt, recharge, conductivity, codes):
    layers = salt.shape[0]
    tile = salt.shape[1]
    wet = recharge.astype(jnp.float32)
    blocks = jnp.concatenate([block_mean(salt), block_mean(wet)[None]], axis=0)
    owned = lax.all_to_all(
        jnp.transpose(blocks, (0, 2, 1)), "gx", split_axis=1, concat_axis=2, tiled=True
    )
    salt_coarse = owned[:layers]
    recharge_frac = owned[layers]
    penalty = boundary_penalty(codes)
    cond_padded = padded_2(conductivity, (("gx", 1),), 1)
    coeffs = coefficients(cond_padded, penalty, 1.0)
    above, below = buoyancy_terms(salt_coarse)
    right_side = source_terms(coeffs, above, below, recharge_frac, codes)
    coarse_cond = 0.25 * pair_sum(conductivity)
    coarse_pen = pair_sum(penalty)
    coarse_padded = padded_2(coarse_cond, (("gx", 1),), 1)
    coarse_coeffs = coefficients(coarse_padded, coarse_pen, 4.0)

    def smooth(current):
        padded = padded_2(current, (("gx", 1),), 1)
        return relax(padded, coeffs, right_side)

    head = jnp.zeros_like(conductivity)
    for cycle_no in range(CYCLES):
        for sweep in range(SMOOTH):
            head = smooth(head)
        head_padded = padded_2(head, (("gx", 1),), 1)
        residual = right_side - apply_operator(head_padded, coeffs)
        coarse_resid = pair_sum(residual)
        correction = jnp.zeros_like(coarse_resid)
        for sweep in range(COARSE_SWEEPS):
            corr_padded = padded_2(correction, (("gx", 1),), 1)
            correction = relax(corr_padded, coarse_coeffs, coarse_resid)
        head = head + upsample(correction, 2)
        for sweep in range(SMOOTH):
            head = smooth(head)
    final_padded = padded_2(head, (("gx", 1),), 1)
    vel_z, vel_x, vel_y = velocities(final_padded, coeffs, above, below)
    local_fastest = jnp.max(jnp.abs(vel_x) + jnp.abs(vel_y) + jnp.abs(vel_z))
    fastest = lax.pmax(local_fastest, "gx")
    step = courant / (fastest + 1e-06)
    packed = jnp.stack([vel_z, vel_x, vel_y])
    returned = jnp.transpose(
        lax.all_to_all(packed, "gx", split_axis=3, concat_axis=2, tiled=True), (0, 1, 3, 2)
    )
    fine_x = upsample(returned[1], 4)
    both = padded_2(jnp.stack([salt, fine_x]), (("gx", 2),), 2)
    extended = both[0]
    inner_x = both[1][:, 1:-1]
    faces = 0.5 * (inner_x[:, :-1] + inner_x[:, 1:])
    position = jnp.arange(tile + 1)
    device = lax.axis_index("gx")
    final_device = lax.axis_size("gx") - 1
    edge = (position == 0) & (device == 0) | (position == tile) & (device == final_device)
    faces = jnp.where(edge[None, :, None], 0.0, faces)
    fine_z = upsample(returned[0], 4)
    fine_y = upsample(returned[2], 4)
    change = (
        divergence(salt, fine_z, 0) + divergence_x(extended, faces) + divergence(salt, fine_y, 2)
    )
    dilution = jnp.concatenate(
        [(freshening * wet * salt[0])[None], jnp.zeros_like(salt[1:])], axis=0
    )
    tendency = -step * change - step * dilution
    return (tendency, head)


def solution(mesh):
    return jax.shard_map(
        local,
        mesh=mesh,
        in_specs=(
            P("parts", "gx", None),
            P("gx", "parts"),
            P("parts", "gx", None),
            P("gx", "parts"),
        ),
        out_specs=(P("parts", "gx", None), P("parts", "gx", None)),
        check_vma=False,
    )
```

profile of v0, /device:TPU:0, one launch (start us, length us, event | category | flops | bytes accessed | tf_op | source)
XLA Modules:
  0.0 252.5 jit_solution(7148079121431136107)
XLA Ops:
  0.7 2.4 collective-permute-start.2
  3.0 1.3 collective-permute-start.3
  7.0 9.4 %all-to-all-start = ((f32[9,64,2]{0,2,1:T(2,128)}), f32[9,64,2]{0,2,1:T(2,128)S(1)}, u32[]{:S(2)}, u32[]{:S(2)}) async-start(f32[9,64,2]{0,2,1:T(2,128)} %copy.444), calls=%async_computation | async-start | bytes 131072 | tf_op jit(solution)/shard_map/all_to_all | solution.py:172
  16.5 2.3 collective-permute-start
  18.9 1.3 collective-permute-start.1
  20.2 1.3 collective-permute-start.11
  22.1 1.3 all-to-all-done
  24.8 3.6 %collective-permute-start.10 = (f32[8,1,16]{0,2,1:T(8,128)S(1)}, f32[8,1,16]{0,2,1:T(8,128)S(1)}, u32[]{:S(2)}, u32[]{:S(2)}) collective-permute-start(f32[8,1,16]{0,2,1:T(8,128)S(1)} %broadcast.328), channel_id=1, source_target_pairs={{0,1},{1,2},{2,3},{3,4},{4,5},{5,6},{6,7},{7,8},{8,9},{9,10},{10,1... | collective-permute-start | bytes 1544 | tf_op jit(solution)/shard_map/ppermute | solution.py:28
  28.4 3.6 %collective-permute-start.8 = (f32[8,1,16]{0,2,1:T(8,128)S(1)}, f32[8,1,16]{0,2,1:T(8,128)S(1)}, u32[]{:S(2)}, u32[]{:S(2)}) collective-permute-start(f32[8,1,16]{0,2,1:T(8,128)S(1)} %get-tuple-element.158), channel_id=1, source_target_pairs={{0,1},{1,2},{2,3},{3,4},{4,5},{5,6},{6,7},{7,8},{8,9},{9,10},{10,1... | collective-permute-start | bytes 1544 | tf_op jit(solution)/shard_map/ppermute | solution.py:28
  32.3 1.3 collective-permute-start.5
  33.6 3.0 %collective-permute-start.4 = (f32[8,1,32]{0,2,1:T(8,128)S(1)}, f32[8,1,32]{0,2,1:T(8,128)S(1)}, u32[]{:S(2)}, u32[]{:S(2)}) collective-permute-start(f32[8,1,32]{0,2,1:T(8,128)S(1)} %get-tuple-element.93), channel_id=1, source_target_pairs={{0,1},{1,2},{2,3},{3,4},{4,5},{5,6},{6,7},{7,8},{8,9},{9,10},{10,1... | collective-permute-start | bytes 3080 | tf_op jit(solution)/shard_map/ppermute | solution.py:28
  37.7 1.3 collective-permute-start.7
  39.0 4.5 %collective-permute-start.6 = (f32[8,1,32]{0,2,1:T(8,128)S(1)}, f32[8,1,32]{0,2,1:T(8,128)S(1)}, u32[]{:S(2)}, u32[]{:S(2)}) collective-permute-start(f32[8,1,32]{0,2,1:T(8,128)S(1)} %get-tuple-element.87), channel_id=1, source_target_pairs={{0,1},{1,2},{2,3},{3,4},{4,5},{5,6},{6,7},{7,8},{8,9},{9,10},{10,1... | collective-permute-start | bytes 3080 | tf_op jit(solution)/shard_map/ppermute | solution.py:28
  43.6 1.3 collective-permute-start.9
  45.1 3.3 %collective-permute-done.9 = f32[8,1,16]{0,2,1:T(8,128)S(1)} collective-permute-done((f32[8,1,16]{0,2,1:T(8,128)S(1)}, f32[8,1,16]{0,2,1:T(8,128)S(1)}, u32[]{:S(2)}, u32[]{:S(2)}) %collective-permute-start.9) | collective-permute-done | bytes 544 | tf_op jit(solution)/shard_map/ppermute | solution.py:29
  48.6 1.3 collective-permute-start.13
  49.9 4.9 %collective-permute-start.12 = (f32[8,1,16]{0,2,1:T(8,128)S(1)}, f32[8,1,16]{0,2,1:T(8,128)S(1)}, u32[]{:S(2)}, u32[]{:S(2)}) collective-permute-start(f32[8,1,16]{0,2,1:T(8,128)S(1)} %get-tuple-element.155), channel_id=1, source_target_pairs={{0,1},{1,2},{2,3},{3,4},{4,5},{5,6},{6,7},{7,8},{8,9},{9,10},{10,1... | collective-permute-start | bytes 1544 | tf_op jit(solution)/shard_map/ppermute | solution.py:28
  55.8 1.3 collective-permute-start.15
  57.1 4.2 %collective-permute-start.14 = (f32[8,1,16]{0,2,1:T(8,128)S(1)}, f32[8,1,16]{0,2,1:T(8,128)S(1)}, u32[]{:S(2)}, u32[]{:S(2)}) collective-permute-start(f32[8,1,16]{0,2,1:T(8,128)S(1)} %get-tuple-element.149), channel_id=1, source_target_pairs={{0,1},{1,2},{2,3},{3,4},{4,5},{5,6},{6,7},{7,8},{8,9},{9,10},{10,1... | collective-permute-start | bytes 1544 | tf_op jit(solution)/shard_map/ppermute | solution.py:28
  61.4 0.8 collective-permute-done.14
  62.3 1.3 collective-permute-start.17
  63.6 5.7 %collective-permute-start.16 = (f32[8,1,16]{0,2,1:T(8,128)S(1)}, f32[8,1,16]{0,2,1:T(8,128)S(1)}, u32[]{:S(2)}, u32[]{:S(2)}) collective-permute-start(f32[8,1,16]{0,2,1:T(8,128)S(1)} %get-tuple-element.143), channel_id=1, source_target_pairs={{0,1},{1,2},{2,3},{3,4},{4,5},{5,6},{6,7},{7,8},{8,9},{9,10},{10,1... | collective-permute-start | bytes 1544 | tf_op jit(solution)/shard_map/ppermute | solution.py:28
  70.3 1.3 collective-permute-start.19
  71.6 5.1 %collective-permute-start.18 = (f32[8,1,16]{0,2,1:T(8,128)S(1)}, f32[8,1,16]{0,2,1:T(8,128)S(1)}, u32[]{:S(2)}, u32[]{:S(2)}) collective-permute-start(f32[8,1,16]{0,2,1:T(8,128)S(1)} %get-tuple-element.137), channel_id=1, source_target_pairs={{0,1},{1,2},{2,3},{3,4},{4,5},{5,6},{6,7},{7,8},{8,9},{9,10},{10,1... | collective-permute-start | bytes 1544 | tf_op jit(solution)/shard_map/ppermute | solution.py:28
  77.7 1.3 collective-permute-start.21
  79.0 5.7 %collective-permute-start.20 = (f32[8,1,16]{0,2,1:T(8,128)S(1)}, f32[8,1,16]{0,2,1:T(8,128)S(1)}, u32[]{:S(2)}, u32[]{:S(2)}) collective-permute-start(f32[8,1,16]{0,2,1:T(8,128)S(1)} %get-tuple-element.131), channel_id=1, source_target_pairs={{0,1},{1,2},{2,3},{3,4},{4,5},{5,6},{6,7},{7,8},{8,9},{9,10},{10,1... | collective-permute-start | bytes 1544 | tf_op jit(solution)/shard_map/ppermute | solution.py:28
  85.8 1.3 collective-permute-start.23
  87.1 5.7 %collective-permute-start.22 = (f32[8,1,32]{0,2,1:T(8,128)S(1)}, f32[8,1,32]{0,2,1:T(8,128)S(1)}, u32[]{:S(2)}, u32[]{:S(2)}) collective-permute-start(f32[8,1,32]{0,2,1:T(8,128)S(1)} %get-tuple-element.81), channel_id=1, source_target_pairs={{0,1},{1,2},{2,3},{3,4},{4,5},{5,6},{6,7},{7,8},{8,9},{9,10},{10,1... | collective-permute-start | bytes 3080 | tf_op jit(solution)/shard_map/ppermute | solution.py:28
  92.8 0.8 collective-permute-done.22
  93.8 1.3 collective-permute-start.25
  95.1 5.7 %collective-permute-start.24 = (f32[8,1,32]{0,2,1:T(8,128)S(1)}, f32[8,1,32]{0,2,1:T(8,128)S(1)}, u32[]{:S(2)}, u32[]{:S(2)}) collective-permute-start(f32[8,1,32]{0,2,1:T(8,128)S(1)} %get-tuple-element.75), channel_id=1, source_target_pairs={{0,1},{1,2},{2,3},{3,4},{4,5},{5,6},{6,7},{7,8},{8,9},{9,10},{10,1... | collective-permute-start | bytes 3080 | tf_op jit(solution)/shard_map/ppermute | solution.py:28
  100.9 0.8 collective-permute-done.24
  101.9 1.3 collective-permute-start.27
  103.2 5.7 %collective-permute-start.26 = (f32[8,1,32]{0,2,1:T(8,128)S(1)}, f32[8,1,32]{0,2,1:T(8,128)S(1)}, u32[]{:S(2)}, u32[]{:S(2)}) collective-permute-start(f32[8,1,32]{0,2,1:T(8,128)S(1)} %get-tuple-element.69), channel_id=1, source_target_pairs={{0,1},{1,2},{2,3},{3,4},{4,5},{5,6},{6,7},{7,8},{8,9},{9,10},{10,1... | collective-permute-start | bytes 3080 | tf_op jit(solution)/shard_map/ppermute | solution.py:28
  108.9 0.8 collective-permute-done.26
  109.9 1.3 collective-permute-start.29
  111.2 5.7 %collective-permute-start.28 = (f32[8,1,32]{0,2,1:T(8,128)S(1)}, f32[8,1,32]{0,2,1:T(8,128)S(1)}, u32[]{:S(2)}, u32[]{:S(2)}) collective-permute-start(f32[8,1,32]{0,2,1:T(8,128)S(1)} %get-tuple-element.63), channel_id=1, source_target_pairs={{0,1},{1,2},{2,3},{3,4},{4,5},{5,6},{6,7},{7,8},{8,9},{9,10},{10,1... | collective-permute-start | bytes 3080 | tf_op jit(solution)/shard_map/ppermute | solution.py:28
  117.0 0.8 collective-permute-done.28
  118.0 1.3 collective-permute-start.31
  119.3 5.8 %collective-permute-start.30 = (f32[8,1,32]{0,2,1:T(8,128)S(1)}, f32[8,1,32]{0,2,1:T(8,128)S(1)}, u32[]{:S(2)}, u32[]{:S(2)}) collective-permute-start(f32[8,1,32]{0,2,1:T(8,128)S(1)} %get-tuple-element.57), channel_id=1, source_target_pairs={{0,1},{1,2},{2,3},{3,4},{4,5},{5,6},{6,7},{7,8},{8,9},{9,10},{10,1... | collective-permute-start | bytes 3080 | tf_op jit(solution)/shard_map/ppermute | solution.py:28
  125.1 0.8 collective-permute-done.30
  126.1 1.3 collective-permute-start.33
  127.4 5.8 %collective-permute-start.32 = (f32[8,1,16]{0,2,1:T(8,128)S(1)}, f32[8,1,16]{0,2,1:T(8,128)S(1)}, u32[]{:S(2)}, u32[]{:S(2)}) collective-permute-start(f32[8,1,16]{0,2,1:T(8,128)S(1)} %get-tuple-element.125), channel_id=1, source_target_pairs={{0,1},{1,2},{2,3},{3,4},{4,5},{5,6},{6,7},{7,8},{8,9},{9,10},{10,1... | collective-permute-start | bytes 1544 | tf_op jit(solution)/shard_map/ppermute | solution.py:28
  134.2 1.3 collective-permute-start.35
  135.5 5.7 %collective-permute-start.34 = (f32[8,1,16]{0,2,1:T(8,128)S(1)}, f32[8,1,16]{0,2,1:T(8,128)S(1)}, u32[]{:S(2)}, u32[]{:S(2)}) collective-permute-start(f32[8,1,16]{0,2,1:T(8,128)S(1)} %get-tuple-element.119), channel_id=1, source_target_pairs={{0,1},{1,2},{2,3},{3,4},{4,5},{5,6},{6,7},{7,8},{8,9},{9,10},{10,1... | collective-permute-start | bytes 1544 | tf_op jit(solution)/shard_map/ppermute | solution.py:28
  142.1 1.3 collective-permute-start.37
  143.4 5.8 %collective-permute-start.36 = (f32[8,1,16]{0,2,1:T(8,128)S(1)}, f32[8,1,16]{0,2,1:T(8,128)S(1)}, u32[]{:S(2)}, u32[]{:S(2)}) collective-permute-start(f32[8,1,16]{0,2,1:T(8,128)S(1)} %get-tuple-element.113), channel_id=1, source_target_pairs={{0,1},{1,2},{2,3},{3,4},{4,5},{5,6},{6,7},{7,8},{8,9},{9,10},{10,1... | collective-permute-start | bytes 1544 | tf_op jit(solution)/shard_map/ppermute | solution.py:28
  150.2 1.3 collective-permute-start.39
  151.5 5.7 %collective-permute-start.38 = (f32[8,1,16]{0,2,1:T(8,128)S(1)}, f32[8,1,16]{0,2,1:T(8,128)S(1)}, u32[]{:S(2)}, u32[]{:S(2)}) collective-permute-start(f32[8,1,16]{0,2,1:T(8,128)S(1)} %get-tuple-element.107), channel_id=1, source_target_pairs={{0,1},{1,2},{2,3},{3,4},{4,5},{5,6},{6,7},{7,8},{8,9},{9,10},{10,1... | collective-permute-start | bytes 1544 | tf_op jit(solution)/shard_map/ppermute | solution.py:28
  158.1 1.3 collective-permute-start.41
  159.4 5.7 %collective-permute-start.40 = (f32[8,1,16]{0,2,1:T(8,128)S(1)}, f32[8,1,16]{0,2,1:T(8,128)S(1)}, u32[]{:S(2)}, u32[]{:S(2)}) collective-permute-start(f32[8,1,16]{0,2,1:T(8,128)S(1)} %get-tuple-element.101), channel_id=1, source_target_pairs={{0,1},{1,2},{2,3},{3,4},{4,5},{5,6},{6,7},{7,8},{8,9},{9,10},{10,1... | collective-permute-start | bytes 1544 | tf_op jit(solution)/shard_map/ppermute | solution.py:28
  166.2 1.3 collective-permute-start.43
  167.5 5.7 %collective-permute-start.42 = (f32[8,1,32]{0,2,1:T(8,128)S(1)}, f32[8,1,32]{0,2,1:T(8,128)S(1)}, u32[]{:S(2)}, u32[]{:S(2)}) collective-permute-start(f32[8,1,32]{0,2,1:T(8,128)S(1)} %get-tuple-element.51), channel_id=1, source_target_pairs={{0,1},{1,2},{2,3},{3,4},{4,5},{5,6},{6,7},{7,8},{8,9},{9,10},{10,1... | collective-permute-start | bytes 3080 | tf_op jit(solution)/shard_map/ppermute | solution.py:28
  173.2 0.8 collective-permute-done.42
  174.2 1.3 collective-permute-start.45
  175.5 5.7 %collective-permute-start.44 = (f32[8,1,32]{0,2,1:T(8,128)S(1)}, f32[8,1,32]{0,2,1:T(8,128)S(1)}, u32[]{:S(2)}, u32[]{:S(2)}) collective-permute-start(f32[8,1,32]{0,2,1:T(8,128)S(1)} %get-tuple-element.45), channel_id=1, source_target_pairs={{0,1},{1,2},{2,3},{3,4},{4,5},{5,6},{6,7},{7,8},{8,9},{9,10},{10,1... | collective-permute-start | bytes 3080 | tf_op jit(solution)/shard_map/ppermute | solution.py:28
  181.3 0.8 collective-permute-done.44
  182.3 1.3 collective-permute-start.47
  183.6 5.7 %collective-permute-start.46 = (f32[8,1,32]{0,2,1:T(8,128)S(1)}, f32[8,1,32]{0,2,1:T(8,128)S(1)}, u32[]{:S(2)}, u32[]{:S(2)}) collective-permute-start(f32[8,1,32]{0,2,1:T(8,128)S(1)} %get-tuple-element.35), channel_id=1, source_target_pairs={{0,1},{1,2},{2,3},{3,4},{4,5},{5,6},{6,7},{7,8},{8,9},{9,10},{10,1... | collective-permute-start | bytes 3080 | tf_op jit(solution)/shard_map/ppermute | solution.py:28
  189.3 0.8 collective-permute-done.46
  191.8 14.3 %all-to-all-start.1 = ((f32[16,1,192]{2,1,0:T(1,128)}), f32[16,1,192]{2,1,0:T(1,128)S(1)}, u32[]{:S(2)}, u32[]{:S(2)}) async-start(f32[16,1,192]{2,1,0:T(1,128)} %reshape.99), calls=%async_computation.1 | async-start | bytes 32768 | tf_op jit(solution)/shard_map/all_to_all | solution.py:212
  206.8 34.5 %pmax.7 = f32[]{:T(128)} all-reduce(f32[]{:T(128)} %get-tuple-element.14), channel_id=1, replica_groups=mesh['parts'=2,'gx'=16] {'gx'}, use_global_device_ids=true, to_apply=%region_7.8 | all-reduce | flops 1 | bytes 8 | tf_op jit(solution)/shard_map/pmax | solution.py:208
  246.3 1.3 collective-permute-start.49
  247.6 3.0 %collective-permute-start.48 = (f32[2,8,2,256]{3,1,2,0:T(8,128)S(1)}, f32[2,8,2,256]{3,1,2,0:T(8,128)S(1)}, u32[]{:S(2)}, u32[]{:S(2)}) collective-permute-start(f32[2,8,2,256]{3,1,2,0:T(8,128)S(1)} %copy.470), channel_id=1, source_target_pairs={{0,1},{1,2},{2,3},{3,4},{4,5},{5,6},{6,7},{7,8},{8,9},{9,10},{10,1... | collective-permute-start | bytes 98312 | tf_op jit(solution)/shard_map/ppermute | solution.py:28
  (220 shorter events, 25.1 us)
Async XLA Ops:
  0.6 3.7 %copy-start.1 = (s32[8,256]{1,0:T(8,128)S(1)}, s32[8,256]{1,0:T(8,128)}, u32[]{:S(2)}) copy-start(s32[8,256]{1,0:T(8,128)} %param.5) | copy-start | bytes 24580
  0.7 24.2 %collective-permute-start.2 = (f32[8,1,32]{0,2,1:T(8,128)S(1)}, f32[8,1,32]{0,2,1:T(8,128)S(1)}, u32[]{:S(2)}, u32[]{:S(2)}) collective-permute-start(f32[8,1,32]{0,2,1:T(8,128)S(1)} %broadcast.323), channel_id=1, source_target_pairs={{0,1},{1,2},{2,3},{3,4},{4,5},{5,6},{6,7},{7,8},{8,9},{9,10},{10,1... | collective-permute-start | bytes 3080 | tf_op jit(solution)/shard_map/ppermute | solution.py:28
  3.0 25.4 %collective-permute-start.3 = (f32[8,1,32]{0,2,1:T(8,128)S(1)}, f32[8,1,32]{0,2,1:T(8,128)S(1)}, u32[]{:S(2)}, u32[]{:S(2)}) collective-permute-start(f32[8,1,32]{0,2,1:T(8,128)S(1)} %broadcast.323), channel_id=1, source_target_pairs={{1,0},{2,1},{3,2},{4,3},{5,4},{6,5},{7,6},{8,7},{9,8},{10,9},{11,1... | collective-permute-start | bytes 3080 | tf_op jit(solution)/shard_map/ppermute | solution.py:29
  4.7 0.8 copy-start
  7.0 9.4 %copy-start.2 = (f32[8,4,32]{2,1,0:T(4,128)S(1)}, f32[8,4,32]{2,1,0:T(4,128)}, u32[]{:S(2)}) copy-start(f32[8,4,32]{2,1,0:T(4,128)} %param.6) | copy-start | bytes 12292
  7.0 16.3 %all-to-all-start = ((f32[9,64,2]{0,2,1:T(2,128)}), f32[9,64,2]{0,2,1:T(2,128)S(1)}, u32[]{:S(2)}, u32[]{:S(2)}) async-start(f32[9,64,2]{0,2,1:T(2,128)} %copy.444), calls=%async_computation | async-start | bytes 131072 | tf_op jit(solution)/shard_map/all_to_all | solution.py:172
  16.5 15.5 %collective-permute-start = (f32[8,1,32]{0,2,1:T(8,128)S(1)}, f32[8,1,32]{0,2,1:T(8,128)S(1)}, u32[]{:S(2)}, u32[]{:S(2)}) collective-permute-start(f32[8,1,32]{0,2,1:T(8,128)S(1)} %get-tuple-element.96), channel_id=1, source_target_pairs={{0,1},{1,2},{2,3},{3,4},{4,5},{5,6},{6,7},{7,8},{8,9},{9,10},{10,1... | collective-permute-start | bytes 3080 | tf_op jit(solution)/shard_map/ppermute | solution.py:28
  18.9 13.2 %collective-permute-start.1 = (f32[8,1,32]{0,2,1:T(8,128)S(1)}, f32[8,1,32]{0,2,1:T(8,128)S(1)}, u32[]{:S(2)}, u32[]{:S(2)}) collective-permute-start(f32[8,1,32]{0,2,1:T(8,128)S(1)} %get-tuple-element.95), channel_id=1, source_target_pairs={{1,0},{2,1},{3,2},{4,3},{5,4},{6,5},{7,6},{8,7},{9,8},{10,9},{11,1... | collective-permute-start | bytes 3080 | tf_op jit(solution)/shard_map/ppermute | solution.py:29
  20.2 24.9 %collective-permute-start.11 = (f32[8,1,16]{0,2,1:T(8,128)S(1)}, f32[8,1,16]{0,2,1:T(8,128)S(1)}, u32[]{:S(2)}, u32[]{:S(2)}) collective-permute-start(f32[8,1,16]{0,2,1:T(8,128)S(1)} %broadcast.328), channel_id=1, source_target_pairs={{1,0},{2,1},{3,2},{4,3},{5,4},{6,5},{7,6},{8,7},{9,8},{10,9},{11,1... | collective-permute-start | bytes 1544 | tf_op jit(solution)/shard_map/ppermute | solution.py:29
  23.9 0.7 copy-start.3
  24.8 20.3 %collective-permute-start.10 = (f32[8,1,16]{0,2,1:T(8,128)S(1)}, f32[8,1,16]{0,2,1:T(8,128)S(1)}, u32[]{:S(2)}, u32[]{:S(2)}) collective-permute-start(f32[8,1,16]{0,2,1:T(8,128)S(1)} %broadcast.328), channel_id=1, source_target_pairs={{0,1},{1,2},{2,3},{3,4},{4,5},{5,6},{6,7},{7,8},{8,9},{9,10},{10,1... | collective-permute-start | bytes 1544 | tf_op jit(solution)/shard_map/ppermute | solution.py:28
  28.4 16.7 %collective-permute-start.8 = (f32[8,1,16]{0,2,1:T(8,128)S(1)}, f32[8,1,16]{0,2,1:T(8,128)S(1)}, u32[]{:S(2)}, u32[]{:S(2)}) collective-permute-start(f32[8,1,16]{0,2,1:T(8,128)S(1)} %get-tuple-element.158), channel_id=1, source_target_pairs={{0,1},{1,2},{2,3},{3,4},{4,5},{5,6},{6,7},{7,8},{8,9},{9,10},{10,1... | collective-permute-start | bytes 1544 | tf_op jit(solution)/shard_map/ppermute | solution.py:28
  32.3 4.6 %collective-permute-start.5 = (f32[8,1,32]{0,2,1:T(8,128)S(1)}, f32[8,1,32]{0,2,1:T(8,128)S(1)}, u32[]{:S(2)}, u32[]{:S(2)}) collective-permute-start(f32[8,1,32]{0,2,1:T(8,128)S(1)} %get-tuple-element.94), channel_id=1, source_target_pairs={{1,0},{2,1},{3,2},{4,3},{5,4},{6,5},{7,6},{8,7},{9,8},{10,9},{11,1... | collective-permute-start | bytes 3080 | tf_op jit(solution)/shard_map/ppermute | solution.py:29
  33.6 3.9 %collective-permute-start.4 = (f32[8,1,32]{0,2,1:T(8,128)S(1)}, f32[8,1,32]{0,2,1:T(8,128)S(1)}, u32[]{:S(2)}, u32[]{:S(2)}) collective-permute-start(f32[8,1,32]{0,2,1:T(8,128)S(1)} %get-tuple-element.93), channel_id=1, source_target_pairs={{0,1},{1,2},{2,3},{3,4},{4,5},{5,6},{6,7},{7,8},{8,9},{9,10},{10,1... | collective-permute-start | bytes 3080 | tf_op jit(solution)/shard_map/ppermute | solution.py:28
  37.7 5.9 %collective-permute-start.7 = (f32[8,1,32]{0,2,1:T(8,128)S(1)}, f32[8,1,32]{0,2,1:T(8,128)S(1)}, u32[]{:S(2)}, u32[]{:S(2)}) collective-permute-start(f32[8,1,32]{0,2,1:T(8,128)S(1)} %get-tuple-element.88), channel_id=1, source_target_pairs={{1,0},{2,1},{3,2},{4,3},{5,4},{6,5},{7,6},{8,7},{9,8},{10,9},{11,1... | collective-permute-start | bytes 3080 | tf_op jit(solution)/shard_map/ppermute | solution.py:29
  39.0 5.9 %collective-permute-start.6 = (f32[8,1,32]{0,2,1:T(8,128)S(1)}, f32[8,1,32]{0,2,1:T(8,128)S(1)}, u32[]{:S(2)}, u32[]{:S(2)}) collective-permute-start(f32[8,1,32]{0,2,1:T(8,128)S(1)} %get-tuple-element.87), channel_id=1, source_target_pairs={{0,1},{1,2},{2,3},{3,4},{4,5},{5,6},{6,7},{7,8},{8,9},{9,10},{10,1... | collective-permute-start | bytes 3080 | tf_op jit(solution)/shard_map/ppermute | solution.py:28
  43.6 4.9 %collective-permute-start.9 = (f32[8,1,16]{0,2,1:T(8,128)S(1)}, f32[8,1,16]{0,2,1:T(8,128)S(1)}, u32[]{:S(2)}, u32[]{:S(2)}) collective-permute-start(f32[8,1,16]{0,2,1:T(8,128)S(1)} %get-tuple-element.157), channel_id=1, source_target_pairs={{1,0},{2,1},{3,2},{4,3},{5,4},{6,5},{7,6},{8,7},{9,8},{10,9},{11,1... | collective-permute-start | bytes 1544 | tf_op jit(solution)/shard_map/ppermute | solution.py:29
  48.6 6.2 %collective-permute-start.13 = (f32[8,1,16]{0,2,1:T(8,128)S(1)}, f32[8,1,16]{0,2,1:T(8,128)S(1)}, u32[]{:S(2)}, u32[]{:S(2)}) collective-permute-start(f32[8,1,16]{0,2,1:T(8,128)S(1)} %get-tuple-element.156), channel_id=1, source_target_pairs={{1,0},{2,1},{3,2},{4,3},{5,4},{6,5},{7,6},{8,7},{9,8},{10,9},{11,1... | collective-permute-start | bytes 1544 | tf_op jit(solution)/shard_map/ppermute | solution.py:29
  49.9 5.8 %collective-permute-start.12 = (f32[8,1,16]{0,2,1:T(8,128)S(1)}, f32[8,1,16]{0,2,1:T(8,128)S(1)}, u32[]{:S(2)}, u32[]{:S(2)}) collective-permute-start(f32[8,1,16]{0,2,1:T(8,128)S(1)} %get-tuple-element.155), channel_id=1, source_target_pairs={{0,1},{1,2},{2,3},{3,4},{4,5},{5,6},{6,7},{7,8},{8,9},{9,10},{10,1... | collective-permute-start | bytes 1544 | tf_op jit(solution)/shard_map/ppermute | solution.py:28
  55.8 5.5 %collective-permute-start.15 = (f32[8,1,16]{0,2,1:T(8,128)S(1)}, f32[8,1,16]{0,2,1:T(8,128)S(1)}, u32[]{:S(2)}, u32[]{:S(2)}) collective-permute-start(f32[8,1,16]{0,2,1:T(8,128)S(1)} %get-tuple-element.150), channel_id=1, source_target_pairs={{1,0},{2,1},{3,2},{4,3},{5,4},{6,5},{7,6},{8,7},{9,8},{10,9},{11,1... | collective-permute-start | bytes 1544 | tf_op jit(solution)/shard_map/ppermute | solution.py:29
  57.1 5.0 %collective-permute-start.14 = (f32[8,1,16]{0,2,1:T(8,128)S(1)}, f32[8,1,16]{0,2,1:T(8,128)S(1)}, u32[]{:S(2)}, u32[]{:S(2)}) collective-permute-start(f32[8,1,16]{0,2,1:T(8,128)S(1)} %get-tuple-element.149), channel_id=1, source_target_pairs={{0,1},{1,2},{2,3},{3,4},{4,5},{5,6},{6,7},{7,8},{8,9},{9,10},{10,1... | collective-permute-start | bytes 1544 | tf_op jit(solution)/shard_map/ppermute | solution.py:28
  62.3 7.0 %collective-permute-start.17 = (f32[8,1,16]{0,2,1:T(8,128)S(1)}, f32[8,1,16]{0,2,1:T(8,128)S(1)}, u32[]{:S(2)}, u32[]{:S(2)}) collective-permute-start(f32[8,1,16]{0,2,1:T(8,128)S(1)} %get-tuple-element.144), channel_id=1, source_target_pairs={{1,0},{2,1},{3,2},{4,3},{5,4},{6,5},{7,6},{8,7},{9,8},{10,9},{11,1... | collective-permute-start | bytes 1544 | tf_op jit(solution)/shard_map/ppermute | solution.py:29
  63.6 6.5 %collective-permute-start.16 = (f32[8,1,16]{0,2,1:T(8,128)S(1)}, f32[8,1,16]{0,2,1:T(8,128)S(1)}, u32[]{:S(2)}, u32[]{:S(2)}) collective-permute-start(f32[8,1,16]{0,2,1:T(8,128)S(1)} %get-tuple-element.143), channel_id=1, source_target_pairs={{0,1},{1,2},{2,3},{3,4},{4,5},{5,6},{6,7},{7,8},{8,9},{9,10},{10,1... | collective-permute-start | bytes 1544 | tf_op jit(solution)/shard_map/ppermute | solution.py:28
  70.3 6.4 %collective-permute-start.19 = (f32[8,1,16]{0,2,1:T(8,128)S(1)}, f32[8,1,16]{0,2,1:T(8,128)S(1)}, u32[]{:S(2)}, u32[]{:S(2)}) collective-permute-start(f32[8,1,16]{0,2,1:T(8,128)S(1)} %get-tuple-element.138), channel_id=1, source_target_pairs={{1,0},{2,1},{3,2},{4,3},{5,4},{6,5},{7,6},{8,7},{9,8},{10,9},{11,1... | collective-permute-start | bytes 1544 | tf_op jit(solution)/shard_map/ppermute | solution.py:29
  71.6 5.9 %collective-permute-start.18 = (f32[8,1,16]{0,2,1:T(8,128)S(1)}, f32[8,1,16]{0,2,1:T(8,128)S(1)}, u32[]{:S(2)}, u32[]{:S(2)}) collective-permute-start(f32[8,1,16]{0,2,1:T(8,128)S(1)} %get-tuple-element.137), channel_id=1, source_target_pairs={{0,1},{1,2},{2,3},{3,4},{4,5},{5,6},{6,7},{7,8},{8,9},{9,10},{10,1... | collective-permute-start | bytes 1544 | tf_op jit(solution)/shard_map/ppermute | solution.py:28
  77.7 7.0 %collective-permute-start.21 = (f32[8,1,16]{0,2,1:T(8,128)S(1)}, f32[8,1,16]{0,2,1:T(8,128)S(1)}, u32[]{:S(2)}, u32[]{:S(2)}) collective-permute-start(f32[8,1,16]{0,2,1:T(8,128)S(1)} %get-tuple-element.132), channel_id=1, source_target_pairs={{1,0},{2,1},{3,2},{4,3},{5,4},{6,5},{7,6},{8,7},{9,8},{10,9},{11,1... | collective-permute-start | bytes 1544 | tf_op jit(solution)/shard_map/ppermute | solution.py:29
  79.0 6.5 %collective-permute-start.20 = (f32[8,1,16]{0,2,1:T(8,128)S(1)}, f32[8,1,16]{0,2,1:T(8,128)S(1)}, u32[]{:S(2)}, u32[]{:S(2)}) collective-permute-start(f32[8,1,16]{0,2,1:T(8,128)S(1)} %get-tuple-element.131), channel_id=1, source_target_pairs={{0,1},{1,2},{2,3},{3,4},{4,5},{5,6},{6,7},{7,8},{8,9},{9,10},{10,1... | collective-permute-start | bytes 1544 | tf_op jit(solution)/shard_map/ppermute | solution.py:28
  85.8 7.0 %collective-permute-start.23 = (f32[8,1,32]{0,2,1:T(8,128)S(1)}, f32[8,1,32]{0,2,1:T(8,128)S(1)}, u32[]{:S(2)}, u32[]{:S(2)}) collective-permute-start(f32[8,1,32]{0,2,1:T(8,128)S(1)} %get-tuple-element.82), channel_id=1, source_target_pairs={{1,0},{2,1},{3,2},{4,3},{5,4},{6,5},{7,6},{8,7},{9,8},{10,9},{11,1... | collective-permute-start | bytes 3080 | tf_op jit(solution)/shard_map/ppermute | solution.py:29
  87.1 6.5 %collective-permute-start.22 = (f32[8,1,32]{0,2,1:T(8,128)S(1)}, f32[8,1,32]{0,2,1:T(8,128)S(1)}, u32[]{:S(2)}, u32[]{:S(2)}) collective-permute-start(f32[8,1,32]{0,2,1:T(8,128)S(1)} %get-tuple-element.81), channel_id=1, source_target_pairs={{0,1},{1,2},{2,3},{3,4},{4,5},{5,6},{6,7},{7,8},{8,9},{9,10},{10,1... | collective-permute-start | bytes 3080 | tf_op jit(solution)/shard_map/ppermute | solution.py:28
  93.8 7.1 %collective-permute-start.25 = (f32[8,1,32]{0,2,1:T(8,128)S(1)}, f32[8,1,32]{0,2,1:T(8,128)S(1)}, u32[]{:S(2)}, u32[]{:S(2)}) collective-permute-start(f32[8,1,32]{0,2,1:T(8,128)S(1)} %get-tuple-element.76), channel_id=1, source_target_pairs={{1,0},{2,1},{3,2},{4,3},{5,4},{6,5},{7,6},{8,7},{9,8},{10,9},{11,1... | collective-permute-start | bytes 3080 | tf_op jit(solution)/shard_map/ppermute | solution.py:29
  95.1 6.6 %collective-permute-start.24 = (f32[8,1,32]{0,2,1:T(8,128)S(1)}, f32[8,1,32]{0,2,1:T(8,128)S(1)}, u32[]{:S(2)}, u32[]{:S(2)}) collective-permute-start(f32[8,1,32]{0,2,1:T(8,128)S(1)} %get-tuple-element.75), channel_id=1, source_target_pairs={{0,1},{1,2},{2,3},{3,4},{4,5},{5,6},{6,7},{7,8},{8,9},{9,10},{10,1... | collective-permute-start | bytes 3080 | tf_op jit(solution)/shard_map/ppermute | solution.py:28
  101.9 7.0 %collective-permute-start.27 = (f32[8,1,32]{0,2,1:T(8,128)S(1)}, f32[8,1,32]{0,2,1:T(8,128)S(1)}, u32[]{:S(2)}, u32[]{:S(2)}) collective-permute-start(f32[8,1,32]{0,2,1:T(8,128)S(1)} %get-tuple-element.70), channel_id=1, source_target_pairs={{1,0},{2,1},{3,2},{4,3},{5,4},{6,5},{7,6},{8,7},{9,8},{10,9},{11,1... | collective-permute-start | bytes 3080 | tf_op jit(solution)/shard_map/ppermute | solution.py:29
  103.2 6.5 %collective-permute-start.26 = (f32[8,1,32]{0,2,1:T(8,128)S(1)}, f32[8,1,32]{0,2,1:T(8,128)S(1)}, u32[]{:S(2)}, u32[]{:S(2)}) collective-permute-start(f32[8,1,32]{0,2,1:T(8,128)S(1)} %get-tuple-element.69), channel_id=1, source_target_pairs={{0,1},{1,2},{2,3},{3,4},{4,5},{5,6},{6,7},{7,8},{8,9},{9,10},{10,1... | collective-permute-start | bytes 3080 | tf_op jit(solution)/shard_map/ppermute | solution.py:28
  109.9 7.1 %collective-permute-start.29 = (f32[8,1,32]{0,2,1:T(8,128)S(1)}, f32[8,1,32]{0,2,1:T(8,128)S(1)}, u32[]{:S(2)}, u32[]{:S(2)}) collective-permute-start(f32[8,1,32]{0,2,1:T(8,128)S(1)} %get-tuple-element.64), channel_id=1, source_target_pairs={{1,0},{2,1},{3,2},{4,3},{5,4},{6,5},{7,6},{8,7},{9,8},{10,9},{11,1... | collective-permute-start | bytes 3080 | tf_op jit(solution)/shard_map/ppermute | solution.py:29
  111.2 6.6 %collective-permute-start.28 = (f32[8,1,32]{0,2,1:T(8,128)S(1)}, f32[8,1,32]{0,2,1:T(8,128)S(1)}, u32[]{:S(2)}, u32[]{:S(2)}) collective-permute-start(f32[8,1,32]{0,2,1:T(8,128)S(1)} %get-tuple-element.63), channel_id=1, source_target_pairs={{0,1},{1,2},{2,3},{3,4},{4,5},{5,6},{6,7},{7,8},{8,9},{9,10},{10,1... | collective-permute-start | bytes 3080 | tf_op jit(solution)/shard_map/ppermute | solution.py:28
  118.0 7.1 %collective-permute-start.31 = (f32[8,1,32]{0,2,1:T(8,128)S(1)}, f32[8,1,32]{0,2,1:T(8,128)S(1)}, u32[]{:S(2)}, u32[]{:S(2)}) collective-permute-start(f32[8,1,32]{0,2,1:T(8,128)S(1)} %get-tuple-element.58), channel_id=1, source_target_pairs={{1,0},{2,1},{3,2},{4,3},{5,4},{6,5},{7,6},{8,7},{9,8},{10,9},{11,1... | collective-permute-start | bytes 3080 | tf_op jit(solution)/shard_map/ppermute | solution.py:29
  119.3 6.6 %collective-permute-start.30 = (f32[8,1,32]{0,2,1:T(8,128)S(1)}, f32[8,1,32]{0,2,1:T(8,128)S(1)}, u32[]{:S(2)}, u32[]{:S(2)}) collective-permute-start(f32[8,1,32]{0,2,1:T(8,128)S(1)} %get-tuple-element.57), channel_id=1, source_target_pairs={{0,1},{1,2},{2,3},{3,4},{4,5},{5,6},{6,7},{7,8},{8,9},{9,10},{10,1... | collective-permute-start | bytes 3080 | tf_op jit(solution)/shard_map/ppermute | solution.py:28
  126.1 7.1 %collective-permute-start.33 = (f32[8,1,16]{0,2,1:T(8,128)S(1)}, f32[8,1,16]{0,2,1:T(8,128)S(1)}, u32[]{:S(2)}, u32[]{:S(2)}) collective-permute-start(f32[8,1,16]{0,2,1:T(8,128)S(1)} %get-tuple-element.126), channel_id=1, source_target_pairs={{1,0},{2,1},{3,2},{4,3},{5,4},{6,5},{7,6},{8,7},{9,8},{10,9},{11,1... | collective-permute-start | bytes 1544 | tf_op jit(solution)/shard_map/ppermute | solution.py:29
  127.4 6.6 %collective-permute-start.32 = (f32[8,1,16]{0,2,1:T(8,128)S(1)}, f32[8,1,16]{0,2,1:T(8,128)S(1)}, u32[]{:S(2)}, u32[]{:S(2)}) collective-permute-start(f32[8,1,16]{0,2,1:T(8,128)S(1)} %get-tuple-element.125), channel_id=1, source_target_pairs={{0,1},{1,2},{2,3},{3,4},{4,5},{5,6},{6,7},{7,8},{8,9},{9,10},{10,1... | collective-permute-start | bytes 1544 | tf_op jit(solution)/shard_map/ppermute | solution.py:28
  134.2 7.0 %collective-permute-start.35 = (f32[8,1,16]{0,2,1:T(8,128)S(1)}, f32[8,1,16]{0,2,1:T(8,128)S(1)}, u32[]{:S(2)}, u32[]{:S(2)}) collective-permute-start(f32[8,1,16]{0,2,1:T(8,128)S(1)} %get-tuple-element.120), channel_id=1, source_target_pairs={{1,0},{2,1},{3,2},{4,3},{5,4},{6,5},{7,6},{8,7},{9,8},{10,9},{11,1... | collective-permute-start | bytes 1544 | tf_op jit(solution)/shard_map/ppermute | solution.py:29
  135.5 6.5 %collective-permute-start.34 = (f32[8,1,16]{0,2,1:T(8,128)S(1)}, f32[8,1,16]{0,2,1:T(8,128)S(1)}, u32[]{:S(2)}, u32[]{:S(2)}) collective-permute-start(f32[8,1,16]{0,2,1:T(8,128)S(1)} %get-tuple-element.119), channel_id=1, source_target_pairs={{0,1},{1,2},{2,3},{3,4},{4,5},{5,6},{6,7},{7,8},{8,9},{9,10},{10,1... | collective-permute-start | bytes 1544 | tf_op jit(solution)/shard_map/ppermute | solution.py:28
  142.1 7.1 %collective-permute-start.37 = (f32[8,1,16]{0,2,1:T(8,128)S(1)}, f32[8,1,16]{0,2,1:T(8,128)S(1)}, u32[]{:S(2)}, u32[]{:S(2)}) collective-permute-start(f32[8,1,16]{0,2,1:T(8,128)S(1)} %get-tuple-element.114), channel_id=1, source_target_pairs={{1,0},{2,1},{3,2},{4,3},{5,4},{6,5},{7,6},{8,7},{9,8},{10,9},{11,1... | collective-permute-start | bytes 1544 | tf_op jit(solution)/shard_map/ppermute | solution.py:29
  143.4 6.6 %collective-permute-start.36 = (f32[8,1,16]{0,2,1:T(8,128)S(1)}, f32[8,1,16]{0,2,1:T(8,128)S(1)}, u32[]{:S(2)}, u32[]{:S(2)}) collective-permute-start(f32[8,1,16]{0,2,1:T(8,128)S(1)} %get-tuple-element.113), channel_id=1, source_target_pairs={{0,1},{1,2},{2,3},{3,4},{4,5},{5,6},{6,7},{7,8},{8,9},{9,10},{10,1... | collective-permute-start | bytes 1544 | tf_op jit(solution)/shard_map/ppermute | solution.py:28
  150.2 7.0 %collective-permute-start.39 = (f32[8,1,16]{0,2,1:T(8,128)S(1)}, f32[8,1,16]{0,2,1:T(8,128)S(1)}, u32[]{:S(2)}, u32[]{:S(2)}) collective-permute-start(f32[8,1,16]{0,2,1:T(8,128)S(1)} %get-tuple-element.108), channel_id=1, source_target_pairs={{1,0},{2,1},{3,2},{4,3},{5,4},{6,5},{7,6},{8,7},{9,8},{10,9},{11,1... | collective-permute-start | bytes 1544 | tf_op jit(solution)/shard_map/ppermute | solution.py:29
  151.5 6.5 %collective-permute-start.38 = (f32[8,1,16]{0,2,1:T(8,128)S(1)}, f32[8,1,16]{0,2,1:T(8,128)S(1)}, u32[]{:S(2)}, u32[]{:S(2)}) collective-permute-start(f32[8,1,16]{0,2,1:T(8,128)S(1)} %get-tuple-element.107), channel_id=1, source_target_pairs={{0,1},{1,2},{2,3},{3,4},{4,5},{5,6},{6,7},{7,8},{8,9},{9,10},{10,1... | collective-permute-start | bytes 1544 | tf_op jit(solution)/shard_map/ppermute | solution.py:28
  158.1 7.0 %collective-permute-start.41 = (f32[8,1,16]{0,2,1:T(8,128)S(1)}, f32[8,1,16]{0,2,1:T(8,128)S(1)}, u32[]{:S(2)}, u32[]{:S(2)}) collective-permute-start(f32[8,1,16]{0,2,1:T(8,128)S(1)} %get-tuple-element.102), channel_id=1, source_target_pairs={{1,0},{2,1},{3,2},{4,3},{5,4},{6,5},{7,6},{8,7},{9,8},{10,9},{11,1... | collective-permute-start | bytes 1544 | tf_op jit(solution)/shard_map/ppermute | solution.py:29
  159.4 6.5 %collective-permute-start.40 = (f32[8,1,16]{0,2,1:T(8,128)S(1)}, f32[8,1,16]{0,2,1:T(8,128)S(1)}, u32[]{:S(2)}, u32[]{:S(2)}) collective-permute-start(f32[8,1,16]{0,2,1:T(8,128)S(1)} %get-tuple-element.101), channel_id=1, source_target_pairs={{0,1},{1,2},{2,3},{3,4},{4,5},{5,6},{6,7},{7,8},{8,9},{9,10},{10,1... | collective-permute-start | bytes 1544 | tf_op jit(solution)/shard_map/ppermute | solution.py:28
  166.2 7.0 %collective-permute-start.43 = (f32[8,1,32]{0,2,1:T(8,128)S(1)}, f32[8,1,32]{0,2,1:T(8,128)S(1)}, u32[]{:S(2)}, u32[]{:S(2)}) collective-permute-start(f32[8,1,32]{0,2,1:T(8,128)S(1)} %get-tuple-element.52), channel_id=1, source_target_pairs={{1,0},{2,1},{3,2},{4,3},{5,4},{6,5},{7,6},{8,7},{9,8},{10,9},{11,1... | collective-permute-start | bytes 3080 | tf_op jit(solution)/shard_map/ppermute | solution.py:29
  167.5 6.5 %collective-permute-start.42 = (f32[8,1,32]{0,2,1:T(8,128)S(1)}, f32[8,1,32]{0,2,1:T(8,128)S(1)}, u32[]{:S(2)}, u32[]{:S(2)}) collective-permute-start(f32[8,1,32]{0,2,1:T(8,128)S(1)} %get-tuple-element.51), channel_id=1, source_target_pairs={{0,1},{1,2},{2,3},{3,4},{4,5},{5,6},{6,7},{7,8},{8,9},{9,10},{10,1... | collective-permute-start | bytes 3080 | tf_op jit(solution)/shard_map/ppermute | solution.py:28
  174.2 7.1 %collective-permute-start.45 = (f32[8,1,32]{0,2,1:T(8,128)S(1)}, f32[8,1,32]{0,2,1:T(8,128)S(1)}, u32[]{:S(2)}, u32[]{:S(2)}) collective-permute-start(f32[8,1,32]{0,2,1:T(8,128)S(1)} %get-tuple-element.46), channel_id=1, source_target_pairs={{1,0},{2,1},{3,2},{4,3},{5,4},{6,5},{7,6},{8,7},{9,8},{10,9},{11,1... | collective-permute-start | bytes 3080 | tf_op jit(solution)/shard_map/ppermute | solution.py:29
  175.5 6.6 %collective-permute-start.44 = (f32[8,1,32]{0,2,1:T(8,128)S(1)}, f32[8,1,32]{0,2,1:T(8,128)S(1)}, u32[]{:S(2)}, u32[]{:S(2)}) collective-permute-start(f32[8,1,32]{0,2,1:T(8,128)S(1)} %get-tuple-element.45), channel_id=1, source_target_pairs={{0,1},{1,2},{2,3},{3,4},{4,5},{5,6},{6,7},{7,8},{8,9},{9,10},{10,1... | collective-permute-start | bytes 3080 | tf_op jit(solution)/shard_map/ppermute | solution.py:28
  182.3 7.0 %collective-permute-start.47 = (f32[8,1,32]{0,2,1:T(8,128)S(1)}, f32[8,1,32]{0,2,1:T(8,128)S(1)}, u32[]{:S(2)}, u32[]{:S(2)}) collective-permute-start(f32[8,1,32]{0,2,1:T(8,128)S(1)} %get-tuple-element.36), channel_id=1, source_target_pairs={{1,0},{2,1},{3,2},{4,3},{5,4},{6,5},{7,6},{8,7},{9,8},{10,9},{11,1... | collective-permute-start | bytes 3080 | tf_op jit(solution)/shard_map/ppermute | solution.py:29
  183.6 6.5 %collective-permute-start.46 = (f32[8,1,32]{0,2,1:T(8,128)S(1)}, f32[8,1,32]{0,2,1:T(8,128)S(1)}, u32[]{:S(2)}, u32[]{:S(2)}) collective-permute-start(f32[8,1,32]{0,2,1:T(8,128)S(1)} %get-tuple-element.35), channel_id=1, source_target_pairs={{0,1},{1,2},{2,3},{3,4},{4,5},{5,6},{6,7},{7,8},{8,9},{9,10},{10,1... | collective-permute-start | bytes 3080 | tf_op jit(solution)/shard_map/ppermute | solution.py:28
  191.8 50.2 %all-to-all-start.1 = ((f32[16,1,192]{2,1,0:T(1,128)}), f32[16,1,192]{2,1,0:T(1,128)S(1)}, u32[]{:S(2)}, u32[]{:S(2)}) async-start(f32[16,1,192]{2,1,0:T(1,128)} %reshape.99), calls=%async_computation.1 | async-start | bytes 32768 | tf_op jit(solution)/shard_map/all_to_all | solution.py:212
  246.3 4.5 %collective-permute-start.49 = (f32[2,8,2,256]{3,1,2,0:T(8,128)S(1)}, f32[2,8,2,256]{3,1,2,0:T(8,128)S(1)}, u32[]{:S(2)}, u32[]{:S(2)}) collective-permute-start(f32[2,8,2,256]{3,1,2,0:T(8,128)S(1)} %copy.471), channel_id=1, source_target_pairs={{1,0},{2,1},{3,2},{4,3},{5,4},{6,5},{7,6},{8,7},{9,8},{10,9},{11,1... | collective-permute-start | bytes 98312 | tf_op jit(solution)/shard_map/ppermute | solution.py:29
  247.6 3.9 %collective-permute-start.48 = (f32[2,8,2,256]{3,1,2,0:T(8,128)S(1)}, f32[2,8,2,256]{3,1,2,0:T(8,128)S(1)}, u32[]{:S(2)}, u32[]{:S(2)}) collective-permute-start(f32[2,8,2,256]{3,1,2,0:T(8,128)S(1)} %copy.470), channel_id=1, source_target_pairs={{0,1},{1,2},{2,3},{3,4},{4,5},{5,6},{6,7},{7,8},{8,9},{9,10},{10,1... | collective-permute-start | bytes 98312 | tf_op jit(solution)/shard_map/ppermute | solution.py:28
where the time goes:
time: 254 us; the launch traced here: 253 us
  starting transfers between devices  178 us (70%)
  blocking collectives  34.5 us (14%)
  waiting for transfers between devices  20.1 us (8%)
  local copies, waits for them, and re-layouts  10.6 us (4%)
  other arithmetic  6.21 us (2%)
  between operations  2.75 us (1%)
    ppermute x25, starting transfers between devices, padded_2(): before = lax.ppermute(last, axis, up)  122 us
    pmax x1, blocking collectives, local(): fastest = lax.pmax(local_fastest, 'gx')  34.5 us
    ppermute x25, starting transfers between devices, padded_2(): after = lax.ppermute(first, axis, down)  32.2 us
    ppermute x25, waiting for transfers between devices, padded_2(): before = lax.ppermute(last, axis, up)  15.4 us
    all_to_all x1, starting transfers between devices, local(): lax.all_to_all(packed, 'gx', split_axis=3, concat_axis=2, tiled=True)  14.3 us
    all_to_all x1, starting transfers between devices, local(): lax.all_to_all(jnp.transpose(blocks, (0, 2, 1)), 'gx', split_axis=1, conc...  9.43 us
  transfers between devices with their start and end apart: 52, of which 22 were waited for; matrix products, arithmetic and copies ran while one was open for 2% of the time, Pallas kernels for 0%

commit v1 on v0

--- a/solution.py
+++ b/solution.py
@@ -1,12 +1,13 @@
 import jax
 import jax.numpy as jnp
 from jax import lax
+from jax.experimental import pallas as pl
+from jax.experimental.pallas import tpu as pltpu
 from jax.sharding import PartitionSpec as P
 
 CYCLES = 2
 SMOOTH = 2
 COARSE_SWEEPS = 6
-
 
 relax_weight = 0.8
 vertical_ratio = 0.5
@@ -16,7 +17,6 @@
 recharge_rate = 1.0
 courant = 0.45
 freshening = 1.0
-
 
 def padded_2(array, sides, width):
     for axis, dim in sides:
@@ -30,11 +30,9 @@
         array = jnp.concatenate([before, array, after], axis=dim)
     return array
 
-
 def harmonic(first, second):
     total = first + second
     return 2.0 * first * second / (total + jnp.where(total > 0, 0.0, 1.0))
-
 
 def coefficients(padded, penalty, vertical_scale):
     inner = padded[:, 1:-1, :]
@@ -52,7 +50,6 @@
     diagonal = x_low + x_high + y_low + y_high + z_up + z_down + top_term
     return (x_low, x_high, y_low, y_high, z_up, z_down, diagonal)
 
-
 def neighbors(padded):
     center = padded[:, 1:-1, :]
     zero_col = jnp.zeros_like(center[:, :, :1])
@@ -62,7 +59,6 @@
     upper = jnp.concatenate([zero_layer, center[:-1]], axis=0)
     lower = jnp.concatenate([center[1:], zero_layer], axis=0)
     return (center, west, east, padded[:, :-2, :], padded[:, 2:, :], upper, lower)
-
 
 def apply_operator(padded, coeffs):
     center, west, east, south, north, upper, lower = neighbors(padded)
@@ -77,13 +73,11 @@
         - z_down * lower
     )
 
-
 def relax(padded, coeffs, right_side):
     return (
         padded[:, 1:-1, :]
         + relax_weight * (right_side - apply_operator(padded, coeffs)) / coeffs[6]
     )
-
 
 def block_mean(field):
     leading = field.shape[:-2]
@@ -91,25 +85,20 @@
     grouped = field.reshape(leading + (count_a // 4, 4, count_b // 4, 4))
     return jnp.sum(grouped, axis=(-3, -1)) * 0.0625
 
-
 def pair_sum(field):
     leading = field.shape[:-2]
     count_a, count_b = field.shape[-2:]
     grouped = field.reshape(leading + (count_a // 2, 2, count_b // 2, 2))
     return jnp.sum(grouped, axis=(-3, -1))
 
-
 def upsample(field, factor):
     return jnp.repeat(jnp.repeat(field, factor, axis=-2), factor, axis=-1)
 
-
 def minmod(first, second):
     return 0.5 * (jnp.sign(first) + jnp.sign(second)) * jnp.minimum(jnp.abs(first), jnp.abs(second))
 
-
 def portion(field, start, stop, axis):
     return lax.slice_in_dim(field, start, stop, axis=axis)
-
 
 def divergence(cells, speed, axis):
     length = cells.shape[axis]
@@ -124,7 +113,6 @@
     flux = jnp.pad(faces * jnp.where(faces > 0, left, right), widths)
     return portion(flux, 1, length + 1, axis) - portion(flux, 0, length, axis)
 
-
 def divergence_x(extended, faces):
     steps_diff = extended[:, 1:] - extended[:, :-1]
     slope = minmod(steps_diff[:, :-1], steps_diff[:, 1:])
@@ -134,7 +122,6 @@
     flux = faces * jnp.where(faces > 0, left, right)
     return flux[:, 1:] - flux[:, :-1]
 
-
 def velocities(padded, coeffs, above, below):
     center, west, east, south, north, upper, lower = neighbors(padded)
     x_low, x_high, y_low, y_high, z_up, z_down, diagonal = coeffs
@@ -143,7 +130,6 @@
     vel_z = 0.5 * (z_up * (upper - center + above) + z_down * (center - lower + below))
     return (vel_z, vel_x, vel_y)
 
-
 def buoyancy_terms(salt_coarse):
     face_salt = 0.5 * (salt_coarse[:-1] + salt_coarse[1:])
     zero_layer = jnp.zeros_like(salt_coarse[:1])
@@ -151,10 +137,8 @@
     below = jnp.concatenate([face_salt, zero_layer], axis=0)
     return (above, below)
 
-
 def boundary_penalty(codes):
     return jnp.where(codes == 1, sea_penalty, 0.0) + jnp.where(codes == 2, river_penalty, 0.0)
-
 
 def source_terms(coeffs, above, below, recharge_frac, codes):
     top_source = recharge_rate * recharge_frac + river_head * jnp.where(
@@ -163,8 +147,7 @@
     surface = jnp.concatenate([top_source[None], jnp.zeros_like(above[1:])], axis=0)
     return coeffs[4] * above - coeffs[5] * below + surface
 
-
-def local(salt, recharge, conductivity, codes):
+def local_shared(salt, recharge, conductivity, codes):
     layers = salt.shape[0]
     tile = salt.shape[1]
     wet = recharge.astype(jnp.float32)
@@ -232,6 +215,330 @@
     tendency = -step * change - step * dilution
     return (tendency, head)
 
+def split_dot(values, table):
+    rows = values.shape[0]
+    high = values.astype(jnp.bfloat16)
+    rest = values - high.astype(jnp.float32)
+    mid = rest.astype(jnp.bfloat16)
+    low = (rest - mid.astype(jnp.float32)).astype(jnp.bfloat16)
+    stacked = jnp.concatenate([high, mid, low], axis=0)
+    out = jnp.dot(stacked, table, preferred_element_type=jnp.float32)
+    return out[:rows] + out[rows : 2 * rows] + out[2 * rows :]
+
+def table_of(shape, same):
+    row = lax.broadcasted_iota(jnp.int32, shape, 0)
+    col = lax.broadcasted_iota(jnp.int32, shape, 1)
+    return jnp.where(same(row, col), 1.0, 0.0).astype(jnp.bfloat16)
+
+def iotas(shape):
+    return lax.broadcasted_iota(jnp.int32, shape, 0), lax.broadcasted_iota(jnp.int32, shape, 1)
+
+BLOCK = 24
+ROUNDS = (8, 4, 2, 1)
+
+def pack_kernel(salt_ref, recharge_ref, cond_ref, codes_ref, block_ref, inner_ref, outer_ref, flat_ref):
+    even = lax.rem(lax.axis_index("gx"), 2) == 0
+    for j in range(2):
+        first = salt_ref[:, j, :]
+        last = salt_ref[:, 6 + j, :]
+        inner_ref[j] = jnp.where(even, last, first)
+        outer_ref[j] = jnp.where(even, first, last)
+    sums = table_of((256, 128), lambda r, c: r // 4 == c // 2)
+    salt_y = split_dot(salt_ref[...].reshape(64, 256), sums).reshape(8, 8, 128)
+    sub, lane = iotas((8, 128))
+    mine = sub // 4 == lane % 2
+    block_ref[0:8, :] = jnp.sum(jnp.where(mine[None], salt_y, 0.0), axis=1) * 0.0625
+    wet_y = jnp.dot(
+        recharge_ref[...].astype(jnp.float32).astype(jnp.bfloat16), sums, preferred_element_type=jnp.float32
+    )
+    wet_row = jnp.sum(jnp.where(mine, wet_y, 0.0), axis=0, keepdims=True) * 0.0625
+    for layer in range(8):
+        flat_ref[4 * layer : 4 * layer + 4, :] = cond_ref[layer]
+    spread = table_of((32, 256), lambda r, c: r == (c // 128) * 16 + (c % 128) // 8)
+    cond_x = split_dot(flat_ref[...], spread)
+    row32, lane32 = iotas((32, 256))
+    cond_x = jnp.where(row32 // 4 == lane32 % 8, cond_x, 0.0)
+    summed = cond_x[0:8] + cond_x[8:16] + cond_x[16:24] + cond_x[24:32]
+    summed = summed + pltpu.roll(summed, 4, 0)
+    block_ref[pl.ds(8, 4, stride=2), :] = summed[0:4, 0:128]
+    block_ref[pl.ds(9, 4, stride=2), :] = summed[0:4, 128:256]
+    spread_codes = table_of((32, 128), lambda r, c: r == 16 * ((7 - c % 8) % 2) + c // 8)
+    code_x = jnp.dot(
+        codes_ref[...].astype(jnp.float32).astype(jnp.bfloat16), spread_codes, preferred_element_type=jnp.float32
+    )
+    row4, lane4 = iotas((4, 128))
+    code_row = jnp.sum(jnp.where(row4 == (7 - lane4 % 8) // 2, code_x, 0.0), axis=0, keepdims=True)
+    block_ref[16:24, :] = jnp.where(sub == 0, wet_row, jnp.where(sub == 1, code_row, 0.0))
+
+def harm(first, second):
+    return 2.0 * first * second / (first + second)
+
+def slope_of(back, ahead):
+    return jnp.maximum(jnp.minimum(back, ahead), 0.0) + jnp.minimum(jnp.maximum(back, ahead), 0.0)
+
+def east_of(cells, k):
+    return cells[k + 1] if k + 1 < len(cells) else pltpu.roll(cells[0], 127, 1)
+
+def west_of(cells, k):
+    return cells[k - 1] if k > 0 else pltpu.roll(cells[-1], 1, 1)
+
+def step_kernel(
+    gathered_ref, inner_ref, outer_ref, salt_ref, recharge_ref, tendency_ref, head_ref, fine_ref, coarse_ref, turn_ref, wide_ref
+):
+    device = lax.axis_index("gx")
+    sub, lane = iotas((8, 128))
+    top = sub == 0
+    low_g = lane % 2 == 0
+    blocks = []
+    for e in range(16):
+        apart = device ^ e
+        place = 0
+        for bit, distance in enumerate(ROUNDS):
+            place = place + jnp.where((apart & distance) != 0, 1 << bit, 0)
+        blocks.append(pl.multiple_of(place * BLOCK, 8))
+
+    cond_rows = jnp.concatenate([gathered_ref[pl.ds(b + 8, 8), :] for b in blocks], axis=0)
+    cond_all = cond_rows.T
+    cond = [cond_all[8 * k : 8 * k + 8] for k in range(16)]
+    code_rows = jnp.concatenate(
+        [
+            pltpu.roll(jnp.broadcast_to(gathered_ref[pl.ds(b + 17, 1), :], (8, 128)), 121, 1, stride=1, stride_axis=0)
+            for b in blocks
+        ],
+        axis=0,
+    )
+    code_all = code_rows.T
+    means = [gathered_ref[pl.ds(b, 8), :] for b in blocks]
+    wets = [gathered_ref[pl.ds(b + 16, 1), :] for b in blocks]
+
+    def by_column(per_device, mask):
+        out = []
+        for k in range(16):
+            a, b = per_device[k // 2], per_device[8 + k // 2]
+            out.append(
+                jnp.where(mask, a, pltpu.roll(b, 1, 1)) if k % 2 == 0 else jnp.where(mask, pltpu.roll(a, 127, 1), b)
+            )
+        return out
+
+    salt = by_column(means, low_g)
+    wet_frac = by_column(wets, low_g[0:1])
+
+    def coefficients(cells, penalty, hop, vertical, weight_ref):
+        count = len(cells)
+        face_e, face_n, face_d = [], [], []
+        for k in range(count):
+            e = harm(cells[k], east_of(cells, k))
+            if k == count - 1:
+                e = jnp.where(low_g, e, 0.0)
+            n = jnp.where(lane < 128 - hop, harm(cells[k], pltpu.roll(cells[k], 128 - hop, 1)), 0.0)
+            d = jnp.where(sub < 7, vertical * harm(cells[k], pltpu.roll(cells[k], 7, 0)), 0.0)
+            face_e.append(e)
+            face_n.append(n)
+            face_d.append(d)
+        diags = []
+        for k in range(count):
+            six = (
+                west_of(face_e, k),
+                face_e[k],
+                pltpu.roll(face_n[k], hop, 1),
+                face_n[k],
+                pltpu.roll(face_d[k], 1, 0),
+                face_d[k],
+            )
+            diag = six[0] + six[1] + six[2] + six[3] + six[4] + six[5] + penalty[k]
+            weight = relax_weight / diag
+            for number, face in enumerate(six):
+                weight_ref[number, k] = weight * face
+            weight_ref[6, k] = diag * (1.0 / relax_weight)
+            weight_ref[7, k] = weight
+            diags.append(weight)
+        return face_e, face_n, face_d, diags
+
+    def relaxed(cells, hop, weight_ref, source_ref):
+        out = []
+        for k in range(len(cells)):
+            here = cells[k]
+            pairs = (
+                west_of(cells, k),
+                east_of(cells, k),
+                pltpu.roll(here, hop, 1),
+                pltpu.roll(here, 128 - hop, 1),
+                pltpu.roll(here, 1, 0),
+                pltpu.roll(here, 7, 0),
+            )
+            terms = [weight_ref[number, k] * pair for number, pair in enumerate(pairs)]
+            base = (1.0 - relax_weight) * here + source_ref[8, k]
+            out.append(((terms[0] + terms[1]) + (terms[2] + terms[3])) + ((terms[4] + terms[5]) + base))
+        return out
+
+    odd_y = (lane // 2) % 2 == 1
+
+    def pair_sums(cells):
+        out = []
+        for k in range(0, len(cells), 2):
+            both = cells[k] + cells[k + 1]
+            out.append(both + jnp.where(odd_y, pltpu.roll(both, 2, 1), pltpu.roll(both, 126, 1)))
+        return out
+
+    penalty, river = [], []
+    for k in range(16):
+        code = code_all[8 * k : 8 * k + 8]
+        river.append(jnp.where(top & (code == 2.0), river_penalty, 0.0))
+        penalty.append(jnp.where(top & (code == 1.0), sea_penalty, 0.0) + river[k])
+    face_e, face_n, face_d, weights = coefficients(cond, penalty, 2, vertical_ratio, fine_ref)
+    drop = []
+    for k in range(16):
+        below = jnp.where(sub < 7, 0.5 * (salt[k] + pltpu.roll(salt[k], 7, 0)), 0.0)
+        drop.append(below)
+        pull = face_d[k] * below
+        source = jnp.where(top, recharge_rate * wet_frac[k] + river_head * river[k], 0.0)
+        fine_ref[8, k] = weights[k] * (pltpu.roll(pull, 1, 0) - pull + source)
+        fine_ref[9, k] = face_e[k]
+        fine_ref[10, k] = face_n[k]
+        fine_ref[11, k] = face_d[k]
+        fine_ref[12, k] = below
+    coefficients([0.25 * c for c in pair_sums(cond)], pair_sums(penalty), 4, 4.0 * vertical_ratio, coarse_ref)
+
+    head = None
+    for cycle_no in range(CYCLES):
+        for sweep in range(SMOOTH):
+            head = [fine_ref[8, k] for k in range(16)] if head is None else relaxed(head, 2, fine_ref, fine_ref)
+        ahead = relaxed(head, 2, fine_ref, fine_ref)
+        resid = pair_sums([(ahead[k] - head[k]) * fine_ref[6, k] for k in range(16)])
+        correction = []
+        for k in range(8):
+            correction.append(coarse_ref[7, k] * resid[k])
+            coarse_ref[8, k] = correction[k]
+        for sweep in range(COARSE_SWEEPS - 1):
+            correction = relaxed(correction, 4, coarse_ref, coarse_ref)
+        head = [head[k] + correction[k // 2] for k in range(16)]
+        for sweep in range(SMOOTH):
+            head = relaxed(head, 2, fine_ref, fine_ref)
+
+    turn_ref[...] = jnp.concatenate(head, axis=0).T
+    rows = turn_ref[pl.ds(pl.multiple_of(8 * device, 8), 8), :]
+    copies = jnp.concatenate([rows] * 8, axis=0)
+    row64, lane64 = iotas((64, 128))
+    picked = split_dot(
+        jnp.where(row64 // 8 == lane64 % 8, copies, 0.0), table_of((128, 128), lambda r, c: r // 8 == c % 16)
+    )
+    turn_ref[0:64, :] = picked
+    lane32 = lax.broadcasted_iota(jnp.int32, (32, 128), 1)
+    own = jnp.where(lane32 < 16, turn_ref[pl.ds(0, 32, stride=2), :], turn_ref[pl.ds(1, 32, stride=2), :])[:, 0:32]
+    for layer in range(8):
+        head_ref[layer] = own[4 * layer : 4 * layer + 4]
+
+    flow_e, flow_n, flow_d = [], [], []
+    for k in range(16):
+        flow_e.append(fine_ref[9, k] * (head[k] - east_of(head, k)))
+        flow_n.append(fine_ref[10, k] * (head[k] - pltpu.roll(head[k], 126, 1)))
+        flow_d.append(fine_ref[11, k] * (head[k] - pltpu.roll(head[k], 7, 0) + fine_ref[12, k]))
+    largest = None
+    for k in range(16):
+        vel_x = 0.5 * (west_of(flow_e, k) + flow_e[k])
+        vel_y = 0.5 * (pltpu.roll(flow_n[k], 2, 1) + flow_n[k])
+        vel_z = 0.5 * (pltpu.roll(flow_d[k], 1, 0) + flow_d[k])
+        wide_ref[0, k] = vel_x
+        wide_ref[1, k] = vel_y
+        wide_ref[2, k] = vel_z
+        speed = jnp.abs(vel_x) + jnp.abs(vel_y) + jnp.abs(vel_z)
+        largest = speed if largest is None else jnp.maximum(largest, speed)
+    step = courant / (jnp.max(largest, axis=(0, 1), keepdims=True) + 1e-06)
+
+    columns = []
+    for field, wanted in ((0, (0, 1, 2, 3)), (1, (1, 2)), (2, (1, 2))):
+        for j in wanted:
+            x = jnp.clip(2 * device - 1 + j, 0, 31)
+            columns.append(jnp.where(lane % 2 == x // 16, wide_ref[field, lax.rem(x, 16)], 0.0))
+    spread = split_dot(jnp.concatenate(columns, axis=0), table_of((128, 256), lambda r, c: r // 2 == c // 4))
+    speed_x = [spread[8 * j : 8 * j + 8] for j in range(4)]
+    speed_y = [spread[32 + 8 * j : 40 + 8 * j] for j in range(2)]
+    speed_z = [spread[48 + 8 * j : 56 + 8 * j] for j in range(2)]
+
+    layer, column = iotas((8, 256))
+    even = lax.rem(device, 2) == 0
+    cells = (
+        [jnp.where(even, outer_ref[j], inner_ref[j]) for j in range(2)]
+        + [salt_ref[:, x, :] for x in range(8)]
+        + [jnp.where(even, inner_ref[j], outer_ref[j]) for j in range(2)]
+    )
+    diffs = [cells[i + 1] - cells[i] for i in range(11)]
+    halves = [0.5 * slope_of(diffs[i], diffs[i + 1]) for i in range(10)]
+    flux_x = []
+    for f in range(9):
+        if f % 4 == 0:
+            face = 0.5 * (speed_x[f // 4] + speed_x[f // 4 + 1])
+            if f == 0:
+                face = jnp.where(device == 0, 0.0, face)
+            if f == 8:
+                face = jnp.where(device == 15, 0.0, face)
+        else:
+            face = speed_x[1 + f // 4]
+        flux_x.append(face * jnp.where(face > 0, cells[f + 1] + halves[f], cells[f + 2] - halves[f + 1]))
+    faces_y = [jnp.where(column < 255, 0.5 * (v + pltpu.roll(v, 255, 1)), 0.0) for v in speed_y]
+    faces_z = [jnp.where(layer < 7, 0.5 * (v + pltpu.roll(v, 7, 0)), 0.0) for v in speed_z]
+    for x in range(8):
+        cell = cells[x + 2]
+        ahead = jnp.where(layer < 7, pltpu.roll(cell, 7, 0), 0.0) - cell
+        half = 0.5 * slope_of(jnp.where(layer > 0, pltpu.roll(ahead, 1, 0), cell), ahead)
+        face = faces_z[x // 4]
+        flux_z = face * jnp.where(face > 0, cell + half, pltpu.roll(cell - half, 7, 0))
+        change = flux_z - pltpu.roll(flux_z, 1, 0)
+        change = change + (flux_x[x + 1] - flux_x[x])
+        ahead = jnp.where(column < 255, pltpu.roll(cell, 255, 1), 0.0) - cell
+        half = 0.5 * slope_of(jnp.where(column > 0, pltpu.roll(ahead, 1, 1), cell), ahead)
+        face = faces_y[x // 4]
+        flux_y = face * jnp.where(face > 0, cell + half, pltpu.roll(cell - half, 255, 1))
+        change = change + (flux_y - pltpu.roll(flux_y, 1, 1))
+        wet = recharge_ref[x : x + 1, :].astype(jnp.float32)
+        dilution = jnp.where(layer == 0, freshening * wet * cell, 0.0)
+        tendency_ref[:, x, :] = -step * change - step * dilution
+
+def local_small(salt, recharge, conductivity, codes):
+    vmem = pl.BlockSpec(memory_space=pltpu.VMEM)
+    pair = jax.ShapeDtypeStruct((2, 8, 256), jnp.float32)
+    block, inner, outer = pl.pallas_call(
+        pack_kernel,
+        out_shape=(jax.ShapeDtypeStruct((BLOCK, 128), jnp.float32), pair, pair),
+        in_specs=[vmem] * 4,
+        out_specs=(vmem,) * 3,
+        scratch_shapes=[pltpu.VMEM((32, 32), jnp.float32)],
+        name="pack",
+    )(salt, recharge, conductivity, codes)
+    count = lax.axis_size("gx")
+    inner = lax.ppermute(inner, "gx", [(i, i ^ 1) for i in range(count)])
+    outer_pairs = [(i, i + 1) for i in range(1, count - 1, 2)]
+    outer = lax.ppermute(outer, "gx", outer_pairs + [(j, i) for i, j in outer_pairs])
+    for distance in ROUNDS:
+        other = lax.ppermute(block, "gx", [(i, i ^ distance) for i in range(count)])
+        block = jnp.concatenate([block, other], axis=0)
+    return pl.pallas_call(
+        step_kernel,
+        out_shape=(
+            jax.ShapeDtypeStruct(salt.shape, jnp.float32),
+            jax.ShapeDtypeStruct(conductivity.shape, jnp.float32),
+        ),
+        in_specs=[vmem] * 5,
+        out_specs=(vmem,) * 2,
+        scratch_shapes=[
+            pltpu.VMEM((13, 16, 8, 128), jnp.float32),
+            pltpu.VMEM((9, 8, 8, 128), jnp.float32),
+            pltpu.VMEM((128, 128), jnp.float32),
+            pltpu.VMEM((3, 16, 8, 128), jnp.float32),
+        ],
+        compiler_params=pltpu.CompilerParams(vmem_limit_bytes=16 * 1024 * 1024),
+        name="step",
+    )(block, inner, outer, salt, recharge)
+
+def local(salt, recharge, conductivity, codes):
+    small = (
+        lax.axis_size("gx") == 16
+        and salt.shape == (8, 8, 256)
+        and recharge.shape == (8, 256)
+        and conductivity.shape == (8, 4, 32)
+        and codes.shape == (4, 32)
+    )
+    return (local_small if small else local_shared)(salt, recharge, conductivity, codes)
 
 def solution(mesh):
     return jax.shard_map(

time: 254 us -> 23 us (0.09)
  starting transfers between devices: 178 us -> 10.2 us
  blocking collectives: 34.5 us -> 0 us
  waiting for transfers between devices: 20.1 us -> 6.24 us
  local copies, waits for them, and re-layouts: 10.6 us -> 0.75 us
  other arithmetic: 6.21 us -> 0.01 us
  Pallas kernels: 0 us -> 4.81 us
    ppermute x50 -> x6, starting transfers between devices: 155 us -> 10.2 us  [the longest x4 9.42 us: local_small(): other = lax.ppermute(block, 'gx', [(i, i ^ distance) for i in range(count)])]
    pmax x1 -> x0, blocking collectives: 34.5 us -> none  [local(): fastest = lax.pmax(local_fastest, 'gx')]
    all_to_all x2 -> x0, starting transfers between devices: 23.7 us -> none  [the longest x1 14.3 us: local(): lax.all_to_all(packed, 'gx', split_axis=3, concat_axis=2, tiled=True)]
    ppermute x50 -> x6, waiting for transfers between devices: 18.8 us -> 6.24 us  [the longest x4 6.24 us: local_small(): other = lax.ppermute(block, 'gx', [(i, i ^ distance) for i in range(count)])]
    pallas_call x0 -> x2, Pallas kernels: none -> 4.81 us  [the longest x1 3.14 us: local_small(): pl.pallas_call(step_kernel, out_shape=(jax.ShapeDtypeStruct(salt.shape, j...]
    unnamed x15 -> x10, local copies, waits for them, and re-layouts: 4.11 us -> 0.74 us
  transfers between devices with their start and end apart: 52 -> 6, of which waited for: 22 -> 4; matrix products, arithmetic and copies ran while one was open for 2% -> 3% of each run, Pallas kernels for 0% -> 0%
where the time goes in v1:
time: 23 us; the launch traced here: 22.7 us
  starting transfers between devices  10.2 us (44%)
  waiting for transfers between devices  6.24 us (27%)
  Pallas kernels  4.81 us (21%)
  local copies, waits for them, and re-layouts  0.75 us (3%)
  between operations  0.72 us (3%)
    ppermute x4, starting transfers between devices, local_small(): other = lax.ppermute(block, 'gx', [(i, i ^ distance) for i in range(count)])  9.42 us
    ppermute x4, waiting for transfers between devices, local_small(): other = lax.ppermute(block, 'gx', [(i, i ^ distance) for i in range(count)])  6.24 us
    pallas_call x1, Pallas kernels, local_small(): pl.pallas_call(step_kernel, out_shape=(jax.ShapeDtypeStruct(salt.shape, j...  3.14 us
    pallas_call x1, Pallas kernels, local_small(): pl.pallas_call(pack_kernel, out_shape=(jax.ShapeDtypeStruct((BLOCK, 128),...  1.67 us
    ppermute x1, starting transfers between devices, local_small(): lax.ppermute(outer, 'gx', outer_pairs + [(j, i) for i, j in outer_pairs])  0.78 us
    unnamed x10, local copies, waits for them, and re-layouts  0.74 us
  transfers between devices with their start and end apart: 6, of which 4 were waited for; matrix products, arithmetic and copies ran while one was open for 3% of the time, Pallas kernels for 0%

profile of v1, /device:TPU:0, one launch (start us, length us, event | category | flops | bytes accessed | tf_op | source)
XLA Modules:
  0.0 22.7 jit_solution(1474445853341666158)
XLA Ops:
  0.6 1.7 %pack.1 = (f32[24,128]{1,0:T(8,128)}, f32[2,8,256]{2,1,0:T(8,128)}, f32[2,8,256]{2,1,0:T(8,128)}) custom-call(f32[8,8,256]{2,1,0:T(8,128)} %salt_ref.3, s32[8,256]{1,0:T(8,128)} %recharge_ref.3, f32[8,4,32]{2,1,0:T(4,128)} %cond_ref.1, s32[4,32]{1,0:T(4,128)} %codes_ref.1), custom_call_target="tpu_custom_call" | custom-call | tf_op jit(solution)/shard_map/pack/pallas_call | solution.py:500
  2.3 4.0 %collective-permute-start = (f32[24,128]{1,0:T(8,128)}, f32[24,128]{1,0:T(8,128)S(1)}, u32[]{:S(2)}, u32[]{:S(2)}) collective-permute-start(f32[24,128]{1,0:T(8,128)} %get-tuple-element.5), channel_id=1, source_target_pairs={{0,8},{1,9},{2,10},{3,11},{4,12},{5,13},{6,14},{7,15},{8,0},{9,1},... | collective-permute-start | bytes 36872 | tf_op jit(solution)/shard_map/ppermute | solution.py:513
  6.3 0.0 collective-permute-start.4
  6.3 0.0 copy-start.2
  6.3 0.8 %collective-permute-start.5 = (f32[2,8,256]{2,1,0:T(8,128)}, f32[2,8,256]{2,1,0:T(8,128)S(1)}, u32[]{:S(2)}, u32[]{:S(2)}) collective-permute-start(f32[2,8,256]{2,1,0:T(8,128)} %get-tuple-element.7), channel_id=1, source_target_pairs={{1,2},{3,4},{5,6},{7,8},{9,10},{11,12},{13,14},{2,1},{4,3},{6,5},{... | collective-permute-start | bytes 49160 | tf_op jit(solution)/shard_map/ppermute | solution.py:511
  7.1 0.7 %constant_dynamic-update-slice_fusion.4 = f32[384,128]{1,0:T(8,128)S(1)} fusion(f32[24,128]{1,0:T(8,128)} %get-tuple-element.5), kind=kLoop, calls=%fused_computation.7 | loop fusion | bytes 24576
  7.8 0.4 %collective-permute-done = f32[24,128]{1,0:T(8,128)S(1)} collective-permute-done((f32[24,128]{1,0:T(8,128)}, f32[24,128]{1,0:T(8,128)S(1)}, u32[]{:S(2)}, u32[]{:S(2)}) %collective-permute-start) | collective-permute-done | bytes 12320 | tf_op jit(solution)/shard_map/ppermute | solution.py:513
  8.2 0.0 copy-done.2
  8.2 4.0 %collective-permute-start.1 = (f32[48,128]{1,0:T(8,128)S(1)}, f32[48,128]{1,0:T(8,128)S(1)}, u32[]{:S(2)}, u32[]{:S(2)}) collective-permute-start(f32[48,128]{1,0:T(8,128)S(1)} %pad_maximum_fusion.2), channel_id=1, source_target_pairs={{0,4},{1,5},{2,6},{3,7},{4,0},{5,1},{6,2},{7,3},{8,12},{9,13},{10,... | collective-permute-start | bytes 73736 | tf_op jit(solution)/shard_map/ppermute | solution.py:513
  12.3 1.8 %collective-permute-done.1 = f32[48,128]{1,0:T(8,128)S(1)} collective-permute-done((f32[48,128]{1,0:T(8,128)S(1)}, f32[48,128]{1,0:T(8,128)S(1)}, u32[]{:S(2)}, u32[]{:S(2)}) %collective-permute-start.1) | collective-permute-done | bytes 24608 | tf_op jit(solution)/shard_map/ppermute | solution.py:513
  14.1 1.3 %collective-permute-start.2 = (f32[96,128]{1,0:T(8,128)S(1)}, f32[96,128]{1,0:T(8,128)S(1)}, u32[]{:S(2)}, u32[]{:S(2)}) collective-permute-start(f32[96,128]{1,0:T(8,128)S(1)} %pad_maximum_fusion.1), channel_id=1, source_target_pairs={{0,2},{1,3},{2,0},{3,1},{4,6},{5,7},{6,4},{7,5},{8,10},{9,11},{10,... | collective-permute-start | bytes 147464 | tf_op jit(solution)/shard_map/ppermute | solution.py:513
  15.4 2.8 %collective-permute-done.2 = f32[96,128]{1,0:T(8,128)S(1)} collective-permute-done((f32[96,128]{1,0:T(8,128)S(1)}, f32[96,128]{1,0:T(8,128)S(1)}, u32[]{:S(2)}, u32[]{:S(2)}) %collective-permute-start.2) | collective-permute-done | bytes 49184 | tf_op jit(solution)/shard_map/ppermute | solution.py:513
  18.2 0.1 collective-permute-start.3
  18.3 0.0 copy-start
  18.3 0.0 copy-start.1
  18.3 1.2 %collective-permute-done.3 = f32[192,128]{1,0:T(8,128)S(1)} collective-permute-done((f32[192,128]{1,0:T(8,128)S(1)}, f32[192,128]{1,0:T(8,128)S(1)}, u32[]{:S(2)}, u32[]{:S(2)}) %collective-permute-start.3) | collective-permute-done | bytes 98336 | tf_op jit(solution)/shard_map/ppermute | solution.py:513
  19.6 0.0 collective-permute-done.4.inner_ref
  19.6 0.0 collective-permute-done.5.outer_ref
  19.6 0.0 copy-done
  19.6 0.0 copy-done.1
  19.6 3.1 %step.1 = (f32[8,8,256]{2,1,0:T(8,128)}, f32[8,4,32]{2,1,0:T(4,128)}) custom-call(f32[384,128]{1,0:T(8,128)S(1)} %constant_dynamic-update-slice_fusion.gathered_ref, f32[2,8,256]{2,1,0:T(8,128)S(1)} %collective-permute-done.4.inner_ref, f32[2,8,256]{2,1,0:T(8,128)S(1)} %collective-permute-done.5.outer_ref, f32[8,8,256]{2,1,0:T(8,128)S(1)} %copy-done, ...), custom_call_target="tpu_custom_call" | custom-call | tf_op jit(solution)/shard_map/step/pallas_call | solution.py:515
  (7 shorter events, 0.0 us)
Async XLA Ops:
  2.3 5.9 %collective-permute-start = (f32[24,128]{1,0:T(8,128)}, f32[24,128]{1,0:T(8,128)S(1)}, u32[]{:S(2)}, u32[]{:S(2)}) collective-permute-start(f32[24,128]{1,0:T(8,128)} %get-tuple-element.5), channel_id=1, source_target_pairs={{0,8},{1,9},{2,10},{3,11},{4,12},{5,13},{6,14},{7,15},{8,0},{9,1},... | collective-permute-start | bytes 36872 | tf_op jit(solution)/shard_map/ppermute | solution.py:513
  6.3 13.2 %collective-permute-start.4 = (f32[2,8,256]{2,1,0:T(8,128)}, f32[2,8,256]{2,1,0:T(8,128)S(1)}, u32[]{:S(2)}, u32[]{:S(2)}) collective-permute-start(f32[2,8,256]{2,1,0:T(8,128)} %get-tuple-element.6), channel_id=1, source_target_pairs={{0,1},{1,0},{2,3},{3,2},{4,5},{5,4},{6,7},{7,6},{8,9},{9,8},{10,11... | collective-permute-start | bytes 49160 | tf_op jit(solution)/shard_map/ppermute | solution.py:509
  6.3 1.9 %copy-start.2 = (f32[24,128]{1,0:T(8,128)S(1)}, f32[24,128]{1,0:T(8,128)}, u32[]{:S(2)}) copy-start(f32[24,128]{1,0:T(8,128)} %get-tuple-element.5) | copy-start | bytes 36868
  6.3 13.2 %collective-permute-start.5 = (f32[2,8,256]{2,1,0:T(8,128)}, f32[2,8,256]{2,1,0:T(8,128)S(1)}, u32[]{:S(2)}, u32[]{:S(2)}) collective-permute-start(f32[2,8,256]{2,1,0:T(8,128)} %get-tuple-element.7), channel_id=1, source_target_pairs={{1,2},{3,4},{5,6},{7,8},{9,10},{11,12},{13,14},{2,1},{4,3},{6,5},{... | collective-permute-start | bytes 49160 | tf_op jit(solution)/shard_map/ppermute | solution.py:511
  8.2 5.8 %collective-permute-start.1 = (f32[48,128]{1,0:T(8,128)S(1)}, f32[48,128]{1,0:T(8,128)S(1)}, u32[]{:S(2)}, u32[]{:S(2)}) collective-permute-start(f32[48,128]{1,0:T(8,128)S(1)} %pad_maximum_fusion.2), channel_id=1, source_target_pairs={{0,4},{1,5},{2,6},{3,7},{4,0},{5,1},{6,2},{7,3},{8,12},{9,13},{10,... | collective-permute-start | bytes 73736 | tf_op jit(solution)/shard_map/ppermute | solution.py:513
  14.1 4.1 %collective-permute-start.2 = (f32[96,128]{1,0:T(8,128)S(1)}, f32[96,128]{1,0:T(8,128)S(1)}, u32[]{:S(2)}, u32[]{:S(2)}) collective-permute-start(f32[96,128]{1,0:T(8,128)S(1)} %pad_maximum_fusion.1), channel_id=1, source_target_pairs={{0,2},{1,3},{2,0},{3,1},{4,6},{5,7},{6,4},{7,5},{8,10},{9,11},{10,... | collective-permute-start | bytes 147464 | tf_op jit(solution)/shard_map/ppermute | solution.py:513
  18.2 1.4 %collective-permute-start.3 = (f32[192,128]{1,0:T(8,128)S(1)}, f32[192,128]{1,0:T(8,128)S(1)}, u32[]{:S(2)}, u32[]{:S(2)}) collective-permute-start(f32[192,128]{1,0:T(8,128)S(1)} %pad_maximum_fusion), channel_id=1, source_target_pairs={{0,1},{1,0},{2,3},{3,2},{4,5},{5,4},{6,7},{7,6},{8,9},{9,8},{10,11... | collective-permute-start | bytes 294920 | tf_op jit(solution)/shard_map/ppermute | solution.py:513
  18.3 1.3 %copy-start = (f32[8,8,256]{2,1,0:T(8,128)S(1)}, f32[8,8,256]{2,1,0:T(8,128)}, u32[]{:S(2)}) copy-start(f32[8,8,256]{2,1,0:T(8,128)} %salt_ref.3) | copy-start | bytes 196612
  18.3 1.3 %copy-start.1 = (s32[8,256]{1,0:T(8,128)S(1)}, s32[8,256]{1,0:T(8,128)}, u32[]{:S(2)}) copy-start(s32[8,256]{1,0:T(8,128)} %recharge_ref.3) | copy-start | bytes 24580

commit v2 on v1

--- a/solution.py
+++ b/solution.py
@@ -236,13 +236,23 @@
 BLOCK = 24
 ROUNDS = (8, 4, 2, 1)
 
-def pack_kernel(salt_ref, recharge_ref, cond_ref, codes_ref, block_ref, inner_ref, outer_ref, flat_ref):
-    even = lax.rem(lax.axis_index("gx"), 2) == 0
+def pack_kernel(salt_ref, recharge_ref, cond_ref, codes_ref, block_ref, middle_ref, late_ref, inner_ref, flat_ref):
+    device = lax.axis_index("gx")
+    even = lax.rem(device, 2) == 0
+    inside = (device > 0) & (device < 15)
+    crossed = device ^ jnp.where(even, device - 1, device + 1)
     for j in range(2):
         first = salt_ref[:, j, :]
         last = salt_ref[:, 6 + j, :]
-        inner_ref[j] = jnp.where(even, last, first)
-        outer_ref[j] = jnp.where(even, first, last)
+        inward = jnp.where(even, last, first)
+        outward = jnp.where(even, first, last)
+        for half in range(2):
+            place = 8 * (2 * j + half)
+            part = outward[:, 128 * half : 128 * half + 128]
+            inner_ref[place : place + 8, :] = inward[:, 128 * half : 128 * half + 128]
+            block_ref[BLOCK + place : BLOCK + place + 8, :] = jnp.where(inside & (crossed == 15), part, 0.0)
+            middle_ref[place : place + 8, :] = jnp.where(inside & (crossed == 7), part, 0.0)
+            late_ref[place : place + 8, :] = jnp.where(inside & (crossed == 3), part, 0.0)
     sums = table_of((256, 128), lambda r, c: r // 4 == c // 2)
     salt_y = split_dot(salt_ref[...].reshape(64, 256), sums).reshape(8, 8, 128)
     sub, lane = iotas((8, 128))
@@ -283,33 +293,37 @@
     return cells[k - 1] if k > 0 else pltpu.roll(cells[-1], 1, 1)
 
 def step_kernel(
-    gathered_ref, inner_ref, outer_ref, salt_ref, recharge_ref, tendency_ref, head_ref, fine_ref, coarse_ref, turn_ref, wide_ref
+    near_ref, far_ref, salt_ref, recharge_ref, tendency_ref, head_ref, fine_ref, coarse_ref, turn_ref, wide_ref
 ):
     device = lax.axis_index("gx")
     sub, lane = iotas((8, 128))
     top = sub == 0
     low_g = lane % 2 == 0
+    even = lax.rem(device, 2) == 0
     blocks = []
-    for e in range(16):
+    for e in range(0, 16, 2):
         apart = device ^ e
         place = 0
-        for bit, distance in enumerate(ROUNDS):
+        for bit, distance in enumerate(ROUNDS[:3]):
             place = place + jnp.where((apart & distance) != 0, 1 << bit, 0)
-        blocks.append(pl.multiple_of(place * BLOCK, 8))
-
-    cond_rows = jnp.concatenate([gathered_ref[pl.ds(b + 8, 8), :] for b in blocks], axis=0)
+        start = pl.multiple_of(place * BLOCK, 8)
+        near = near_ref[pl.ds(start, BLOCK), :]
+        far = far_ref[pl.ds(start, BLOCK), :]
+        blocks += [jnp.where(even, near, far), jnp.where(even, far, near)]
+
+    cond_rows = jnp.concatenate([b[8:16] for b in blocks], axis=0)
     cond_all = cond_rows.T
     cond = [cond_all[8 * k : 8 * k + 8] for k in range(16)]
     code_rows = jnp.concatenate(
         [
-            pltpu.roll(jnp.broadcast_to(gathered_ref[pl.ds(b + 17, 1), :], (8, 128)), 121, 1, stride=1, stride_axis=0)
+            pltpu.roll(jnp.broadcast_to(b[17:18], (8, 128)), 121, 1, stride=1, stride_axis=0)
             for b in blocks
         ],
         axis=0,
     )
     code_all = code_rows.T
-    means = [gathered_ref[pl.ds(b, 8), :] for b in blocks]
-    wets = [gathered_ref[pl.ds(b + 16, 1), :] for b in blocks]
+    means = [b[0:8] for b in blocks]
+    wets = [b[16:17] for b in blocks]
 
     def by_column(per_device, mask):
         out = []
@@ -456,11 +470,14 @@
     speed_z = [spread[48 + 8 * j : 56 + 8 * j] for j in range(2)]
 
     layer, column = iotas((8, 256))
-    even = lax.rem(device, 2) == 0
+    halo = [
+        jnp.concatenate([far_ref[192 + 16 * i : 200 + 16 * i, :], far_ref[200 + 16 * i : 208 + 16 * i, :]], axis=1)
+        for i in range(4)
+    ]
     cells = (
-        [jnp.where(even, outer_ref[j], inner_ref[j]) for j in range(2)]
+        [jnp.where(even, halo[j], halo[2 + j]) for j in range(2)]
         + [salt_ref[:, x, :] for x in range(8)]
-        + [jnp.where(even, inner_ref[j], outer_ref[j]) for j in range(2)]
+        + [jnp.where(even, halo[2 + j], halo[j]) for j in range(2)]
     )
     diffs = [cells[i + 1] - cells[i] for i in range(11)]
     halves = [0.5 * slope_of(diffs[i], diffs[i + 1]) for i in range(10)]
@@ -496,29 +513,33 @@
 
 def local_small(salt, recharge, conductivity, codes):
     vmem = pl.BlockSpec(memory_space=pltpu.VMEM)
-    pair = jax.ShapeDtypeStruct((2, 8, 256), jnp.float32)
-    block, inner, outer = pl.pallas_call(
+    columns = jax.ShapeDtypeStruct((32, 128), jnp.float32)
+    block, middle, late, inner = pl.pallas_call(
         pack_kernel,
-        out_shape=(jax.ShapeDtypeStruct((BLOCK, 128), jnp.float32), pair, pair),
+        out_shape=(jax.ShapeDtypeStruct((BLOCK + 32, 128), jnp.float32), columns, columns, columns),
         in_specs=[vmem] * 4,
-        out_specs=(vmem,) * 3,
+        out_specs=(vmem,) * 4,
         scratch_shapes=[pltpu.VMEM((32, 32), jnp.float32)],
         name="pack",
     )(salt, recharge, conductivity, codes)
-    count = lax.axis_size("gx")
-    inner = lax.ppermute(inner, "gx", [(i, i ^ 1) for i in range(count)])
-    outer_pairs = [(i, i + 1) for i in range(1, count - 1, 2)]
-    outer = lax.ppermute(outer, "gx", outer_pairs + [(j, i) for i, j in outer_pairs])
-    for distance in ROUNDS:
-        other = lax.ppermute(block, "gx", [(i, i ^ distance) for i in range(count)])
-        block = jnp.concatenate([block, other], axis=0)
+
+    def swapped(array, distance):
+        return lax.ppermute(array, "gx", [(i, i ^ distance) for i in range(lax.axis_size("gx"))])
+
+    other = swapped(block, ROUNDS[0])
+    block = jnp.concatenate([block[:BLOCK], other[:BLOCK], other[BLOCK:] + middle])
+    other = swapped(block, ROUNDS[1])
+    block = jnp.concatenate([block[: 2 * BLOCK], other[: 2 * BLOCK], other[2 * BLOCK :] + late])
+    other = swapped(block, ROUNDS[2])
+    block = jnp.concatenate([block[: 4 * BLOCK], other, inner])
+    other = swapped(block, ROUNDS[3])
     return pl.pallas_call(
         step_kernel,
         out_shape=(
             jax.ShapeDtypeStruct(salt.shape, jnp.float32),
             jax.ShapeDtypeStruct(conductivity.shape, jnp.float32),
         ),
-        in_specs=[vmem] * 5,
+        in_specs=[vmem] * 4,
         out_specs=(vmem,) * 2,
         scratch_shapes=[
             pltpu.VMEM((13, 16, 8, 128), jnp.float32),
@@ -528,7 +549,7 @@
         ],
         compiler_params=pltpu.CompilerParams(vmem_limit_bytes=16 * 1024 * 1024),
         name="step",
-    )(block, inner, outer, salt, recharge)
+    )(block, other, salt, recharge)
 
 def local(salt, recharge, conductivity, codes):
     small = (

time: 23 us -> 22.4 us (0.974)
  starting transfers between devices: 10.2 us -> 8.09 us
  waiting for transfers between devices: 6.24 us -> 7.02 us
  local copies, waits for them, and re-layouts: 0.75 us -> 1.48 us
    ppermute x6 -> x4, starting transfers between devices: 10.2 us -> 8.09 us  [swapped(): lax.ppermute(array, 'gx', [(i, i ^ distance) for i in range(lax.axis_size...]
    ppermute x6 -> x4, waiting for transfers between devices: 6.24 us -> 7.02 us  [swapped(): lax.ppermute(array, 'gx', [(i, i ^ distance) for i in range(lax.axis_size...]
    slice x0 -> x3, local copies, waits for them, and re-layouts: none -> 0.75 us  [the longest x1 0.74 us: local_small(): block[:BLOCK]]
    unnamed x10 -> x11, local copies, waits for them, and re-layouts: 0.74 us -> 0.73 us
  transfers between devices with their start and end apart: 6 -> 4, of which waited for: 4 -> 4; matrix products, arithmetic and copies ran while one was open for 3% -> 3% of each run, Pallas kernels for 0% -> 0%
where the time goes in v2:
time: 22.4 us; the launch traced here: 22.1 us
  starting transfers between devices  8.09 us (36%)
  waiting for transfers between devices  7.02 us (31%)
  Pallas kernels  4.78 us (21%)
  local copies, waits for them, and re-layouts  1.48 us (7%)
  between operations  0.68 us (3%)
    ppermute x4, starting transfers between devices, swapped(): lax.ppermute(array, 'gx', [(i, i ^ distance) for i in range(lax.axis_size...  8.09 us
    ppermute x4, waiting for transfers between devices, swapped(): lax.ppermute(array, 'gx', [(i, i ^ distance) for i in range(lax.axis_size...  7.02 us
    pallas_call x1, Pallas kernels, local_small(): pl.pallas_call(step_kernel, out_shape=(jax.ShapeDtypeStruct(salt.shape, j...  3.09 us
    pallas_call x1, Pallas kernels, local_small(): pl.pallas_call(pack_kernel, out_shape=(jax.ShapeDtypeStruct((BLOCK + 32,...  1.69 us
    slice x1, local copies, waits for them, and re-layouts, local_small(): block[:BLOCK]  0.74 us
    unnamed x11, local copies, waits for them, and re-layouts  0.73 us
  transfers between devices with their start and end apart: 4, of which 4 were waited for; matrix products, arithmetic and copies ran while one was open for 3% of the time, Pallas kernels for 0%

profile of v2, /device:TPU:0, one launch (start us, length us, event | category | flops | bytes accessed | tf_op | source)
XLA Modules:
  0.0 22.1 jit_solution(7182951327979113834)
XLA Ops:
  0.6 1.7 %pack.1 = (f32[56,128]{1,0:T(8,128)}, f32[32,128]{1,0:T(8,128)}, f32[32,128]{1,0:T(8,128)}, f32[32,128]{1,0:T(8,128)}) custom-call(f32[8,8,256]{2,1,0:T(8,128)} %salt_ref.3, s32[8,256]{1,0:T(8,128)} %recharge_ref.3, f32[8,4,32]{2,1,0:T(4,128)} %cond_ref.1, s32[4,32]{1,0:T(4,128)} %codes_ref.1), custom_call_target="tpu_custom_call" | custom-call | tf_op jit(solution)/shard_map/pack/pallas_call | solution.py:517
  2.3 0.0 copy-start.3
  2.3 4.0 %collective-permute-start = (f32[56,128]{1,0:T(8,128)}, f32[56,128]{1,0:T(8,128)S(1)}, u32[]{:S(2)}, u32[]{:S(2)}) collective-permute-start(f32[56,128]{1,0:T(8,128)} %get-tuple-element.6), channel_id=1, source_target_pairs={{0,8},{1,9},{2,10},{3,11},{4,12},{5,13},{6,14},{7,15},{8,0},{9,1},... | collective-permute-start | bytes 86024 | tf_op jit(solution)/shard_map/ppermute | solution.py:527
  6.4 0.7 %fusion.1 = (f32[24,128]{1,0:T(8,128)S(1)}, f32[256,128]{1,0:T(8,128)S(1)}) fusion(f32[56,128]{1,0:T(8,128)} %get-tuple-element.6), kind=kLoop, calls=%fused_computation.10 | loop fusion | bytes 36864 | tf_op jit(solution)/shard_map/slice | solution.py:530
  7.1 1.3 %collective-permute-done = f32[56,128]{1,0:T(8,128)S(1)} collective-permute-done((f32[56,128]{1,0:T(8,128)}, f32[56,128]{1,0:T(8,128)S(1)}, u32[]{:S(2)}, u32[]{:S(2)}) %collective-permute-start) | collective-permute-done | bytes 28704 | tf_op jit(solution)/shard_map/ppermute | solution.py:527
  8.4 0.0 copy-done.3
  8.4 0.0 copy-start.2
  8.5 2.0 %collective-permute-start.1 = (f32[80,128]{1,0:T(8,128)S(1)}, f32[80,128]{1,0:T(8,128)S(1)}, u32[]{:S(2)}, u32[]{:S(2)}) collective-permute-start(f32[80,128]{1,0:T(8,128)S(1)} %pad_maximum_fusion.1), channel_id=1, source_target_pairs={{0,4},{1,5},{2,6},{3,7},{4,0},{5,1},{6,2},{7,3},{8,12},{9,13},{10,... | collective-permute-start | bytes 122888 | tf_op jit(solution)/shard_map/ppermute | solution.py:527
  10.4 2.1 %collective-permute-done.1 = f32[80,128]{1,0:T(8,128)S(1)} collective-permute-done((f32[80,128]{1,0:T(8,128)S(1)}, f32[80,128]{1,0:T(8,128)S(1)}, u32[]{:S(2)}, u32[]{:S(2)}) %collective-permute-start.1) | collective-permute-done | bytes 40992 | tf_op jit(solution)/shard_map/ppermute | solution.py:527
  12.5 0.0 copy-done.2
  12.6 2.1 %collective-permute-start.2 = (f32[128,128]{1,0:T(8,128)S(1)}, f32[128,128]{1,0:T(8,128)S(1)}, u32[]{:S(2)}, u32[]{:S(2)}) collective-permute-start(f32[128,128]{1,0:T(8,128)S(1)} %pad_maximum_fusion), channel_id=1, source_target_pairs={{0,2},{1,3},{2,0},{3,1},{4,6},{5,7},{6,4},{7,5},{8,10},{9,11},{10,... | collective-permute-start | bytes 196616 | tf_op jit(solution)/shard_map/ppermute | solution.py:527
  14.7 2.2 %collective-permute-done.2 = f32[128,128]{1,0:T(8,128)S(1)} collective-permute-done((f32[128,128]{1,0:T(8,128)S(1)}, f32[128,128]{1,0:T(8,128)S(1)}, u32[]{:S(2)}, u32[]{:S(2)}) %collective-permute-start.2) | collective-permute-done | bytes 65568 | tf_op jit(solution)/shard_map/ppermute | solution.py:527
  16.9 0.0 copy-start.4
  16.9 0.0 copy-start
  16.9 0.7 %copy-done.4 = f32[32,128]{1,0:T(8,128)S(1)} copy-done((f32[32,128]{1,0:T(8,128)S(1)}, f32[32,128]{1,0:T(8,128)}, u32[]{:S(2)}) %copy-start.4) | copy-done | bytes 16408
  17.6 0.0 copy-start.1
  17.6 0.0 collective-permute-start.3
  17.6 1.3 %collective-permute-done.3.far_ref = f32[256,128]{1,0:T(8,128)S(1)} collective-permute-done((f32[256,128]{1,0:T(8,128)S(1)}, f32[256,128]{1,0:T(8,128)S(1)}, u32[]{:S(2)}, u32[]{:S(2)}) %collective-permute-start.3) | collective-permute-done | bytes 131104 | tf_op jit(solution)/shard_map/ppermute | solution.py:527
  19.0 0.0 copy-done
  19.0 0.0 copy-done.1
  19.0 3.1 %step.1 = (f32[8,8,256]{2,1,0:T(8,128)}, f32[8,4,32]{2,1,0:T(4,128)}) custom-call(f32[256,128]{1,0:T(8,128)S(1)} %constant_dynamic-update-slice_fusion.near_ref, f32[256,128]{1,0:T(8,128)S(1)} %collective-permute-done.3.far_ref, f32[8,8,256]{2,1,0:T(8,128)S(1)} %copy-done, s32[8,256]{1,0:T(8,128)S(1)} %copy-done.1), custom_call_target="tpu_custom_call" | custom-call | tf_op jit(solution)/shard_map/step/pallas_call | solution.py:536
  (8 shorter events, 0.0 us)
Async XLA Ops:
  2.3 6.1 %copy-start.3 = (f32[32,128]{1,0:T(8,128)S(1)}, f32[32,128]{1,0:T(8,128)}, u32[]{:S(2)}) copy-start(f32[32,128]{1,0:T(8,128)} %get-tuple-element.7) | copy-start | bytes 49156
  2.3 6.1 %collective-permute-start = (f32[56,128]{1,0:T(8,128)}, f32[56,128]{1,0:T(8,128)S(1)}, u32[]{:S(2)}, u32[]{:S(2)}) collective-permute-start(f32[56,128]{1,0:T(8,128)} %get-tuple-element.6), channel_id=1, source_target_pairs={{0,8},{1,9},{2,10},{3,11},{4,12},{5,13},{6,14},{7,15},{8,0},{9,1},... | collective-permute-start | bytes 86024 | tf_op jit(solution)/shard_map/ppermute | solution.py:527
  8.4 4.1 %copy-start.2 = (f32[32,128]{1,0:T(8,128)S(1)}, f32[32,128]{1,0:T(8,128)}, u32[]{:S(2)}) copy-start(f32[32,128]{1,0:T(8,128)} %get-tuple-element.8) | copy-start | bytes 49156
  8.5 4.1 %collective-permute-start.1 = (f32[80,128]{1,0:T(8,128)S(1)}, f32[80,128]{1,0:T(8,128)S(1)}, u32[]{:S(2)}, u32[]{:S(2)}) collective-permute-start(f32[80,128]{1,0:T(8,128)S(1)} %pad_maximum_fusion.1), channel_id=1, source_target_pairs={{0,4},{1,5},{2,6},{3,7},{4,0},{5,1},{6,2},{7,3},{8,12},{9,13},{10,... | collective-permute-start | bytes 122888 | tf_op jit(solution)/shard_map/ppermute | solution.py:527
  12.6 4.3 %collective-permute-start.2 = (f32[128,128]{1,0:T(8,128)S(1)}, f32[128,128]{1,0:T(8,128)S(1)}, u32[]{:S(2)}, u32[]{:S(2)}) collective-permute-start(f32[128,128]{1,0:T(8,128)S(1)} %pad_maximum_fusion), channel_id=1, source_target_pairs={{0,2},{1,3},{2,0},{3,1},{4,6},{5,7},{6,4},{7,5},{8,10},{9,11},{10,... | collective-permute-start | bytes 196616 | tf_op jit(solution)/shard_map/ppermute | solution.py:527
  16.9 0.7 %copy-start.4 = (f32[32,128]{1,0:T(8,128)S(1)}, f32[32,128]{1,0:T(8,128)}, u32[]{:S(2)}) copy-start(f32[32,128]{1,0:T(8,128)} %get-tuple-element.9) | copy-start | bytes 49156
  16.9 2.1 %copy-start = (f32[8,8,256]{2,1,0:T(8,128)S(1)}, f32[8,8,256]{2,1,0:T(8,128)}, u32[]{:S(2)}) copy-start(f32[8,8,256]{2,1,0:T(8,128)} %salt_ref.3) | copy-start | bytes 196612
  17.6 1.4 %copy-start.1 = (s32[8,256]{1,0:T(8,128)S(1)}, s32[8,256]{1,0:T(8,128)}, u32[]{:S(2)}) copy-start(s32[8,256]{1,0:T(8,128)} %recharge_ref.3) | copy-start | bytes 24580
  17.6 1.3 %collective-permute-start.3 = (f32[256,128]{1,0:T(8,128)S(1)}, f32[256,128]{1,0:T(8,128)S(1)}, u32[]{:S(2)}, u32[]{:S(2)}) collective-permute-start(f32[256,128]{1,0:T(8,128)S(1)} %constant_dynamic-update-slice_fusion.near_ref), channel_id=1, source_target_pairs={{0,1},{1,0},{2,3},{3,2},{4,5},{5,4},{6,7},{7,6},{8,9},{9,8},{10,11... | collective-permute-start | bytes 393224 | tf_op jit(solution)/shard_map/ppermute | solution.py:527

commit v3 on v2

--- a/solution.py
+++ b/solution.py
@@ -233,14 +233,12 @@
 def iotas(shape):
     return lax.broadcasted_iota(jnp.int32, shape, 0), lax.broadcasted_iota(jnp.int32, shape, 1)
 
-BLOCK = 24
-ROUNDS = (8, 4, 2, 1)
-
-def pack_kernel(salt_ref, recharge_ref, cond_ref, codes_ref, block_ref, middle_ref, late_ref, inner_ref, flat_ref):
+MAIN, SMALL, COLUMNS = 16, 8, 32
+ROUNDS = (3, 9, 5, 1)
+
+def pack_kernel(salt_ref, recharge_ref, cond_ref, codes_ref, block_ref, inner_ref, relay_ref, flat_ref):
     device = lax.axis_index("gx")
     even = lax.rem(device, 2) == 0
-    inside = (device > 0) & (device < 15)
-    crossed = device ^ jnp.where(even, device - 1, device + 1)
     for j in range(2):
         first = salt_ref[:, j, :]
         last = salt_ref[:, 6 + j, :]
@@ -248,11 +246,10 @@
         outward = jnp.where(even, first, last)
         for half in range(2):
             place = 8 * (2 * j + half)
-            part = outward[:, 128 * half : 128 * half + 128]
             inner_ref[place : place + 8, :] = inward[:, 128 * half : 128 * half + 128]
-            block_ref[BLOCK + place : BLOCK + place + 8, :] = jnp.where(inside & (crossed == 15), part, 0.0)
-            middle_ref[place : place + 8, :] = jnp.where(inside & (crossed == 7), part, 0.0)
-            late_ref[place : place + 8, :] = jnp.where(inside & (crossed == 3), part, 0.0)
+            place = place + MAIN + SMALL
+            block_ref[place : place + 8, :] = outward[:, 128 * half : 128 * half + 128]
+    relay_ref[...] = jnp.broadcast_to(jnp.where((device == 2) | (device == 13), 1.0, 0.0), (8, 128))
     sums = table_of((256, 128), lambda r, c: r // 4 == c // 2)
     salt_y = split_dot(salt_ref[...].reshape(64, 256), sums).reshape(8, 8, 128)
     sub, lane = iotas((8, 128))
@@ -278,7 +275,8 @@
     )
     row4, lane4 = iotas((4, 128))
     code_row = jnp.sum(jnp.where(row4 == (7 - lane4 % 8) // 2, code_x, 0.0), axis=0, keepdims=True)
-    block_ref[16:24, :] = jnp.where(sub == 0, wet_row, jnp.where(sub == 1, code_row, 0.0))
+    slot = 2 * ((device // 2) % 2) + 4 * (device // 8)
+    block_ref[16:24, :] = jnp.where(sub == slot, wet_row, jnp.where(sub == slot + 1, code_row, 0.0))
 
 def harm(first, second):
     return 2.0 * first * second / (first + second)
@@ -293,37 +291,36 @@
     return cells[k - 1] if k > 0 else pltpu.roll(cells[-1], 1, 1)
 
 def step_kernel(
-    near_ref, far_ref, salt_ref, recharge_ref, tendency_ref, head_ref, fine_ref, coarse_ref, turn_ref, wide_ref
+    near_ref, far_ref, early_ref, salt_ref, recharge_ref, tendency_ref, head_ref, fine_ref, coarse_ref, turn_ref, wide_ref
 ):
     device = lax.axis_index("gx")
     sub, lane = iotas((8, 128))
     top = sub == 0
     low_g = lane % 2 == 0
     even = lax.rem(device, 2) == 0
-    blocks = []
+    parity = lax.rem(device + device // 2 + device // 4 + device // 8, 2)
+    means, conds, smalls = [], [], []
     for e in range(0, 16, 2):
         apart = device ^ e
-        place = 0
-        for bit, distance in enumerate(ROUNDS[:3]):
-            place = place + jnp.where((apart & distance) != 0, 1 << bit, 0)
-        start = pl.multiple_of(place * BLOCK, 8)
-        near = near_ref[pl.ds(start, BLOCK), :]
-        far = far_ref[pl.ds(start, BLOCK), :]
-        blocks += [jnp.where(even, near, far), jnp.where(even, far, near)]
-
-    cond_rows = jnp.concatenate([b[8:16] for b in blocks], axis=0)
-    cond_all = cond_rows.T
+        place = (apart // 2) % 2 + 2 * (apart // 8) + 4 * ((apart // 4) % 2)
+        mine = parity == bin(e).count("1") % 2
+
+        def block_pair(start, rows):
+            near, far = near_ref[pl.ds(start, rows), :], far_ref[pl.ds(start, rows), :]
+            return [jnp.where(mine, near, far), jnp.where(mine, far, near)]
+
+        start = pl.multiple_of(MAIN * place, 8)
+        means += block_pair(start, 8)
+        conds += block_pair(start + 8, 8)
+        smalls += block_pair(pl.multiple_of(8 * MAIN + SMALL * ((apart // 4) % 2), 8), 8)
+
+    slots = [2 * ((e // 2) % 2) + 4 * (e // 8) for e in range(16)]
+    wets = [smalls[e][slots[e] : slots[e] + 1] for e in range(16)]
+    codes = [smalls[e][slots[e] + 1 : slots[e] + 2] for e in range(16)]
+    cond_all = jnp.concatenate(conds, axis=0).T
     cond = [cond_all[8 * k : 8 * k + 8] for k in range(16)]
-    code_rows = jnp.concatenate(
-        [
-            pltpu.roll(jnp.broadcast_to(b[17:18], (8, 128)), 121, 1, stride=1, stride_axis=0)
-            for b in blocks
-        ],
-        axis=0,
-    )
-    code_all = code_rows.T
-    means = [b[0:8] for b in blocks]
-    wets = [b[16:17] for b in blocks]
+    codes = [pltpu.roll(jnp.broadcast_to(c, (8, 128)), 121, 1, stride=1, stride_axis=0) for c in codes]
+    code_all = jnp.concatenate(codes, axis=0).T
 
     def by_column(per_device, mask):
         out = []
@@ -470,10 +467,20 @@
     speed_z = [spread[48 + 8 * j : 56 + 8 * j] for j in range(2)]
 
     layer, column = iotas((8, 256))
-    halo = [
-        jnp.concatenate([far_ref[192 + 16 * i : 200 + 16 * i, :], far_ref[200 + 16 * i : 208 + 16 * i, :]], axis=1)
-        for i in range(4)
-    ]
+    crossed = device ^ jnp.where(even, device - 1, device + 1)
+    halo = []
+    for i in range(4):
+        parts = []
+        for half in range(2):
+            place = 8 * (2 * i + half)
+            here = 8 * (MAIN + 2) + place
+            part = far_ref[here : here + 8, :]
+            if i < 2:
+                straight = early_ref[MAIN + SMALL + place : MAIN + SMALL + place + 8, :]
+                part = jnp.where(crossed == 7, part, jnp.where(crossed == 15, near_ref[here : here + 8, :], 0.0))
+                part = jnp.where(crossed == 3, straight, part)
+            parts.append(part)
+        halo.append(jnp.concatenate(parts, axis=1))
     cells = (
         [jnp.where(even, halo[j], halo[2 + j]) for j in range(2)]
         + [salt_ref[:, x, :] for x in range(8)]
@@ -513,12 +520,15 @@
 
 def local_small(salt, recharge, conductivity, codes):
     vmem = pl.BlockSpec(memory_space=pltpu.VMEM)
-    columns = jax.ShapeDtypeStruct((32, 128), jnp.float32)
-    block, middle, late, inner = pl.pallas_call(
+    block, inner, relay = pl.pallas_call(
         pack_kernel,
-        out_shape=(jax.ShapeDtypeStruct((BLOCK + 32, 128), jnp.float32), columns, columns, columns),
+        out_shape=(
+            pltpu.VMEM((MAIN + SMALL + COLUMNS, 128), jnp.float32),
+            pltpu.VMEM((COLUMNS, 128), jnp.float32),
+            pltpu.VMEM((8, 128), jnp.float32),
+        ),
         in_specs=[vmem] * 4,
-        out_specs=(vmem,) * 4,
+        out_specs=(vmem,) * 3,
         scratch_shapes=[pltpu.VMEM((32, 32), jnp.float32)],
         name="pack",
     )(salt, recharge, conductivity, codes)
@@ -526,12 +536,25 @@
     def swapped(array, distance):
         return lax.ppermute(array, "gx", [(i, i ^ distance) for i in range(lax.axis_size("gx"))])
 
-    other = swapped(block, ROUNDS[0])
-    block = jnp.concatenate([block[:BLOCK], other[:BLOCK], other[BLOCK:] + middle])
+    def small(array, count):
+        return array[count * MAIN : count * MAIN + SMALL]
+
+    def columns(array, count):
+        return array[count * MAIN + SMALL :]
+
+    first = swapped(block, ROUNDS[0])
+    block = jnp.concatenate(
+        [block[:MAIN], first[:MAIN], small(block, 1) + small(first, 1), columns(first, 1)]
+    )
     other = swapped(block, ROUNDS[1])
-    block = jnp.concatenate([block[: 2 * BLOCK], other[: 2 * BLOCK], other[2 * BLOCK :] + late])
+    handed = jnp.where(jnp.tile(relay, (COLUMNS // 8, 1)) > 0, columns(other, 2), columns(first, 1))
+    block = jnp.concatenate(
+        [block[: 2 * MAIN], other[: 2 * MAIN], small(block, 2) + small(other, 2), handed]
+    )
     other = swapped(block, ROUNDS[2])
-    block = jnp.concatenate([block[: 4 * BLOCK], other, inner])
+    block = jnp.concatenate(
+        [block[: 4 * MAIN], other[: 4 * MAIN], small(block, 4), small(other, 4), columns(other, 4), inner]
+    )
     other = swapped(block, ROUNDS[3])
     return pl.pallas_call(
         step_kernel,
@@ -539,7 +562,7 @@
             jax.ShapeDtypeStruct(salt.shape, jnp.float32),
             jax.ShapeDtypeStruct(conductivity.shape, jnp.float32),
         ),
-        in_specs=[vmem] * 4,
+        in_specs=[vmem] * 5,
         out_specs=(vmem,) * 2,
         scratch_shapes=[
             pltpu.VMEM((13, 16, 8, 128), jnp.float32),
@@ -549,7 +572,7 @@
         ],
         compiler_params=pltpu.CompilerParams(vmem_limit_bytes=16 * 1024 * 1024),
         name="step",
-    )(block, other, salt, recharge)
+    )(block, other, first, salt, recharge)
 
 def local(salt, recharge, conductivity, codes):
     small = (

time: 22.4 us -> 19.8 us (0.88)
  the two profiles are of different devices: /device:TPU:0 before, /device:TPU:29 now
where the time goes in v3:
time: 19.8 us; the launch traced here: 19.6 us
  waiting for transfers between devices  12.8 us (65%)
  Pallas kernels  4.22 us (21%)
  starting transfers between devices  1.78 us (9%)
  between operations  0.69 us (3%)
    ppermute x4, waiting for transfers between devices, swapped(): lax.ppermute(array, 'gx', [(i, i ^ distance) for i in range(lax.axis_size...  12.8 us
    pallas_call x1, Pallas kernels, local_small(): pl.pallas_call(step_kernel, out_shape=(jax.ShapeDtypeStruct(salt.shape, j...  3.15 us
    ppermute x4, starting transfers between devices, swapped(): lax.ppermute(array, 'gx', [(i, i ^ distance) for i in range(lax.axis_size...  1.78 us
    pallas_call x1, Pallas kernels, local_small(): pl.pallas_call(pack_kernel, out_shape=(pltpu.VMEM((MAIN + SMALL + COLUMNS...  1.07 us
  transfers between devices with their start and end apart: 4, of which 4 were waited for; matrix products, arithmetic and copies ran while one was open for 0% of the time, Pallas kernels for 0%

profile of v3, /device:TPU:29, one launch (start us, length us, event | category | flops | bytes accessed | tf_op | source)
XLA Modules:
  0.0 19.6 jit_solution(3881806716792344403)
XLA Ops:
  0.6 1.1 %pack.1 = (f32[56,128]{1,0:T(8,128)S(1)}, f32[32,128]{1,0:T(8,128)S(1)}, f32[8,128]{1,0:T(8,128)S(1)}) custom-call(f32[8,8,256]{2,1,0:T(8,128)} %salt_ref.3, s32[8,256]{1,0:T(8,128)} %recharge_ref.3, f32[8,4,32]{2,1,0:T(4,128)} %cond_ref.1, s32[4,32]{1,0:T(4,128)} %codes_ref.1), custom_call_target="tpu_custom_call" | custom-call | tf_op jit(solution)/shard_map/pack/pallas_call | solution.py:523
  1.7 0.9 %collective-permute-start = (f32[56,128]{1,0:T(8,128)S(1)}, f32[56,128]{1,0:T(8,128)S(1)}, u32[]{:S(2)}, u32[]{:S(2)}) collective-permute-start(f32[56,128]{1,0:T(8,128)S(1)} %get-tuple-element.5), channel_id=1, source_target_pairs={{0,3},{1,2},{2,1},{3,0},{4,7},{5,6},{6,5},{7,4},{8,11},{9,10},{10,... | collective-permute-start | bytes 86024 | tf_op jit(solution)/shard_map/ppermute | solution.py:537
  2.6 3.1 %collective-permute-done.early_ref = f32[56,128]{1,0:T(8,128)S(1)} collective-permute-done((f32[56,128]{1,0:T(8,128)S(1)}, f32[56,128]{1,0:T(8,128)S(1)}, u32[]{:S(2)}, u32[]{:S(2)}) %collective-permute-start) | collective-permute-done | bytes 28704 | tf_op jit(solution)/shard_map/ppermute | solution.py:537
  5.7 0.4 %collective-permute-start.1 = (f32[72,128]{1,0:T(8,128)S(1)}, f32[72,128]{1,0:T(8,128)S(1)}, u32[]{:S(2)}, u32[]{:S(2)}) collective-permute-start(f32[72,128]{1,0:T(8,128)S(1)} %pad_maximum_fusion), channel_id=1, source_target_pairs={{0,9},{1,8},{2,11},{3,10},{4,13},{5,12},{6,15},{7,14},{8,1},{9,0},... | collective-permute-start | bytes 110600 | tf_op jit(solution)/shard_map/ppermute | solution.py:537
  6.1 5.0 %collective-permute-done.1 = f32[72,128]{1,0:T(8,128)S(1)} collective-permute-done((f32[72,128]{1,0:T(8,128)S(1)}, f32[72,128]{1,0:T(8,128)S(1)}, u32[]{:S(2)}, u32[]{:S(2)}) %collective-permute-start.1) | collective-permute-done | bytes 36896 | tf_op jit(solution)/shard_map/ppermute | solution.py:537
  11.1 0.1 collective-permute-start.2
  11.1 3.8 %collective-permute-done.2 = f32[104,128]{1,0:T(8,128)S(1)} collective-permute-done((f32[104,128]{1,0:T(8,128)S(1)}, f32[104,128]{1,0:T(8,128)S(1)}, u32[]{:S(2)}, u32[]{:S(2)}) %collective-permute-start.2) | collective-permute-done | bytes 53280 | tf_op jit(solution)/shard_map/ppermute | solution.py:537
  15.0 0.0 copy-start
  15.0 0.0 copy-start.1
  15.0 0.5 %collective-permute-start.3 = (f32[208,128]{1,0:T(8,128)S(1)}, f32[208,128]{1,0:T(8,128)S(1)}, u32[]{:S(2)}, u32[]{:S(2)}) collective-permute-start(f32[208,128]{1,0:T(8,128)S(1)} %constant_dynamic-update-slice_fusion.5.near_ref), channel_id=1, source_target_pairs={{0,1},{1,0},{2,3},{3,2},{4,5},{5,4},{6,7},{7,6},{8,9},{9,8},{10,11... | collective-permute-start | bytes 319496 | tf_op jit(solution)/shard_map/ppermute | solution.py:537
  15.5 1.0 %collective-permute-done.3.far_ref = f32[208,128]{1,0:T(8,128)S(1)} collective-permute-done((f32[208,128]{1,0:T(8,128)S(1)}, f32[208,128]{1,0:T(8,128)S(1)}, u32[]{:S(2)}, u32[]{:S(2)}) %collective-permute-start.3) | collective-permute-done | bytes 106528 | tf_op jit(solution)/shard_map/ppermute | solution.py:537
  16.4 0.0 copy-done
  16.4 0.0 copy-done.1
  16.4 3.2 %step.1 = (f32[8,8,256]{2,1,0:T(8,128)}, f32[8,4,32]{2,1,0:T(4,128)}) custom-call(f32[208,128]{1,0:T(8,128)S(1)} %constant_dynamic-update-slice_fusion.5.near_ref, f32[208,128]{1,0:T(8,128)S(1)} %collective-permute-done.3.far_ref, f32[56,128]{1,0:T(8,128)S(1)} %collective-permute-done.early_ref, f32[8,8,256]{2,1,0:T(8,128)S(1)} %copy-done, ...), custom_call_target="tpu_custom_call" | custom-call | tf_op jit(solution)/shard_map/step/pallas_call | solution.py:559
  (13 shorter events, 0.0 us)
Async XLA Ops:
  1.7 3.9 %collective-permute-start = (f32[56,128]{1,0:T(8,128)S(1)}, f32[56,128]{1,0:T(8,128)S(1)}, u32[]{:S(2)}, u32[]{:S(2)}) collective-permute-start(f32[56,128]{1,0:T(8,128)S(1)} %get-tuple-element.5), channel_id=1, source_target_pairs={{0,3},{1,2},{2,1},{3,0},{4,7},{5,6},{6,5},{7,4},{8,11},{9,10},{10,... | collective-permute-start | bytes 86024 | tf_op jit(solution)/shard_map/ppermute | solution.py:537
  5.7 5.4 %collective-permute-start.1 = (f32[72,128]{1,0:T(8,128)S(1)}, f32[72,128]{1,0:T(8,128)S(1)}, u32[]{:S(2)}, u32[]{:S(2)}) collective-permute-start(f32[72,128]{1,0:T(8,128)S(1)} %pad_maximum_fusion), channel_id=1, source_target_pairs={{0,9},{1,8},{2,11},{3,10},{4,13},{5,12},{6,15},{7,14},{8,1},{9,0},... | collective-permute-start | bytes 110600 | tf_op jit(solution)/shard_map/ppermute | solution.py:537
  11.1 3.9 %collective-permute-start.2 = (f32[104,128]{1,0:T(8,128)S(1)}, f32[104,128]{1,0:T(8,128)S(1)}, u32[]{:S(2)}, u32[]{:S(2)}) collective-permute-start(f32[104,128]{1,0:T(8,128)S(1)} %get-tuple-element.8), channel_id=1, source_target_pairs={{0,5},{1,4},{2,7},{3,6},{4,1},{5,0},{6,3},{7,2},{8,13},{9,12},{10,... | collective-permute-start | bytes 159752 | tf_op jit(solution)/shard_map/ppermute | solution.py:537
  15.0 1.5 %copy-start = (f32[8,8,256]{2,1,0:T(8,128)S(1)}, f32[8,8,256]{2,1,0:T(8,128)}, u32[]{:S(2)}) copy-start(f32[8,8,256]{2,1,0:T(8,128)} %salt_ref.3) | copy-start | bytes 196612
  15.0 1.4 %copy-start.1 = (s32[8,256]{1,0:T(8,128)S(1)}, s32[8,256]{1,0:T(8,128)}, u32[]{:S(2)}) copy-start(s32[8,256]{1,0:T(8,128)} %recharge_ref.3) | copy-start | bytes 24580
  15.0 1.4 %collective-permute-start.3 = (f32[208,128]{1,0:T(8,128)S(1)}, f32[208,128]{1,0:T(8,128)S(1)}, u32[]{:S(2)}, u32[]{:S(2)}) collective-permute-start(f32[208,128]{1,0:T(8,128)S(1)} %constant_dynamic-update-slice_fusion.5.near_ref), channel_id=1, source_target_pairs={{0,1},{1,0},{2,3},{3,2},{4,5},{5,4},{6,7},{7,6},{8,9},{9,8},{10,11... | collective-permute-start | bytes 319496 | tf_op jit(solution)/shard_map/ppermute | solution.py:537

commit v4 on v3

--- a/solution.py
+++ b/solution.py
@@ -234,9 +234,12 @@
     return lax.broadcasted_iota(jnp.int32, shape, 0), lax.broadcasted_iota(jnp.int32, shape, 1)
 
 MAIN, SMALL, COLUMNS = 16, 8, 32
-ROUNDS = (3, 9, 5, 1)
-
-def pack_kernel(salt_ref, recharge_ref, cond_ref, codes_ref, block_ref, inner_ref, relay_ref, flat_ref):
+ROUNDS = ((9, 3, 5, 1), (3, 9, 5, 1))
+
+def odd_ones(device):
+    return lax.rem(device + device // 2 + device // 4 + device // 8, 2) == 1
+
+def pack_kernel(salt_ref, recharge_ref, cond_ref, codes_ref, block_ref, inner_ref, relay_ref, flat_ref, turn_ref):
     device = lax.axis_index("gx")
     even = lax.rem(device, 2) == 0
     for j in range(2):
@@ -249,32 +252,31 @@
             inner_ref[place : place + 8, :] = inward[:, 128 * half : 128 * half + 128]
             place = place + MAIN + SMALL
             block_ref[place : place + 8, :] = outward[:, 128 * half : 128 * half + 128]
-    relay_ref[...] = jnp.broadcast_to(jnp.where((device == 2) | (device == 13), 1.0, 0.0), (8, 128))
-    sums = table_of((256, 128), lambda r, c: r // 4 == c // 2)
+    relay = jnp.where(odd_ones(device), jnp.where((device == 2) | (device == 13), 1.0, 0.0), 2.0)
+    relay_ref[...] = jnp.broadcast_to(relay, (8, 128))
+    turned = device // 2
+    sums = table_of((256, 128), lambda r, c: r // 4 == 4 * (c // 8) + ((c - turned) % 8) // 2)
     salt_y = split_dot(salt_ref[...].reshape(64, 256), sums).reshape(8, 8, 128)
     sub, lane = iotas((8, 128))
-    mine = sub // 4 == lane % 2
+    mine = sub // 4 == (lane - turned) % 2
     block_ref[0:8, :] = jnp.sum(jnp.where(mine[None], salt_y, 0.0), axis=1) * 0.0625
     wet_y = jnp.dot(
         recharge_ref[...].astype(jnp.float32).astype(jnp.bfloat16), sums, preferred_element_type=jnp.float32
     )
     wet_row = jnp.sum(jnp.where(mine, wet_y, 0.0), axis=0, keepdims=True) * 0.0625
     for layer in range(8):
-        flat_ref[4 * layer : 4 * layer + 4, :] = cond_ref[layer]
-    spread = table_of((32, 256), lambda r, c: r == (c // 128) * 16 + (c % 128) // 8)
-    cond_x = split_dot(flat_ref[...], spread)
-    row32, lane32 = iotas((32, 256))
-    cond_x = jnp.where(row32 // 4 == lane32 % 8, cond_x, 0.0)
-    summed = cond_x[0:8] + cond_x[8:16] + cond_x[16:24] + cond_x[24:32]
-    summed = summed + pltpu.roll(summed, 4, 0)
-    block_ref[pl.ds(8, 4, stride=2), :] = summed[0:4, 0:128]
-    block_ref[pl.ds(9, 4, stride=2), :] = summed[0:4, 128:256]
-    spread_codes = table_of((32, 128), lambda r, c: r == 16 * ((7 - c % 8) % 2) + c // 8)
+        flat_ref[4 * layer : 4 * layer + 4, 0:32] = cond_ref[layer]
+    spread = table_of((32, 128), lambda r, c: r == 4 * (c % 8) + (c // 8 - device) % 4)
+    turn_ref[...] = split_dot(flat_ref[:, 0:32], spread)
+    packed = jnp.zeros((8, 128), jnp.float32)
+    for j in range(4):
+        packed = jnp.where((lane // 8 - device) % 16 // 4 == j, turn_ref[pl.ds(j, 8, stride=4), :], packed)
+    block_ref[8:16, :] = packed
     code_x = jnp.dot(
-        codes_ref[...].astype(jnp.float32).astype(jnp.bfloat16), spread_codes, preferred_element_type=jnp.float32
+        codes_ref[...].astype(jnp.float32).astype(jnp.bfloat16), spread, preferred_element_type=jnp.float32
     )
     row4, lane4 = iotas((4, 128))
-    code_row = jnp.sum(jnp.where(row4 == (7 - lane4 % 8) // 2, code_x, 0.0), axis=0, keepdims=True)
+    code_row = jnp.sum(jnp.where(row4 == (lane4 // 8 - device) % 16 // 4, code_x, 0.0), axis=0, keepdims=True)
     slot = 2 * ((device // 2) % 2) + 4 * (device // 8)
     block_ref[16:24, :] = jnp.where(sub == slot, wet_row, jnp.where(sub == slot + 1, code_row, 0.0))
 
@@ -284,171 +286,196 @@
 def slope_of(back, ahead):
     return jnp.maximum(jnp.minimum(back, ahead), 0.0) + jnp.minimum(jnp.maximum(back, ahead), 0.0)
 
-def east_of(cells, k):
-    return cells[k + 1] if k + 1 < len(cells) else pltpu.roll(cells[0], 127, 1)
-
-def west_of(cells, k):
-    return cells[k - 1] if k > 0 else pltpu.roll(cells[-1], 1, 1)
+def east_of(cells, k, side):
+    return cells[k + 1] if k % side < side - 1 else pltpu.roll(cells[k + 1 - side], 127, 1)
+
+def west_of(cells, k, side):
+    return cells[k - 1] if k % side > 0 else pltpu.roll(cells[k - 1 + side], 1, 1)
+
+def north_of(cells, k, side):
+    return cells[k + side] if k < side * (side - 1) else pltpu.roll(cells[k % side], 120, 1)
+
+def south_of(cells, k, side):
+    return cells[k - side] if k >= side else pltpu.roll(cells[k + side * (side - 1)], 8, 1)
+
+def upper_of(cell):
+    return pltpu.roll(cell, 1, 0)
+
+def lower_of(cell):
+    return pltpu.roll(cell, 7, 0)
 
 def step_kernel(
-    near_ref, far_ref, early_ref, salt_ref, recharge_ref, tendency_ref, head_ref, fine_ref, coarse_ref, turn_ref, wide_ref
+    near_ref, far_ref, first_ref, second_ref, salt_ref, recharge_ref, tendency_ref, head_ref, fine_ref, coarse_ref, wide_ref
 ):
     device = lax.axis_index("gx")
     sub, lane = iotas((8, 128))
     top = sub == 0
-    low_g = lane % 2 == 0
     even = lax.rem(device, 2) == 0
-    parity = lax.rem(device + device // 2 + device // 4 + device // 8, 2)
+    odd = odd_ones(device)
     means, conds, smalls = [], [], []
     for e in range(0, 16, 2):
         apart = device ^ e
-        place = (apart // 2) % 2 + 2 * (apart // 8) + 4 * ((apart // 4) % 2)
-        mine = parity == bin(e).count("1") % 2
-
-        def block_pair(start, rows):
-            near, far = near_ref[pl.ds(start, rows), :], far_ref[pl.ds(start, rows), :]
+        ones, nines, fives = (apart // 2) % 2, apart // 8, (apart // 4) % 2
+        places = [nines + 2 * ones + 4 * fives, ones + 2 * nines + 4 * fives]
+        here = jnp.where(odd, places[1], places[0])
+        there = jnp.where(odd, places[0], places[1])
+        mine = odd == (bin(e).count("1") % 2 == 1)
+
+        def block_pair(here, there):
+            near = near_ref[pl.ds(pl.multiple_of(here, 8), 8), :]
+            far = far_ref[pl.ds(pl.multiple_of(there, 8), 8), :]
             return [jnp.where(mine, near, far), jnp.where(mine, far, near)]
 
-        start = pl.multiple_of(MAIN * place, 8)
-        means += block_pair(start, 8)
-        conds += block_pair(start + 8, 8)
-        smalls += block_pair(pl.multiple_of(8 * MAIN + SMALL * ((apart // 4) % 2), 8), 8)
+        means += block_pair(MAIN * here, MAIN * there)
+        conds += block_pair(MAIN * here + 8, MAIN * there + 8)
+        smalls += block_pair(8 * MAIN + SMALL * fives, 8 * MAIN + SMALL * fives)
 
     slots = [2 * ((e // 2) % 2) + 4 * (e // 8) for e in range(16)]
     wets = [smalls[e][slots[e] : slots[e] + 1] for e in range(16)]
     codes = [smalls[e][slots[e] + 1 : slots[e] + 2] for e in range(16)]
-    cond_all = jnp.concatenate(conds, axis=0).T
-    cond = [cond_all[8 * k : 8 * k + 8] for k in range(16)]
-    codes = [pltpu.roll(jnp.broadcast_to(c, (8, 128)), 121, 1, stride=1, stride_axis=0) for c in codes]
-    code_all = jnp.concatenate(codes, axis=0).T
-
-    def by_column(per_device, mask):
+
+    def diagonals(fields, index):
+        count = len(fields)
+        bit = 1
+        while bit < count:
+            high = (index & bit) != 0
+            fields = [jnp.where(high, fields[(m + bit) % count], fields[m]) for m in range(count)]
+            bit *= 2
+        return fields
+
+    def by_block(fields):
+        group = lane[0 : fields[0].shape[0]] // 8
+        picked = diagonals(fields, group)
+        return [pltpu.roll(picked[-k % 16], (128 - 8 * k) % 128, 1) for k in range(16)]
+
+    def by_lane(fields):
+        within = lane % 8
         out = []
-        for k in range(16):
-            a, b = per_device[k // 2], per_device[8 + k // 2]
-            out.append(
-                jnp.where(mask, a, pltpu.roll(b, 1, 1)) if k % 2 == 0 else jnp.where(mask, pltpu.roll(a, 127, 1), b)
-            )
+        picked = diagonals(fields, within)
+        for s in range(8):
+            here = picked[-s % 8]
+            if s > 0:
+                here = jnp.where(within < 8 - s, pltpu.roll(here, 128 - s, 1), pltpu.roll(here, 8 - s, 1))
+            out.append(here)
         return out
 
-    salt = by_column(means, low_g)
-    wet_frac = by_column(wets, low_g[0:1])
-
-    def coefficients(cells, penalty, hop, vertical, weight_ref):
-        count = len(cells)
-        face_e, face_n, face_d = [], [], []
-        for k in range(count):
-            e = harm(cells[k], east_of(cells, k))
-            if k == count - 1:
-                e = jnp.where(low_g, e, 0.0)
-            n = jnp.where(lane < 128 - hop, harm(cells[k], pltpu.roll(cells[k], 128 - hop, 1)), 0.0)
-            d = jnp.where(sub < 7, vertical * harm(cells[k], pltpu.roll(cells[k], 7, 0)), 0.0)
+    cond = by_block(conds)
+    codes = by_block(codes)
+    salt = [None] * 16
+    wet_frac = [None] * 16
+    wet_pairs = by_lane([jnp.where(top, wets[2 * b], wets[2 * b + 1]) for b in range(8)])
+    for half in range(2):
+        columns = by_lane(means[half::2])
+        for s in range(8):
+            k = 4 * (s // 2) + 2 * half + s % 2
+            salt[k] = columns[s]
+            wet_frac[k] = wet_pairs[s] if half == 0 else lower_of(wet_pairs[s])
+
+    def coefficients(cells, penalty, side, vertical, weight_ref):
+        face_w, face_e, face_s, face_n, face_d = [], [], [], [], []
+        for k in range(side * side):
+            e = harm(cells[k], east_of(cells, k, side))
+            if k % side == side - 1:
+                e = jnp.where(lane % 8 < 7, e, 0.0)
+            n = harm(cells[k], north_of(cells, k, side))
+            if k >= side * (side - 1):
+                n = jnp.where(lane < 120, n, 0.0)
+            w = face_e[k - 1] if k % side > 0 else None
+            if w is None:
+                w = jnp.where(lane % 8 > 0, harm(west_of(cells, k, side), cells[k]), 0.0)
+            s = face_n[k - side] if k >= side else None
+            if s is None:
+                s = jnp.where(lane >= 8, harm(south_of(cells, k, side), cells[k]), 0.0)
+            face_w.append(w)
             face_e.append(e)
+            face_s.append(s)
             face_n.append(n)
-            face_d.append(d)
-        diags = []
-        for k in range(count):
-            six = (
-                west_of(face_e, k),
-                face_e[k],
-                pltpu.roll(face_n[k], hop, 1),
-                face_n[k],
-                pltpu.roll(face_d[k], 1, 0),
-                face_d[k],
-            )
+            face_d.append(jnp.where(sub < 7, vertical * harm(cells[k], lower_of(cells[k])), 0.0))
+        weights = []
+        for k in range(side * side):
+            six = (face_w[k], face_e[k], face_s[k], face_n[k], upper_of(face_d[k]), face_d[k])
             diag = six[0] + six[1] + six[2] + six[3] + six[4] + six[5] + penalty[k]
             weight = relax_weight / diag
             for number, face in enumerate(six):
                 weight_ref[number, k] = weight * face
             weight_ref[6, k] = diag * (1.0 / relax_weight)
             weight_ref[7, k] = weight
-            diags.append(weight)
-        return face_e, face_n, face_d, diags
-
-    def relaxed(cells, hop, weight_ref, source_ref):
+            weights.append(weight)
+        return (face_w, face_e, face_s, face_n, face_d), weights
+
+    def relaxed(cells, side, weight_ref):
         out = []
-        for k in range(len(cells)):
+        for k in range(side * side):
             here = cells[k]
             pairs = (
-                west_of(cells, k),
-                east_of(cells, k),
-                pltpu.roll(here, hop, 1),
-                pltpu.roll(here, 128 - hop, 1),
-                pltpu.roll(here, 1, 0),
-                pltpu.roll(here, 7, 0),
+                west_of(cells, k, side),
+                east_of(cells, k, side),
+                south_of(cells, k, side),
+                north_of(cells, k, side),
+                upper_of(here),
+                lower_of(here),
             )
             terms = [weight_ref[number, k] * pair for number, pair in enumerate(pairs)]
-            base = (1.0 - relax_weight) * here + source_ref[8, k]
+            base = (1.0 - relax_weight) * here + weight_ref[8, k]
             out.append(((terms[0] + terms[1]) + (terms[2] + terms[3])) + ((terms[4] + terms[5]) + base))
         return out
 
-    odd_y = (lane // 2) % 2 == 1
-
     def pair_sums(cells):
-        out = []
-        for k in range(0, len(cells), 2):
-            both = cells[k] + cells[k + 1]
-            out.append(both + jnp.where(odd_y, pltpu.roll(both, 2, 1), pltpu.roll(both, 126, 1)))
-        return out
+        return [(cells[k] + cells[k + 1]) + (cells[k + 4] + cells[k + 5]) for k in (0, 2, 8, 10)]
 
     penalty, river = [], []
     for k in range(16):
-        code = code_all[8 * k : 8 * k + 8]
+        code = codes[k]
         river.append(jnp.where(top & (code == 2.0), river_penalty, 0.0))
         penalty.append(jnp.where(top & (code == 1.0), sea_penalty, 0.0) + river[k])
-    face_e, face_n, face_d, weights = coefficients(cond, penalty, 2, vertical_ratio, fine_ref)
-    drop = []
+    faces, weights = coefficients(cond, penalty, 4, vertical_ratio, fine_ref)
     for k in range(16):
-        below = jnp.where(sub < 7, 0.5 * (salt[k] + pltpu.roll(salt[k], 7, 0)), 0.0)
-        drop.append(below)
-        pull = face_d[k] * below
+        below = jnp.where(sub < 7, 0.5 * (salt[k] + lower_of(salt[k])), 0.0)
+        pull = faces[4][k] * below
         source = jnp.where(top, recharge_rate * wet_frac[k] + river_head * river[k], 0.0)
-        fine_ref[8, k] = weights[k] * (pltpu.roll(pull, 1, 0) - pull + source)
-        fine_ref[9, k] = face_e[k]
-        fine_ref[10, k] = face_n[k]
-        fine_ref[11, k] = face_d[k]
-        fine_ref[12, k] = below
-    coefficients([0.25 * c for c in pair_sums(cond)], pair_sums(penalty), 4, 4.0 * vertical_ratio, coarse_ref)
+        fine_ref[8, k] = weights[k] * (upper_of(pull) - pull + source)
+        fine_ref[9, k] = below
+        for number, face in enumerate(faces):
+            fine_ref[10 + number, k] = face[k]
+    coefficients([0.25 * c for c in pair_sums(cond)], pair_sums(penalty), 2, 4.0 * vertical_ratio, coarse_ref)
 
     head = None
     for cycle_no in range(CYCLES):
         for sweep in range(SMOOTH):
-            head = [fine_ref[8, k] for k in range(16)] if head is None else relaxed(head, 2, fine_ref, fine_ref)
-        ahead = relaxed(head, 2, fine_ref, fine_ref)
+            head = [fine_ref[8, k] for k in range(16)] if head is None else relaxed(head, 4, fine_ref)
+        ahead = relaxed(head, 4, fine_ref)
         resid = pair_sums([(ahead[k] - head[k]) * fine_ref[6, k] for k in range(16)])
         correction = []
-        for k in range(8):
+        for k in range(4):
             correction.append(coarse_ref[7, k] * resid[k])
             coarse_ref[8, k] = correction[k]
         for sweep in range(COARSE_SWEEPS - 1):
-            correction = relaxed(correction, 4, coarse_ref, coarse_ref)
-        head = [head[k] + correction[k // 2] for k in range(16)]
+            correction = relaxed(correction, 2, coarse_ref)
+        head = [head[k] + correction[2 * (k // 8) + (k % 4) // 2] for k in range(16)]
         for sweep in range(SMOOTH):
-            head = relaxed(head, 2, fine_ref, fine_ref)
-
-    turn_ref[...] = jnp.concatenate(head, axis=0).T
-    rows = turn_ref[pl.ds(pl.multiple_of(8 * device, 8), 8), :]
-    copies = jnp.concatenate([rows] * 8, axis=0)
-    row64, lane64 = iotas((64, 128))
-    picked = split_dot(
-        jnp.where(row64 // 8 == lane64 % 8, copies, 0.0), table_of((128, 128), lambda r, c: r // 8 == c % 16)
-    )
-    turn_ref[0:64, :] = picked
-    lane32 = lax.broadcasted_iota(jnp.int32, (32, 128), 1)
-    own = jnp.where(lane32 < 16, turn_ref[pl.ds(0, 32, stride=2), :], turn_ref[pl.ds(1, 32, stride=2), :])[:, 0:32]
-    for layer in range(8):
-        head_ref[layer] = own[4 * layer : 4 * layer + 4]
-
-    flow_e, flow_n, flow_d = [], [], []
-    for k in range(16):
-        flow_e.append(fine_ref[9, k] * (head[k] - east_of(head, k)))
-        flow_n.append(fine_ref[10, k] * (head[k] - pltpu.roll(head[k], 126, 1)))
-        flow_d.append(fine_ref[11, k] * (head[k] - pltpu.roll(head[k], 7, 0) + fine_ref[12, k]))
+            head = relaxed(head, 4, fine_ref)
+
+    rows = []
+    for j in range(4):
+        row = jnp.zeros((8, 128), jnp.float32)
+        for i in range(4):
+            row = jnp.where(lane // 8 == i, pltpu.roll(head[4 * j + i], lax.rem(8 * i - 8 * device + 128, 128), 1), row)
+        rows.append(row)
+    own = split_dot(
+        jnp.concatenate(rows, axis=0), table_of((128, 128), lambda r, c: (r < 32) & (c == 4 * (r % 8) + r // 8))
+    )
+    for j in range(4):
+        head_ref[:, j, :] = own[8 * j : 8 * j + 8, 0:32]
+
     largest = None
     for k in range(16):
-        vel_x = 0.5 * (west_of(flow_e, k) + flow_e[k])
-        vel_y = 0.5 * (pltpu.roll(flow_n[k], 2, 1) + flow_n[k])
-        vel_z = 0.5 * (pltpu.roll(flow_d[k], 1, 0) + flow_d[k])
+        here = head[k]
+        west, east = west_of(head, k, 4) - here, here - east_of(head, k, 4)
+        south, north = south_of(head, k, 4) - here, here - north_of(head, k, 4)
+        vel_x = 0.5 * (fine_ref[10, k] * west + fine_ref[11, k] * east)
+        vel_y = 0.5 * (fine_ref[12, k] * south + fine_ref[13, k] * north)
+        flow_d = fine_ref[14, k] * (here - lower_of(here) + fine_ref[9, k])
+        vel_z = 0.5 * (upper_of(flow_d) + flow_d)
         wide_ref[0, k] = vel_x
         wide_ref[1, k] = vel_y
         wide_ref[2, k] = vel_z
@@ -460,11 +487,25 @@
     for field, wanted in ((0, (0, 1, 2, 3)), (1, (1, 2)), (2, (1, 2))):
         for j in wanted:
             x = jnp.clip(2 * device - 1 + j, 0, 31)
-            columns.append(jnp.where(lane % 2 == x // 16, wide_ref[field, lax.rem(x, 16)], 0.0))
-    spread = split_dot(jnp.concatenate(columns, axis=0), table_of((128, 256), lambda r, c: r // 2 == c // 4))
+            column = jnp.zeros((8, 128), jnp.float32)
+            for i in range(4):
+                turned = pltpu.roll(wide_ref[field, 4 * i + lax.rem(x, 4)], lax.rem(128 + i - x // 4, 128), 1)
+                column = jnp.where(lane % 8 == i, turned, column)
+            columns.append(column)
+
+    def along(r, c):
+        return (r % 8 < 4) & (c // 4 == 4 * (r // 8) + r % 8)
+
+    spread = split_dot(jnp.concatenate(columns[:4] + columns[6:], axis=0), table_of((128, 256), along))
     speed_x = [spread[8 * j : 8 * j + 8] for j in range(4)]
-    speed_y = [spread[32 + 8 * j : 40 + 8 * j] for j in range(2)]
-    speed_z = [spread[48 + 8 * j : 56 + 8 * j] for j in range(2)]
+    speed_z = [spread[32 + 8 * j : 40 + 8 * j] for j in range(2)]
+    row, col = iotas((128, 512))
+    col = jnp.where(col < 256, col, col - 257)
+    inner = (col >= 0) & (col < 255)
+    sides = jnp.where(inner & along(row, col), 1.0, 0.0) + jnp.where(inner & along(row, col + 1), 1.0, 0.0)
+    spread = split_dot(jnp.concatenate(columns[4:6], axis=0), sides.astype(jnp.bfloat16))
+    faces_n = [0.5 * spread[8 * j : 8 * j + 8, 0:256] for j in range(2)]
+    faces_s = [0.5 * spread[8 * j : 8 * j + 8, 256:512] for j in range(2)]
 
     layer, column = iotas((8, 256))
     crossed = device ^ jnp.where(even, device - 1, device + 1)
@@ -476,7 +517,9 @@
             here = 8 * (MAIN + 2) + place
             part = far_ref[here : here + 8, :]
             if i < 2:
-                straight = early_ref[MAIN + SMALL + place : MAIN + SMALL + place + 8, :]
+                start = MAIN + SMALL + place
+                straight = first_ref[start : start + 8, :]
+                straight = jnp.where(odd, straight, second_ref[MAIN + start : MAIN + start + 8, :])
                 part = jnp.where(crossed == 7, part, jnp.where(crossed == 15, near_ref[here : here + 8, :], 0.0))
                 part = jnp.where(crossed == 3, straight, part)
             parts.append(part)
@@ -499,7 +542,6 @@
         else:
             face = speed_x[1 + f // 4]
         flux_x.append(face * jnp.where(face > 0, cells[f + 1] + halves[f], cells[f + 2] - halves[f + 1]))
-    faces_y = [jnp.where(column < 255, 0.5 * (v + pltpu.roll(v, 255, 1)), 0.0) for v in speed_y]
     faces_z = [jnp.where(layer < 7, 0.5 * (v + pltpu.roll(v, 7, 0)), 0.0) for v in speed_z]
     for x in range(8):
         cell = cells[x + 2]
@@ -511,9 +553,12 @@
         change = change + (flux_x[x + 1] - flux_x[x])
         ahead = jnp.where(column < 255, pltpu.roll(cell, 255, 1), 0.0) - cell
         half = 0.5 * slope_of(jnp.where(column > 0, pltpu.roll(ahead, 1, 1), cell), ahead)
-        face = faces_y[x // 4]
-        flux_y = face * jnp.where(face > 0, cell + half, pltpu.roll(cell - half, 255, 1))
-        change = change + (flux_y - pltpu.roll(flux_y, 1, 1))
+        below, above = cell + half, cell - half
+        face = faces_n[x // 4]
+        flux_n = face * jnp.where(face > 0, below, pltpu.roll(above, 255, 1))
+        face = faces_s[x // 4]
+        flux_s = face * jnp.where(face > 0, pltpu.roll(below, 1, 1), above)
+        change = change + (flux_n - flux_s)
         wet = recharge_ref[x : x + 1, :].astype(jnp.float32)
         dilution = jnp.where(layer == 0, freshening * wet * cell, 0.0)
         tendency_ref[:, x, :] = -step * change - step * dilution
@@ -529,12 +574,13 @@
         ),
         in_specs=[vmem] * 4,
         out_specs=(vmem,) * 3,
-        scratch_shapes=[pltpu.VMEM((32, 32), jnp.float32)],
+        scratch_shapes=[pltpu.VMEM((32, 128), jnp.float32), pltpu.VMEM((32, 128), jnp.float32)],
         name="pack",
     )(salt, recharge, conductivity, codes)
 
-    def swapped(array, distance):
-        return lax.ppermute(array, "gx", [(i, i ^ distance) for i in range(lax.axis_size("gx"))])
+    def swapped(array, turn):
+        pairs = [(i, i ^ ROUNDS[bin(i).count("1") % 2][turn]) for i in range(lax.axis_size("gx"))]
+        return lax.ppermute(array, "gx", pairs)
 
     def small(array, count):
         return array[count * MAIN : count * MAIN + SMALL]
@@ -542,37 +588,36 @@
     def columns(array, count):
         return array[count * MAIN + SMALL :]
 
-    first = swapped(block, ROUNDS[0])
+    relay = jnp.tile(relay, (COLUMNS // 8, 1))
+    first = swapped(block, 0)
+    handed = jnp.where(relay > 1.5, columns(block, 1), columns(first, 1))
+    block = jnp.concatenate([block[:MAIN], first[:MAIN], small(block, 1) + small(first, 1), handed])
+    second = swapped(block, 1)
+    handed = jnp.where(relay > 0.5, columns(second, 2), columns(first, 1))
     block = jnp.concatenate(
-        [block[:MAIN], first[:MAIN], small(block, 1) + small(first, 1), columns(first, 1)]
-    )
-    other = swapped(block, ROUNDS[1])
-    handed = jnp.where(jnp.tile(relay, (COLUMNS // 8, 1)) > 0, columns(other, 2), columns(first, 1))
-    block = jnp.concatenate(
-        [block[: 2 * MAIN], other[: 2 * MAIN], small(block, 2) + small(other, 2), handed]
-    )
-    other = swapped(block, ROUNDS[2])
+        [block[: 2 * MAIN], second[: 2 * MAIN], small(block, 2) + small(second, 2), handed]
+    )
+    other = swapped(block, 2)
     block = jnp.concatenate(
         [block[: 4 * MAIN], other[: 4 * MAIN], small(block, 4), small(other, 4), columns(other, 4), inner]
     )
-    other = swapped(block, ROUNDS[3])
+    other = swapped(block, 3)
     return pl.pallas_call(
         step_kernel,
         out_shape=(
             jax.ShapeDtypeStruct(salt.shape, jnp.float32),
             jax.ShapeDtypeStruct(conductivity.shape, jnp.float32),
         ),
-        in_specs=[vmem] * 5,
+        in_specs=[vmem] * 6,
         out_specs=(vmem,) * 2,
         scratch_shapes=[
-            pltpu.VMEM((13, 16, 8, 128), jnp.float32),
-            pltpu.VMEM((9, 8, 8, 128), jnp.float32),
-            pltpu.VMEM((128, 128), jnp.float32),
+            pltpu.VMEM((15, 16, 8, 128), jnp.float32),
+            pltpu.VMEM((9, 4, 8, 128), jnp.float32),
             pltpu.VMEM((3, 16, 8, 128), jnp.float32),
         ],
         compiler_params=pltpu.CompilerParams(vmem_limit_bytes=16 * 1024 * 1024),
         name="step",
-    )(block, other, first, salt, recharge)
+    )(block, other, first, second, salt, recharge)
 
 def local(salt, recharge, conductivity, codes):
     small = (

time: 19.8 us -> 19 us (0.960)
  the two profiles are of different devices: /device:TPU:29 before, /device:TPU:0 now
where the time goes in v4:
time: 19 us; the launch traced here: 18.9 us
  starting transfers between devices  7.91 us (42%)
  waiting for transfers between devices  6.08 us (32%)
  Pallas kernels  4.13 us (22%)
  between operations  0.69 us (4%)
    ppermute x4, starting transfers between devices, swapped(): return lax.ppermute(array, 'gx', pairs)  7.91 us
    ppermute x4, waiting for transfers between devices, swapped(): return lax.ppermute(array, 'gx', pairs)  6.08 us
    pallas_call x1, Pallas kernels, local_small(): pl.pallas_call(step_kernel, out_shape=(jax.ShapeDtypeStruct(salt.shape, j...  3.02 us
    pallas_call x1, Pallas kernels, local_small(): pl.pallas_call(pack_kernel, out_shape=(pltpu.VMEM((MAIN + SMALL + COLUMNS...  1.11 us
  transfers between devices with their start and end apart: 4, of which 4 were waited for; matrix products, arithmetic and copies ran while one was open for 0% of the time, Pallas kernels for 0%

profile of v4, /device:TPU:0, one launch (start us, length us, event | category | flops | bytes accessed | tf_op | source)
XLA Modules:
  0.0 18.9 jit_solution(6152698393902532108)
XLA Ops:
  0.6 1.1 %pack.1 = (f32[56,128]{1,0:T(8,128)S(1)}, f32[32,128]{1,0:T(8,128)S(1)}, f32[8,128]{1,0:T(8,128)S(1)}) custom-call(f32[8,8,256]{2,1,0:T(8,128)} %salt_ref.3, s32[8,256]{1,0:T(8,128)} %recharge_ref.3, f32[8,4,32]{2,1,0:T(4,128)} %cond_ref.1, s32[4,32]{1,0:T(4,128)} %codes_ref.1), custom_call_target="tpu_custom_call" | custom-call | tf_op jit(solution)/shard_map/pack/pallas_call | solution.py:568
  1.7 3.5 %collective-permute-start = (f32[56,128]{1,0:T(8,128)S(1)}, f32[56,128]{1,0:T(8,128)S(1)}, u32[]{:S(2)}, u32[]{:S(2)}) collective-permute-start(f32[56,128]{1,0:T(8,128)S(1)} %get-tuple-element.5), channel_id=1, source_target_pairs={{0,9},{1,2},{2,1},{3,10},{4,7},{5,12},{6,15},{7,4},{8,11},{9,0},{1... | collective-permute-start | bytes 86024 | tf_op jit(solution)/shard_map/ppermute | solution.py:583
  5.3 1.6 %collective-permute-done.first_ref = f32[56,128]{1,0:T(8,128)S(1)} collective-permute-done((f32[56,128]{1,0:T(8,128)S(1)}, f32[56,128]{1,0:T(8,128)S(1)}, u32[]{:S(2)}, u32[]{:S(2)}) %collective-permute-start) | collective-permute-done | bytes 28704 | tf_op jit(solution)/shard_map/ppermute | solution.py:583
  6.9 1.9 %collective-permute-start.1 = (f32[72,128]{1,0:T(8,128)S(1)}, f32[72,128]{1,0:T(8,128)S(1)}, u32[]{:S(2)}, u32[]{:S(2)}) collective-permute-start(f32[72,128]{1,0:T(8,128)S(1)} %pad_maximum_fusion), channel_id=1, source_target_pairs={{0,3},{1,8},{2,11},{3,0},{4,13},{5,6},{6,5},{7,14},{8,1},{9,10},{1... | collective-permute-start | bytes 110600 | tf_op jit(solution)/shard_map/ppermute | solution.py:583
  8.7 1.6 %collective-permute-done.1.second_ref = f32[72,128]{1,0:T(8,128)S(1)} collective-permute-done((f32[72,128]{1,0:T(8,128)S(1)}, f32[72,128]{1,0:T(8,128)S(1)}, u32[]{:S(2)}, u32[]{:S(2)}) %collective-permute-start.1) | collective-permute-done | bytes 36896 | tf_op jit(solution)/shard_map/ppermute | solution.py:583
  10.4 1.9 %collective-permute-start.2 = (f32[104,128]{1,0:T(8,128)S(1)}, f32[104,128]{1,0:T(8,128)S(1)}, u32[]{:S(2)}, u32[]{:S(2)}) collective-permute-start(f32[104,128]{1,0:T(8,128)S(1)} %get-tuple-element.8), channel_id=1, source_target_pairs={{0,5},{1,4},{2,7},{3,6},{4,1},{5,0},{6,3},{7,2},{8,13},{9,12},{10,... | collective-permute-start | bytes 159752 | tf_op jit(solution)/shard_map/ppermute | solution.py:583
  12.3 1.9 %collective-permute-done.2 = f32[104,128]{1,0:T(8,128)S(1)} collective-permute-done((f32[104,128]{1,0:T(8,128)S(1)}, f32[104,128]{1,0:T(8,128)S(1)}, u32[]{:S(2)}, u32[]{:S(2)}) %collective-permute-start.2) | collective-permute-done | bytes 53280 | tf_op jit(solution)/shard_map/ppermute | solution.py:583
  14.2 0.0 copy-start
  14.3 0.0 copy-start.1
  14.3 0.6 %collective-permute-start.3 = (f32[208,128]{1,0:T(8,128)S(1)}, f32[208,128]{1,0:T(8,128)S(1)}, u32[]{:S(2)}, u32[]{:S(2)}) collective-permute-start(f32[208,128]{1,0:T(8,128)S(1)} %constant_dynamic-update-slice_fusion.5.near_ref), channel_id=1, source_target_pairs={{0,1},{1,0},{2,3},{3,2},{4,5},{5,4},{6,7},{7,6},{8,9},{9,8},{10,11... | collective-permute-start | bytes 319496 | tf_op jit(solution)/shard_map/ppermute | solution.py:583
  14.9 1.0 %collective-permute-done.3.far_ref = f32[208,128]{1,0:T(8,128)S(1)} collective-permute-done((f32[208,128]{1,0:T(8,128)S(1)}, f32[208,128]{1,0:T(8,128)S(1)}, u32[]{:S(2)}, u32[]{:S(2)}) %collective-permute-start.3) | collective-permute-done | bytes 106528 | tf_op jit(solution)/shard_map/ppermute | solution.py:583
  15.8 0.0 copy-done
  15.8 0.0 copy-done.1
  15.8 3.0 %step.1 = (f32[8,8,256]{2,1,0:T(8,128)}, f32[8,4,32]{2,1,0:T(4,128)}) custom-call(f32[208,128]{1,0:T(8,128)S(1)} %constant_dynamic-update-slice_fusion.5.near_ref, f32[208,128]{1,0:T(8,128)S(1)} %collective-permute-done.3.far_ref, f32[56,128]{1,0:T(8,128)S(1)} %collective-permute-done.first_ref, f32[72,128]{1,0:T(8,128)S(1)} %collective-permute-done.1.second_ref, ...), custom_call_target="tpu_custom_call" | custom-call | tf_op jit(solution)/shard_map/step/pallas_call | solution.py:605
  (13 shorter events, 0.0 us)
Async XLA Ops:
  1.7 5.1 %collective-permute-start = (f32[56,128]{1,0:T(8,128)S(1)}, f32[56,128]{1,0:T(8,128)S(1)}, u32[]{:S(2)}, u32[]{:S(2)}) collective-permute-start(f32[56,128]{1,0:T(8,128)S(1)} %get-tuple-element.5), channel_id=1, source_target_pairs={{0,9},{1,2},{2,1},{3,10},{4,7},{5,12},{6,15},{7,4},{8,11},{9,0},{1... | collective-permute-start | bytes 86024 | tf_op jit(solution)/shard_map/ppermute | solution.py:583
  6.9 3.5 %collective-permute-start.1 = (f32[72,128]{1,0:T(8,128)S(1)}, f32[72,128]{1,0:T(8,128)S(1)}, u32[]{:S(2)}, u32[]{:S(2)}) collective-permute-start(f32[72,128]{1,0:T(8,128)S(1)} %pad_maximum_fusion), channel_id=1, source_target_pairs={{0,3},{1,8},{2,11},{3,0},{4,13},{5,6},{6,5},{7,14},{8,1},{9,10},{1... | collective-permute-start | bytes 110600 | tf_op jit(solution)/shard_map/ppermute | solution.py:583
  10.4 3.8 %collective-permute-start.2 = (f32[104,128]{1,0:T(8,128)S(1)}, f32[104,128]{1,0:T(8,128)S(1)}, u32[]{:S(2)}, u32[]{:S(2)}) collective-permute-start(f32[104,128]{1,0:T(8,128)S(1)} %get-tuple-element.8), channel_id=1, source_target_pairs={{0,5},{1,4},{2,7},{3,6},{4,1},{5,0},{6,3},{7,2},{8,13},{9,12},{10,... | collective-permute-start | bytes 159752 | tf_op jit(solution)/shard_map/ppermute | solution.py:583
  14.2 1.6 %copy-start = (f32[8,8,256]{2,1,0:T(8,128)S(1)}, f32[8,8,256]{2,1,0:T(8,128)}, u32[]{:S(2)}) copy-start(f32[8,8,256]{2,1,0:T(8,128)} %salt_ref.3) | copy-start | bytes 196612
  14.3 1.6 %copy-start.1 = (s32[8,256]{1,0:T(8,128)S(1)}, s32[8,256]{1,0:T(8,128)}, u32[]{:S(2)}) copy-start(s32[8,256]{1,0:T(8,128)} %recharge_ref.3) | copy-start | bytes 24580
  14.3 1.5 %collective-permute-start.3 = (f32[208,128]{1,0:T(8,128)S(1)}, f32[208,128]{1,0:T(8,128)S(1)}, u32[]{:S(2)}, u32[]{:S(2)}) collective-permute-start(f32[208,128]{1,0:T(8,128)S(1)} %constant_dynamic-update-slice_fusion.5.near_ref), channel_id=1, source_target_pairs={{0,1},{1,0},{2,3},{3,2},{4,5},{5,4},{6,7},{7,6},{8,9},{9,8},{10,11... | collective-permute-start | bytes 319496 | tf_op jit(solution)/shard_map/ppermute | solution.py:583

commit v5 on v4

--- a/solution.py
+++ b/solution.py
@@ -215,15 +215,14 @@
     tendency = -step * change - step * dilution
     return (tendency, head)
 
-def split_dot(values, table):
+def split_dot(values, table, terms=3):
     rows = values.shape[0]
-    high = values.astype(jnp.bfloat16)
-    rest = values - high.astype(jnp.float32)
-    mid = rest.astype(jnp.bfloat16)
-    low = (rest - mid.astype(jnp.float32)).astype(jnp.bfloat16)
-    stacked = jnp.concatenate([high, mid, low], axis=0)
-    out = jnp.dot(stacked, table, preferred_element_type=jnp.float32)
-    return out[:rows] + out[rows : 2 * rows] + out[2 * rows :]
+    parts = []
+    for _ in range(terms):
+        parts.append(values.astype(jnp.bfloat16))
+        values = values - parts[-1].astype(jnp.float32)
+    out = jnp.dot(jnp.concatenate(parts, axis=0), table, preferred_element_type=jnp.float32)
+    return sum(out[rows * i : rows * (i + 1)] for i in range(1, terms)) + out[:rows]
 
 def table_of(shape, same):
     row = lax.broadcasted_iota(jnp.int32, shape, 0)
@@ -237,11 +236,11 @@
 ROUNDS = ((9, 3, 5, 1), (3, 9, 5, 1))
 
 def odd_ones(device):
-    return lax.rem(device + device // 2 + device // 4 + device // 8, 2) == 1
+    return ((device ^ (device >> 1) ^ (device >> 2) ^ (device >> 3)) & 1) == 1
 
 def pack_kernel(salt_ref, recharge_ref, cond_ref, codes_ref, block_ref, inner_ref, relay_ref, flat_ref, turn_ref):
     device = lax.axis_index("gx")
-    even = lax.rem(device, 2) == 0
+    even = (device & 1) == 0
     for j in range(2):
         first = salt_ref[:, j, :]
         last = salt_ref[:, 6 + j, :]
@@ -254,11 +253,11 @@
             block_ref[place : place + 8, :] = outward[:, 128 * half : 128 * half + 128]
     relay = jnp.where(odd_ones(device), jnp.where((device == 2) | (device == 13), 1.0, 0.0), 2.0)
     relay_ref[...] = jnp.broadcast_to(relay, (8, 128))
-    turned = device // 2
-    sums = table_of((256, 128), lambda r, c: r // 4 == 4 * (c // 8) + ((c - turned) % 8) // 2)
+    turned = device >> 1
+    sums = table_of((256, 128), lambda r, c: (r >> 2) == ((c >> 3) << 2) + (((c - turned) & 7) >> 1))
     salt_y = split_dot(salt_ref[...].reshape(64, 256), sums).reshape(8, 8, 128)
     sub, lane = iotas((8, 128))
-    mine = sub // 4 == (lane - turned) % 2
+    mine = (sub >> 2) == ((lane - turned) & 1)
     block_ref[0:8, :] = jnp.sum(jnp.where(mine[None], salt_y, 0.0), axis=1) * 0.0625
     wet_y = jnp.dot(
         recharge_ref[...].astype(jnp.float32).astype(jnp.bfloat16), sums, preferred_element_type=jnp.float32
@@ -266,18 +265,18 @@
     wet_row = jnp.sum(jnp.where(mine, wet_y, 0.0), axis=0, keepdims=True) * 0.0625
     for layer in range(8):
         flat_ref[4 * layer : 4 * layer + 4, 0:32] = cond_ref[layer]
-    spread = table_of((32, 128), lambda r, c: r == 4 * (c % 8) + (c // 8 - device) % 4)
+    spread = table_of((32, 128), lambda r, c: r == ((c & 7) << 2) + (((c >> 3) - device) & 3))
     turn_ref[...] = split_dot(flat_ref[:, 0:32], spread)
     packed = jnp.zeros((8, 128), jnp.float32)
     for j in range(4):
-        packed = jnp.where((lane // 8 - device) % 16 // 4 == j, turn_ref[pl.ds(j, 8, stride=4), :], packed)
+        packed = jnp.where(((((lane >> 3) - device) & 15) >> 2) == j, turn_ref[pl.ds(j, 8, stride=4), :], packed)
     block_ref[8:16, :] = packed
     code_x = jnp.dot(
         codes_ref[...].astype(jnp.float32).astype(jnp.bfloat16), spread, preferred_element_type=jnp.float32
     )
     row4, lane4 = iotas((4, 128))
-    code_row = jnp.sum(jnp.where(row4 == (lane4 // 8 - device) % 16 // 4, code_x, 0.0), axis=0, keepdims=True)
-    slot = 2 * ((device // 2) % 2) + 4 * (device // 8)
+    code_row = jnp.sum(jnp.where(row4 == ((((lane4 >> 3) - device) & 15) >> 2), code_x, 0.0), axis=0, keepdims=True)
+    slot = (device & 2) + ((device & 8) >> 1)
     block_ref[16:24, :] = jnp.where(sub == slot, wet_row, jnp.where(sub == slot + 1, code_row, 0.0))
 
 def harm(first, second):
@@ -305,30 +304,32 @@
     return pltpu.roll(cell, 7, 0)
 
 def step_kernel(
-    near_ref, far_ref, first_ref, second_ref, salt_ref, recharge_ref, tendency_ref, head_ref, fine_ref, coarse_ref, wide_ref
+    near_ref, far_ref, first_ref, second_ref, salt_ref, recharge_ref, tendency_ref, head_ref, fine_ref, coarse_ref, ring_ref, wide_ref
 ):
     device = lax.axis_index("gx")
     sub, lane = iotas((8, 128))
     top = sub == 0
-    even = lax.rem(device, 2) == 0
+    even = (device & 1) == 0
     odd = odd_ones(device)
+    orders = [lambda e: ((e >> 3) & 1) + (e & 2) + (e & 4), lambda e: ((e >> 1) & 1) + ((e & 8) >> 2) + (e & 4)]
+    here = jnp.where(odd, orders[1](device), orders[0](device))
+    there = jnp.where(odd, orders[0](device), orders[1](device))
+    flip = (device & 4) != 0
+    small = []
+    for ref in (near_ref, far_ref):
+        halves = [ref[8 * MAIN + SMALL * i : 8 * MAIN + SMALL * (i + 1), :] for i in range(2)]
+        small.append([jnp.where(flip, halves[1 - i], halves[i]) for i in range(2)])
     means, conds, smalls = [], [], []
-    for e in range(0, 16, 2):
-        apart = device ^ e
-        ones, nines, fives = (apart // 2) % 2, apart // 8, (apart // 4) % 2
-        places = [nines + 2 * ones + 4 * fives, ones + 2 * nines + 4 * fives]
-        here = jnp.where(odd, places[1], places[0])
-        there = jnp.where(odd, places[0], places[1])
+    for e in range(16):
         mine = odd == (bin(e).count("1") % 2 == 1)
-
-        def block_pair(here, there):
-            near = near_ref[pl.ds(pl.multiple_of(here, 8), 8), :]
-            far = far_ref[pl.ds(pl.multiple_of(there, 8), 8), :]
-            return [jnp.where(mine, near, far), jnp.where(mine, far, near)]
-
-        means += block_pair(MAIN * here, MAIN * there)
-        conds += block_pair(MAIN * here + 8, MAIN * there + 8)
-        smalls += block_pair(8 * MAIN + SMALL * fives, 8 * MAIN + SMALL * fives)
+        if e % 2 == 0:
+            start = pl.multiple_of((here ^ jnp.where(odd, orders[1](e), orders[0](e))) * MAIN, 8)
+            near = [near_ref[pl.ds(start, 8), :], near_ref[pl.ds(pl.multiple_of(start + 8, 8), 8), :]]
+            start = pl.multiple_of((there ^ jnp.where(odd, orders[0](e), orders[1](e))) * MAIN, 8)
+            far = [far_ref[pl.ds(start, 8), :], far_ref[pl.ds(pl.multiple_of(start + 8, 8), 8), :]]
+        means.append(jnp.where(mine, near[0], far[0]))
+        conds.append(jnp.where(mine, near[1], far[1]))
+        smalls.append(jnp.where(mine, small[0][(e >> 2) & 1], small[1][(e >> 2) & 1]))
 
     slots = [2 * ((e // 2) % 2) + 4 * (e // 8) for e in range(16)]
     wets = [smalls[e][slots[e] : slots[e] + 1] for e in range(16)]
@@ -344,12 +345,12 @@
         return fields
 
     def by_block(fields):
-        group = lane[0 : fields[0].shape[0]] // 8
+        group = lane[0 : fields[0].shape[0]] >> 3
         picked = diagonals(fields, group)
         return [pltpu.roll(picked[-k % 16], (128 - 8 * k) % 128, 1) for k in range(16)]
 
     def by_lane(fields):
-        within = lane % 8
+        within = lane & 7
         out = []
         picked = diagonals(fields, within)
         for s in range(8):
@@ -376,13 +377,13 @@
         for k in range(side * side):
             e = harm(cells[k], east_of(cells, k, side))
             if k % side == side - 1:
-                e = jnp.where(lane % 8 < 7, e, 0.0)
+                e = jnp.where((lane & 7) < 7, e, 0.0)
             n = harm(cells[k], north_of(cells, k, side))
             if k >= side * (side - 1):
                 n = jnp.where(lane < 120, n, 0.0)
             w = face_e[k - 1] if k % side > 0 else None
             if w is None:
-                w = jnp.where(lane % 8 > 0, harm(west_of(cells, k, side), cells[k]), 0.0)
+                w = jnp.where((lane & 7) > 0, harm(west_of(cells, k, side), cells[k]), 0.0)
             s = face_n[k - side] if k >= side else None
             if s is None:
                 s = jnp.where(lane >= 8, harm(south_of(cells, k, side), cells[k]), 0.0)
@@ -420,6 +421,36 @@
             out.append(((terms[0] + terms[1]) + (terms[2] + terms[3])) + ((terms[4] + terms[5]) + base))
         return out
 
+    ring = [(j, i) for j in range(-1, 3) for i in range(-1, 3) if (j in (0, 1)) != (i in (0, 1))]
+
+    def beyond(cells, j, i):
+        shift = -(8 * (j // 2) + i // 2) % 128
+        cell = cells[2 * (j % 2) + i % 2]
+        return pltpu.roll(cell, shift, 1) if shift else cell
+
+    def relaxed_twice(cells):
+        def step(at, j, i, weights):
+            here = at(j, i)
+            pairs = (at(j, i - 1), at(j, i + 1), at(j - 1, i), at(j + 1, i), upper_of(here), lower_of(here))
+            terms = [weights(number) * pair for number, pair in enumerate(pairs)]
+            base = (1.0 - relax_weight) * here + weights(8)
+            return ((terms[0] + terms[1]) + (terms[2] + terms[3])) + ((terms[4] + terms[5]) + base)
+
+        old, new = {}, {}
+
+        def at_old(j, i):
+            if (j, i) not in old:
+                old[j, i] = beyond(cells, j, i)
+            return old[j, i]
+
+        for q, (j, i) in enumerate(ring):
+            new[j, i] = step(at_old, j, i, lambda number, q=q: ring_ref[number, q])
+        for k in range(4):
+            new[k // 2, k % 2] = step(at_old, k // 2, k % 2, lambda number, k=k: coarse_ref[number, k])
+        return [
+            step(lambda j, i: new[j, i], k // 2, k % 2, lambda number, k=k: coarse_ref[number, k]) for k in range(4)
+        ]
+
     def pair_sums(cells):
         return [(cells[k] + cells[k + 1]) + (cells[k + 4] + cells[k + 5]) for k in (0, 2, 8, 10)]
 
@@ -438,6 +469,10 @@
         for number, face in enumerate(faces):
             fine_ref[10 + number, k] = face[k]
     coefficients([0.25 * c for c in pair_sums(cond)], pair_sums(penalty), 2, 4.0 * vertical_ratio, coarse_ref)
+    for number in range(6):
+        cells = [coarse_ref[number, k] for k in range(4)]
+        for q, (j, i) in enumerate(ring):
+            ring_ref[number, q] = beyond(cells, j, i)
 
     head = None
     for cycle_no in range(CYCLES):
@@ -449,23 +484,22 @@
         for k in range(4):
             correction.append(coarse_ref[7, k] * resid[k])
             coarse_ref[8, k] = correction[k]
-        for sweep in range(COARSE_SWEEPS - 1):
+        for q, (j, i) in enumerate(ring):
+            ring_ref[8, q] = beyond(correction, j, i)
+        for sweep in range((COARSE_SWEEPS - 1) // 2):
+            correction = relaxed_twice(correction)
+        for sweep in range((COARSE_SWEEPS - 1) % 2):
             correction = relaxed(correction, 2, coarse_ref)
         head = [head[k] + correction[2 * (k // 8) + (k % 4) // 2] for k in range(16)]
         for sweep in range(SMOOTH):
             head = relaxed(head, 4, fine_ref)
 
-    rows = []
+    own = 8 * device + ((lane & 31) >> 2)
     for j in range(4):
-        row = jnp.zeros((8, 128), jnp.float32)
-        for i in range(4):
-            row = jnp.where(lane // 8 == i, pltpu.roll(head[4 * j + i], lax.rem(8 * i - 8 * device + 128, 128), 1), row)
-        rows.append(row)
-    own = split_dot(
-        jnp.concatenate(rows, axis=0), table_of((128, 128), lambda r, c: (r < 32) & (c == 4 * (r % 8) + r // 8))
-    )
-    for j in range(4):
-        head_ref[:, j, :] = own[8 * j : 8 * j + 8, 0:32]
+        row = jnp.take_along_axis(head[4 * j], own, axis=1)
+        for i in range(1, 4):
+            row = jnp.where((lane & 3) == i, jnp.take_along_axis(head[4 * j + i], own, axis=1), row)
+        head_ref[:, j, :] = row[:, 0:32]
 
     largest = None
     for k in range(16):
@@ -483,29 +517,23 @@
         largest = speed if largest is None else jnp.maximum(largest, speed)
     step = courant / (jnp.max(largest, axis=(0, 1), keepdims=True) + 1e-06)
 
-    columns = []
-    for field, wanted in ((0, (0, 1, 2, 3)), (1, (1, 2)), (2, (1, 2))):
-        for j in wanted:
-            x = jnp.clip(2 * device - 1 + j, 0, 31)
-            column = jnp.zeros((8, 128), jnp.float32)
-            for i in range(4):
-                turned = pltpu.roll(wide_ref[field, 4 * i + lax.rem(x, 4)], lax.rem(128 + i - x // 4, 128), 1)
-                column = jnp.where(lane % 8 == i, turned, column)
-            columns.append(column)
-
-    def along(r, c):
-        return (r % 8 < 4) & (c // 4 == 4 * (r // 8) + r % 8)
-
-    spread = split_dot(jnp.concatenate(columns[:4] + columns[6:], axis=0), table_of((128, 256), along))
-    speed_x = [spread[8 * j : 8 * j + 8] for j in range(4)]
-    speed_z = [spread[32 + 8 * j : 40 + 8 * j] for j in range(2)]
-    row, col = iotas((128, 512))
-    col = jnp.where(col < 256, col, col - 257)
-    inner = (col >= 0) & (col < 255)
-    sides = jnp.where(inner & along(row, col), 1.0, 0.0) + jnp.where(inner & along(row, col + 1), 1.0, 0.0)
-    spread = split_dot(jnp.concatenate(columns[4:6], axis=0), sides.astype(jnp.bfloat16))
-    faces_n = [0.5 * spread[8 * j : 8 * j + 8, 0:256] for j in range(2)]
-    faces_s = [0.5 * spread[8 * j : 8 * j + 8, 256:512] for j in range(2)]
+    def along(field, x, shift=0):
+        halves = []
+        for half in range(2):
+            y = jnp.clip(128 * half + lane + shift, 0, 255) >> 2
+            source = ((y >> 2) << 3) + (x >> 2)
+            part = jnp.take_along_axis(wide_ref[field, x & 3], source, axis=1)
+            for j in range(1, 4):
+                part = jnp.where((y & 3) == j, jnp.take_along_axis(wide_ref[field, 4 * j + (x & 3)], source, axis=1), part)
+            halves.append(part)
+        return jnp.concatenate(halves, axis=1)
+
+    xs = [jnp.clip(2 * device - 1 + j, 0, 31) for j in range(4)]
+    speed_x = [along(0, x) for x in xs]
+    speed_z = [along(2, x) for x in xs[1:3]]
+    speed_y = [along(1, x) for x in xs[1:3]]
+    north_y = [along(1, x, 1) for x in xs[1:3]]
+    south_y = [along(1, x, -1) for x in xs[1:3]]
 
     layer, column = iotas((8, 256))
     crossed = device ^ jnp.where(even, device - 1, device + 1)
@@ -543,6 +571,8 @@
             face = speed_x[1 + f // 4]
         flux_x.append(face * jnp.where(face > 0, cells[f + 1] + halves[f], cells[f + 2] - halves[f + 1]))
     faces_z = [jnp.where(layer < 7, 0.5 * (v + pltpu.roll(v, 7, 0)), 0.0) for v in speed_z]
+    faces_n = [jnp.where(column < 255, 0.5 * (v + beside), 0.0) for v, beside in zip(speed_y, north_y)]
+    faces_s = [jnp.where(column > 0, 0.5 * (beside + v), 0.0) for v, beside in zip(speed_y, south_y)]
     for x in range(8):
         cell = cells[x + 2]
         ahead = jnp.where(layer < 7, pltpu.roll(cell, 7, 0), 0.0) - cell
@@ -613,6 +643,7 @@
         scratch_shapes=[
             pltpu.VMEM((15, 16, 8, 128), jnp.float32),
             pltpu.VMEM((9, 4, 8, 128), jnp.float32),
+            pltpu.VMEM((9, 8, 8, 128), jnp.float32),
             pltpu.VMEM((3, 16, 8, 128), jnp.float32),
         ],
         compiler_params=pltpu.CompilerParams(vmem_limit_bytes=16 * 1024 * 1024),

time: 19 us -> 18.5 us (0.974)
  Pallas kernels: 4.13 us -> 3.66 us
    pallas_call x1, Pallas kernels: 3.02 us -> 2.56 us  [local_small(): pl.pallas_call(step_kernel, out_shape=(jax.ShapeDtypeStruct(salt.shape, j...]
where the time goes in v5:
time: 18.5 us; the launch traced here: 18.4 us
  starting transfers between devices  7.91 us (43%)
  waiting for transfers between devices  6.08 us (33%)
  Pallas kernels  3.66 us (20%)
  between operations  0.69 us (4%)
    ppermute x4, starting transfers between devices, swapped(): return lax.ppermute(array, 'gx', pairs)  7.91 us
    ppermute x4, waiting for transfers between devices, swapped(): return lax.ppermute(array, 'gx', pairs)  6.08 us
    pallas_call x1, Pallas kernels, local_small(): pl.pallas_call(step_kernel, out_shape=(jax.ShapeDtypeStruct(salt.shape, j...  2.56 us
    pallas_call x1, Pallas kernels, local_small(): pl.pallas_call(pack_kernel, out_shape=(pltpu.VMEM((MAIN + SMALL + COLUMNS...  1.09 us
  transfers between devices with their start and end apart: 4, of which 4 were waited for; matrix products, arithmetic and copies ran while one was open for 0% of the time, Pallas kernels for 0%

profile of v5, /device:TPU:0, one launch (start us, length us, event | category | flops | bytes accessed | tf_op | source)
XLA Modules:
  0.0 18.4 jit_solution(10354541808859113859)
XLA Ops:
  0.6 1.1 %pack.1 = (f32[56,128]{1,0:T(8,128)S(1)}, f32[32,128]{1,0:T(8,128)S(1)}, f32[8,128]{1,0:T(8,128)S(1)}) custom-call(f32[8,8,256]{2,1,0:T(8,128)} %salt_ref.3, s32[8,256]{1,0:T(8,128)} %recharge_ref.3, f32[8,4,32]{2,1,0:T(4,128)} %cond_ref.1, s32[4,32]{1,0:T(4,128)} %codes_ref.1), custom_call_target="tpu_custom_call" | custom-call | tf_op jit(solution)/shard_map/pack/pallas_call | solution.py:598
  1.7 3.5 %collective-permute-start = (f32[56,128]{1,0:T(8,128)S(1)}, f32[56,128]{1,0:T(8,128)S(1)}, u32[]{:S(2)}, u32[]{:S(2)}) collective-permute-start(f32[56,128]{1,0:T(8,128)S(1)} %get-tuple-element.5), channel_id=1, source_target_pairs={{0,9},{1,2},{2,1},{3,10},{4,7},{5,12},{6,15},{7,4},{8,11},{9,0},{1... | collective-permute-start | bytes 86024 | tf_op jit(solution)/shard_map/ppermute | solution.py:613
  5.3 1.6 %collective-permute-done.first_ref = f32[56,128]{1,0:T(8,128)S(1)} collective-permute-done((f32[56,128]{1,0:T(8,128)S(1)}, f32[56,128]{1,0:T(8,128)S(1)}, u32[]{:S(2)}, u32[]{:S(2)}) %collective-permute-start) | collective-permute-done | bytes 28704 | tf_op jit(solution)/shard_map/ppermute | solution.py:613
  6.9 1.9 %collective-permute-start.1 = (f32[72,128]{1,0:T(8,128)S(1)}, f32[72,128]{1,0:T(8,128)S(1)}, u32[]{:S(2)}, u32[]{:S(2)}) collective-permute-start(f32[72,128]{1,0:T(8,128)S(1)} %pad_maximum_fusion), channel_id=1, source_target_pairs={{0,3},{1,8},{2,11},{3,0},{4,13},{5,6},{6,5},{7,14},{8,1},{9,10},{1... | collective-permute-start | bytes 110600 | tf_op jit(solution)/shard_map/ppermute | solution.py:613
  8.7 1.6 %collective-permute-done.1.second_ref = f32[72,128]{1,0:T(8,128)S(1)} collective-permute-done((f32[72,128]{1,0:T(8,128)S(1)}, f32[72,128]{1,0:T(8,128)S(1)}, u32[]{:S(2)}, u32[]{:S(2)}) %collective-permute-start.1) | collective-permute-done | bytes 36896 | tf_op jit(solution)/shard_map/ppermute | solution.py:613
  10.4 1.9 %collective-permute-start.2 = (f32[104,128]{1,0:T(8,128)S(1)}, f32[104,128]{1,0:T(8,128)S(1)}, u32[]{:S(2)}, u32[]{:S(2)}) collective-permute-start(f32[104,128]{1,0:T(8,128)S(1)} %get-tuple-element.8), channel_id=1, source_target_pairs={{0,5},{1,4},{2,7},{3,6},{4,1},{5,0},{6,3},{7,2},{8,13},{9,12},{10,... | collective-permute-start | bytes 159752 | tf_op jit(solution)/shard_map/ppermute | solution.py:613
  12.3 1.9 %collective-permute-done.2 = f32[104,128]{1,0:T(8,128)S(1)} collective-permute-done((f32[104,128]{1,0:T(8,128)S(1)}, f32[104,128]{1,0:T(8,128)S(1)}, u32[]{:S(2)}, u32[]{:S(2)}) %collective-permute-start.2) | collective-permute-done | bytes 53280 | tf_op jit(solution)/shard_map/ppermute | solution.py:613
  14.2 0.0 copy-start
  14.2 0.0 copy-start.1
  14.3 0.6 %collective-permute-start.3 = (f32[208,128]{1,0:T(8,128)S(1)}, f32[208,128]{1,0:T(8,128)S(1)}, u32[]{:S(2)}, u32[]{:S(2)}) collective-permute-start(f32[208,128]{1,0:T(8,128)S(1)} %constant_dynamic-update-slice_fusion.5.near_ref), channel_id=1, source_target_pairs={{0,1},{1,0},{2,3},{3,2},{4,5},{5,4},{6,7},{7,6},{8,9},{9,8},{10,11... | collective-permute-start | bytes 319496 | tf_op jit(solution)/shard_map/ppermute | solution.py:613
  14.9 1.0 %collective-permute-done.3.far_ref = f32[208,128]{1,0:T(8,128)S(1)} collective-permute-done((f32[208,128]{1,0:T(8,128)S(1)}, f32[208,128]{1,0:T(8,128)S(1)}, u32[]{:S(2)}, u32[]{:S(2)}) %collective-permute-start.3) | collective-permute-done | bytes 106528 | tf_op jit(solution)/shard_map/ppermute | solution.py:613
  15.8 0.0 copy-done
  15.8 0.0 copy-done.1
  15.8 2.6 %step.1 = (f32[8,8,256]{2,1,0:T(8,128)}, f32[8,4,32]{2,1,0:T(4,128)}) custom-call(f32[208,128]{1,0:T(8,128)S(1)} %constant_dynamic-update-slice_fusion.5.near_ref, f32[208,128]{1,0:T(8,128)S(1)} %collective-permute-done.3.far_ref, f32[56,128]{1,0:T(8,128)S(1)} %collective-permute-done.first_ref, f32[72,128]{1,0:T(8,128)S(1)} %collective-permute-done.1.second_ref, ...), custom_call_target="tpu_custom_call" | custom-call | tf_op jit(solution)/shard_map/step/pallas_call | solution.py:635
  (13 shorter events, 0.0 us)
Async XLA Ops:
  1.7 5.1 %collective-permute-start = (f32[56,128]{1,0:T(8,128)S(1)}, f32[56,128]{1,0:T(8,128)S(1)}, u32[]{:S(2)}, u32[]{:S(2)}) collective-permute-start(f32[56,128]{1,0:T(8,128)S(1)} %get-tuple-element.5), channel_id=1, source_target_pairs={{0,9},{1,2},{2,1},{3,10},{4,7},{5,12},{6,15},{7,4},{8,11},{9,0},{1... | collective-permute-start | bytes 86024 | tf_op jit(solution)/shard_map/ppermute | solution.py:613
  6.9 3.5 %collective-permute-start.1 = (f32[72,128]{1,0:T(8,128)S(1)}, f32[72,128]{1,0:T(8,128)S(1)}, u32[]{:S(2)}, u32[]{:S(2)}) collective-permute-start(f32[72,128]{1,0:T(8,128)S(1)} %pad_maximum_fusion), channel_id=1, source_target_pairs={{0,3},{1,8},{2,11},{3,0},{4,13},{5,6},{6,5},{7,14},{8,1},{9,10},{1... | collective-permute-start | bytes 110600 | tf_op jit(solution)/shard_map/ppermute | solution.py:613
  10.4 3.8 %collective-permute-start.2 = (f32[104,128]{1,0:T(8,128)S(1)}, f32[104,128]{1,0:T(8,128)S(1)}, u32[]{:S(2)}, u32[]{:S(2)}) collective-permute-start(f32[104,128]{1,0:T(8,128)S(1)} %get-tuple-element.8), channel_id=1, source_target_pairs={{0,5},{1,4},{2,7},{3,6},{4,1},{5,0},{6,3},{7,2},{8,13},{9,12},{10,... | collective-permute-start | bytes 159752 | tf_op jit(solution)/shard_map/ppermute | solution.py:613
  14.2 1.6 %copy-start = (f32[8,8,256]{2,1,0:T(8,128)S(1)}, f32[8,8,256]{2,1,0:T(8,128)}, u32[]{:S(2)}) copy-start(f32[8,8,256]{2,1,0:T(8,128)} %salt_ref.3) | copy-start | bytes 196612
  14.2 1.6 %copy-start.1 = (s32[8,256]{1,0:T(8,128)S(1)}, s32[8,256]{1,0:T(8,128)}, u32[]{:S(2)}) copy-start(s32[8,256]{1,0:T(8,128)} %recharge_ref.3) | copy-start | bytes 24580
  14.3 1.5 %collective-permute-start.3 = (f32[208,128]{1,0:T(8,128)S(1)}, f32[208,128]{1,0:T(8,128)S(1)}, u32[]{:S(2)}, u32[]{:S(2)}) collective-permute-start(f32[208,128]{1,0:T(8,128)S(1)} %constant_dynamic-update-slice_fusion.5.near_ref), channel_id=1, source_target_pairs={{0,1},{1,0},{2,3},{3,2},{4,5},{5,4},{6,7},{7,6},{8,9},{9,8},{10,11... | collective-permute-start | bytes 319496 | tf_op jit(solution)/shard_map/ppermute | solution.py:613

commit v6 on v5

--- a/solution.py
+++ b/solution.py
@@ -255,29 +255,37 @@
     relay_ref[...] = jnp.broadcast_to(relay, (8, 128))
     turned = device >> 1
     sums = table_of((256, 128), lambda r, c: (r >> 2) == ((c >> 3) << 2) + (((c - turned) & 7) >> 1))
-    salt_y = split_dot(salt_ref[...].reshape(64, 256), sums).reshape(8, 8, 128)
+    for i in range(8):
+        four = salt_ref[i] + pltpu.roll(salt_ref[i], 7, 0)
+        four = four + pltpu.roll(four, 6, 0)
+        flat_ref[0, 8 * i : 8 * i + 8, :] = four[:, 0:128]
+        flat_ref[1, 8 * i : 8 * i + 8, :] = four[:, 128:256]
+    rows = [
+        jnp.concatenate([flat_ref[half, pl.ds(start, 8, stride=8), :] for half in range(2)], axis=1) for start in (0, 4)
+    ]
+    means = split_dot(jnp.concatenate(rows, axis=0), sums) * 0.0625
     sub, lane = iotas((8, 128))
     mine = (sub >> 2) == ((lane - turned) & 1)
-    block_ref[0:8, :] = jnp.sum(jnp.where(mine[None], salt_y, 0.0), axis=1) * 0.0625
+    block_ref[0:8, :] = jnp.where(((lane - turned) & 1) == 0, means[0:8], means[8:16])
     wet_y = jnp.dot(
         recharge_ref[...].astype(jnp.float32).astype(jnp.bfloat16), sums, preferred_element_type=jnp.float32
     )
     wet_row = jnp.sum(jnp.where(mine, wet_y, 0.0), axis=0, keepdims=True) * 0.0625
     for layer in range(8):
-        flat_ref[4 * layer : 4 * layer + 4, 0:32] = cond_ref[layer]
+        turn_ref[4 * layer : 4 * layer + 4, 0:32] = cond_ref[layer]
     spread = table_of((32, 128), lambda r, c: r == ((c & 7) << 2) + (((c >> 3) - device) & 3))
-    turn_ref[...] = split_dot(flat_ref[:, 0:32], spread)
+    turn_ref[...] = split_dot(turn_ref[:, 0:32], spread)
     packed = jnp.zeros((8, 128), jnp.float32)
     for j in range(4):
         packed = jnp.where(((((lane >> 3) - device) & 15) >> 2) == j, turn_ref[pl.ds(j, 8, stride=4), :], packed)
     block_ref[8:16, :] = packed
-    code_x = jnp.dot(
-        codes_ref[...].astype(jnp.float32).astype(jnp.bfloat16), spread, preferred_element_type=jnp.float32
-    )
+    codes = codes_ref[...]
+    penalty = jnp.where(codes == 1, sea_penalty, 0.0) + jnp.where(codes == 2, river_penalty, 0.0)
+    penalty_x = jnp.dot(penalty.astype(jnp.bfloat16), spread, preferred_element_type=jnp.float32)
     row4, lane4 = iotas((4, 128))
-    code_row = jnp.sum(jnp.where(row4 == ((((lane4 >> 3) - device) & 15) >> 2), code_x, 0.0), axis=0, keepdims=True)
+    penalty_row = jnp.sum(jnp.where(row4 == ((((lane4 >> 3) - device) & 15) >> 2), penalty_x, 0.0), axis=0, keepdims=True)
     slot = (device & 2) + ((device & 8) >> 1)
-    block_ref[16:24, :] = jnp.where(sub == slot, wet_row, jnp.where(sub == slot + 1, code_row, 0.0))
+    block_ref[16:24, :] = jnp.where(sub == slot, wet_row, jnp.where(sub == slot + 1, penalty_row, 0.0))
 
 def harm(first, second):
     return 2.0 * first * second / (first + second)
@@ -333,7 +341,7 @@
 
     slots = [2 * ((e // 2) % 2) + 4 * (e // 8) for e in range(16)]
     wets = [smalls[e][slots[e] : slots[e] + 1] for e in range(16)]
-    codes = [smalls[e][slots[e] + 1 : slots[e] + 2] for e in range(16)]
+    penalties = [smalls[e][slots[e] + 1 : slots[e] + 2] for e in range(16)]
 
     def diagonals(fields, index):
         count = len(fields)
@@ -361,7 +369,7 @@
         return out
 
     cond = by_block(conds)
-    codes = by_block(codes)
+    penalties = by_block(penalties)
     salt = [None] * 16
     wet_frac = [None] * 16
     wet_pairs = by_lane([jnp.where(top, wets[2 * b], wets[2 * b + 1]) for b in range(8)])
@@ -456,9 +464,8 @@
 
     penalty, river = [], []
     for k in range(16):
-        code = codes[k]
-        river.append(jnp.where(top & (code == 2.0), river_penalty, 0.0))
-        penalty.append(jnp.where(top & (code == 1.0), sea_penalty, 0.0) + river[k])
+        penalty.append(jnp.where(top, penalties[k], 0.0))
+        river.append(jnp.where(penalties[k] == river_penalty, river_penalty, 0.0))
     faces, weights = coefficients(cond, penalty, 4, vertical_ratio, fine_ref)
     for k in range(16):
         below = jnp.where(sub < 7, 0.5 * (salt[k] + lower_of(salt[k])), 0.0)
@@ -494,13 +501,6 @@
         for sweep in range(SMOOTH):
             head = relaxed(head, 4, fine_ref)
 
-    own = 8 * device + ((lane & 31) >> 2)
-    for j in range(4):
-        row = jnp.take_along_axis(head[4 * j], own, axis=1)
-        for i in range(1, 4):
-            row = jnp.where((lane & 3) == i, jnp.take_along_axis(head[4 * j + i], own, axis=1), row)
-        head_ref[:, j, :] = row[:, 0:32]
-
     largest = None
     for k in range(16):
         here = head[k]
@@ -517,10 +517,13 @@
         largest = speed if largest is None else jnp.maximum(largest, speed)
     step = courant / (jnp.max(largest, axis=(0, 1), keepdims=True) + 1e-06)
 
-    def along(field, x, shift=0):
+    def along(field, x, beside=False):
         halves = []
         for half in range(2):
-            y = jnp.clip(128 * half + lane + shift, 0, 255) >> 2
+            y = 128 * half + lane
+            if beside:
+                y = jnp.clip(y + jnp.where((lane & 3) == 3, 1, jnp.where((lane & 3) == 0, -1, 0)), 0, 255)
+            y = y >> 2
             source = ((y >> 2) << 3) + (x >> 2)
             part = jnp.take_along_axis(wide_ref[field, x & 3], source, axis=1)
             for j in range(1, 4):
@@ -532,8 +535,7 @@
     speed_x = [along(0, x) for x in xs]
     speed_z = [along(2, x) for x in xs[1:3]]
     speed_y = [along(1, x) for x in xs[1:3]]
-    north_y = [along(1, x, 1) for x in xs[1:3]]
-    south_y = [along(1, x, -1) for x in xs[1:3]]
+    beside_y = [along(1, x, True) for x in xs[1:3]]
 
     layer, column = iotas((8, 256))
     crossed = device ^ jnp.where(even, device - 1, device + 1)
@@ -571,8 +573,11 @@
             face = speed_x[1 + f // 4]
         flux_x.append(face * jnp.where(face > 0, cells[f + 1] + halves[f], cells[f + 2] - halves[f + 1]))
     faces_z = [jnp.where(layer < 7, 0.5 * (v + pltpu.roll(v, 7, 0)), 0.0) for v in speed_z]
-    faces_n = [jnp.where(column < 255, 0.5 * (v + beside), 0.0) for v, beside in zip(speed_y, north_y)]
-    faces_s = [jnp.where(column > 0, 0.5 * (beside + v), 0.0) for v, beside in zip(speed_y, south_y)]
+    between = [0.5 * (v + beside) for v, beside in zip(speed_y, beside_y)]
+    faces_n = [jnp.where((column & 3) == 3, b, v) for v, b in zip(speed_y, between)]
+    faces_n = [jnp.where(column < 255, face, 0.0) for face in faces_n]
+    faces_s = [jnp.where((column & 3) == 0, b, v) for v, b in zip(speed_y, between)]
+    faces_s = [jnp.where(column > 0, face, 0.0) for face in faces_s]
     for x in range(8):
         cell = cells[x + 2]
         ahead = jnp.where(layer < 7, pltpu.roll(cell, 7, 0), 0.0) - cell
@@ -593,6 +598,13 @@
         dilution = jnp.where(layer == 0, freshening * wet * cell, 0.0)
         tendency_ref[:, x, :] = -step * change - step * dilution
 
+    own = 8 * device + ((lane & 31) >> 2)
+    for j in range(4):
+        row = jnp.take_along_axis(head[4 * j], own, axis=1)
+        for i in range(1, 4):
+            row = jnp.where((lane & 3) == i, jnp.take_along_axis(head[4 * j + i], own, axis=1), row)
+        head_ref[:, j, :] = row[:, 0:32]
+
 def local_small(salt, recharge, conductivity, codes):
     vmem = pl.BlockSpec(memory_space=pltpu.VMEM)
     block, inner, relay = pl.pallas_call(
@@ -604,7 +616,7 @@
         ),
         in_specs=[vmem] * 4,
         out_specs=(vmem,) * 3,
-        scratch_shapes=[pltpu.VMEM((32, 128), jnp.float32), pltpu.VMEM((32, 128), jnp.float32)],
+        scratch_shapes=[pltpu.VMEM((2, 64, 128), jnp.float32), pltpu.VMEM((32, 128), jnp.float32)],
         name="pack",
     )(salt, recharge, conductivity, codes)
 

time: 18.5 us -> 18.4 us (level)
  no operation moved by 1% of the time
where the time goes in v6:
time: 18.4 us; the launch traced here: 18.3 us
  starting transfers between devices  7.91 us (43%)
  waiting for transfers between devices  6.08 us (33%)
  Pallas kernels  3.55 us (19%)
  between operations  0.69 us (4%)
    ppermute x4, starting transfers between devices, swapped(): return lax.ppermute(array, 'gx', pairs)  7.91 us
    ppermute x4, waiting for transfers between devices, swapped(): return lax.ppermute(array, 'gx', pairs)  6.08 us
    pallas_call x1, Pallas kernels, local_small(): pl.pallas_call(step_kernel, out_shape=(jax.ShapeDtypeStruct(salt.shape, j...  2.5 us
    pallas_call x1, Pallas kernels, local_small(): pl.pallas_call(pack_kernel, out_shape=(pltpu.VMEM((MAIN + SMALL + COLUMNS...  1.05 us
  transfers between devices with their start and end apart: 4, of which 4 were waited for; matrix products, arithmetic and copies ran while one was open for 0% of the time, Pallas kernels for 0%

profile of v6, /device:TPU:0, one launch (start us, length us, event | category | flops | bytes accessed | tf_op | source)
XLA Modules:
  0.0 18.3 jit_solution(9471765447073822325)
XLA Ops:
  0.6 1.1 %pack.1 = (f32[56,128]{1,0:T(8,128)S(1)}, f32[32,128]{1,0:T(8,128)S(1)}, f32[8,128]{1,0:T(8,128)S(1)}) custom-call(f32[8,8,256]{2,1,0:T(8,128)} %salt_ref.3, s32[8,256]{1,0:T(8,128)} %recharge_ref.3, f32[8,4,32]{2,1,0:T(4,128)} %cond_ref.1, s32[4,32]{1,0:T(4,128)} %codes_ref.1), custom_call_target="tpu_custom_call" | custom-call | tf_op jit(solution)/shard_map/pack/pallas_call | solution.py:610
  1.7 3.5 %collective-permute-start = (f32[56,128]{1,0:T(8,128)S(1)}, f32[56,128]{1,0:T(8,128)S(1)}, u32[]{:S(2)}, u32[]{:S(2)}) collective-permute-start(f32[56,128]{1,0:T(8,128)S(1)} %get-tuple-element.5), channel_id=1, source_target_pairs={{0,9},{1,2},{2,1},{3,10},{4,7},{5,12},{6,15},{7,4},{8,11},{9,0},{1... | collective-permute-start | bytes 86024 | tf_op jit(solution)/shard_map/ppermute | solution.py:625
  5.2 1.6 %collective-permute-done.first_ref = f32[56,128]{1,0:T(8,128)S(1)} collective-permute-done((f32[56,128]{1,0:T(8,128)S(1)}, f32[56,128]{1,0:T(8,128)S(1)}, u32[]{:S(2)}, u32[]{:S(2)}) %collective-permute-start) | collective-permute-done | bytes 28704 | tf_op jit(solution)/shard_map/ppermute | solution.py:625
  6.8 1.9 %collective-permute-start.1 = (f32[72,128]{1,0:T(8,128)S(1)}, f32[72,128]{1,0:T(8,128)S(1)}, u32[]{:S(2)}, u32[]{:S(2)}) collective-permute-start(f32[72,128]{1,0:T(8,128)S(1)} %pad_maximum_fusion), channel_id=1, source_target_pairs={{0,3},{1,8},{2,11},{3,0},{4,13},{5,6},{6,5},{7,14},{8,1},{9,10},{1... | collective-permute-start | bytes 110600 | tf_op jit(solution)/shard_map/ppermute | solution.py:625
  8.7 1.6 %collective-permute-done.1.second_ref = f32[72,128]{1,0:T(8,128)S(1)} collective-permute-done((f32[72,128]{1,0:T(8,128)S(1)}, f32[72,128]{1,0:T(8,128)S(1)}, u32[]{:S(2)}, u32[]{:S(2)}) %collective-permute-start.1) | collective-permute-done | bytes 36896 | tf_op jit(solution)/shard_map/ppermute | solution.py:625
  10.3 1.9 %collective-permute-start.2 = (f32[104,128]{1,0:T(8,128)S(1)}, f32[104,128]{1,0:T(8,128)S(1)}, u32[]{:S(2)}, u32[]{:S(2)}) collective-permute-start(f32[104,128]{1,0:T(8,128)S(1)} %get-tuple-element.8), channel_id=1, source_target_pairs={{0,5},{1,4},{2,7},{3,6},{4,1},{5,0},{6,3},{7,2},{8,13},{9,12},{10,... | collective-permute-start | bytes 159752 | tf_op jit(solution)/shard_map/ppermute | solution.py:625
  12.3 1.9 %collective-permute-done.2 = f32[104,128]{1,0:T(8,128)S(1)} collective-permute-done((f32[104,128]{1,0:T(8,128)S(1)}, f32[104,128]{1,0:T(8,128)S(1)}, u32[]{:S(2)}, u32[]{:S(2)}) %collective-permute-start.2) | collective-permute-done | bytes 53280 | tf_op jit(solution)/shard_map/ppermute | solution.py:625
  14.2 0.0 copy-start
  14.2 0.0 copy-start.1
  14.2 0.6 %collective-permute-start.3 = (f32[208,128]{1,0:T(8,128)S(1)}, f32[208,128]{1,0:T(8,128)S(1)}, u32[]{:S(2)}, u32[]{:S(2)}) collective-permute-start(f32[208,128]{1,0:T(8,128)S(1)} %constant_dynamic-update-slice_fusion.5.near_ref), channel_id=1, source_target_pairs={{0,1},{1,0},{2,3},{3,2},{4,5},{5,4},{6,7},{7,6},{8,9},{9,8},{10,11... | collective-permute-start | bytes 319496 | tf_op jit(solution)/shard_map/ppermute | solution.py:625
  14.8 1.0 %collective-permute-done.3.far_ref = f32[208,128]{1,0:T(8,128)S(1)} collective-permute-done((f32[208,128]{1,0:T(8,128)S(1)}, f32[208,128]{1,0:T(8,128)S(1)}, u32[]{:S(2)}, u32[]{:S(2)}) %collective-permute-start.3) | collective-permute-done | bytes 106528 | tf_op jit(solution)/shard_map/ppermute | solution.py:625
  15.8 0.0 copy-done
  15.8 0.0 copy-done.1
  15.8 2.5 %step.1 = (f32[8,8,256]{2,1,0:T(8,128)}, f32[8,4,32]{2,1,0:T(4,128)}) custom-call(f32[208,128]{1,0:T(8,128)S(1)} %constant_dynamic-update-slice_fusion.5.near_ref, f32[208,128]{1,0:T(8,128)S(1)} %collective-permute-done.3.far_ref, f32[56,128]{1,0:T(8,128)S(1)} %collective-permute-done.first_ref, f32[72,128]{1,0:T(8,128)S(1)} %collective-permute-done.1.second_ref, ...), custom_call_target="tpu_custom_call" | custom-call | tf_op jit(solution)/shard_map/step/pallas_call | solution.py:647
  (13 shorter events, 0.1 us)
Async XLA Ops:
  1.7 5.1 %collective-permute-start = (f32[56,128]{1,0:T(8,128)S(1)}, f32[56,128]{1,0:T(8,128)S(1)}, u32[]{:S(2)}, u32[]{:S(2)}) collective-permute-start(f32[56,128]{1,0:T(8,128)S(1)} %get-tuple-element.5), channel_id=1, source_target_pairs={{0,9},{1,2},{2,1},{3,10},{4,7},{5,12},{6,15},{7,4},{8,11},{9,0},{1... | collective-permute-start | bytes 86024 | tf_op jit(solution)/shard_map/ppermute | solution.py:625
  6.8 3.5 %collective-permute-start.1 = (f32[72,128]{1,0:T(8,128)S(1)}, f32[72,128]{1,0:T(8,128)S(1)}, u32[]{:S(2)}, u32[]{:S(2)}) collective-permute-start(f32[72,128]{1,0:T(8,128)S(1)} %pad_maximum_fusion), channel_id=1, source_target_pairs={{0,3},{1,8},{2,11},{3,0},{4,13},{5,6},{6,5},{7,14},{8,1},{9,10},{1... | collective-permute-start | bytes 110600 | tf_op jit(solution)/shard_map/ppermute | solution.py:625
  10.3 3.8 %collective-permute-start.2 = (f32[104,128]{1,0:T(8,128)S(1)}, f32[104,128]{1,0:T(8,128)S(1)}, u32[]{:S(2)}, u32[]{:S(2)}) collective-permute-start(f32[104,128]{1,0:T(8,128)S(1)} %get-tuple-element.8), channel_id=1, source_target_pairs={{0,5},{1,4},{2,7},{3,6},{4,1},{5,0},{6,3},{7,2},{8,13},{9,12},{10,... | collective-permute-start | bytes 159752 | tf_op jit(solution)/shard_map/ppermute | solution.py:625
  14.2 1.6 %copy-start = (f32[8,8,256]{2,1,0:T(8,128)S(1)}, f32[8,8,256]{2,1,0:T(8,128)}, u32[]{:S(2)}) copy-start(f32[8,8,256]{2,1,0:T(8,128)} %salt_ref.3) | copy-start | bytes 196612
  14.2 1.6 %copy-start.1 = (s32[8,256]{1,0:T(8,128)S(1)}, s32[8,256]{1,0:T(8,128)}, u32[]{:S(2)}) copy-start(s32[8,256]{1,0:T(8,128)} %recharge_ref.3) | copy-start | bytes 24580
  14.2 1.5 %collective-permute-start.3 = (f32[208,128]{1,0:T(8,128)S(1)}, f32[208,128]{1,0:T(8,128)S(1)}, u32[]{:S(2)}, u32[]{:S(2)}) collective-permute-start(f32[208,128]{1,0:T(8,128)S(1)} %constant_dynamic-update-slice_fusion.5.near_ref), channel_id=1, source_target_pairs={{0,1},{1,0},{2,3},{3,2},{4,5},{5,4},{6,7},{7,6},{8,9},{9,8},{10,11... | collective-permute-start | bytes 319496 | tf_op jit(solution)/shard_map/ppermute | solution.py:625

commit v7 on v6

--- a/solution.py
+++ b/solution.py
@@ -412,21 +412,29 @@
             weights.append(weight)
         return (face_w, face_e, face_s, face_n, face_d), weights
 
-    def relaxed(cells, side, weight_ref):
+    def step(here, west, east, south, north, weights):
+        pairs = (west, east, south, north, upper_of(here), lower_of(here))
+        terms = [weights(number) * pair for number, pair in enumerate(pairs)]
+        base = (1.0 - relax_weight) * here + weights(8)
+        return ((terms[0] + terms[1]) + (terms[2] + terms[3])) + ((terms[4] + terms[5]) + base)
+
+    def edges_of(cells):
+        return (
+            [pltpu.roll(cells[4 * j + 3], 1, 1) for j in range(4)],
+            [pltpu.roll(cells[4 * j], 127, 1) for j in range(4)],
+            [pltpu.roll(cells[12 + i], 8, 1) for i in range(4)],
+            [pltpu.roll(cells[i], 120, 1) for i in range(4)],
+        )
+
+    def relaxed(cells, edges):
         out = []
-        for k in range(side * side):
-            here = cells[k]
-            pairs = (
-                west_of(cells, k, side),
-                east_of(cells, k, side),
-                south_of(cells, k, side),
-                north_of(cells, k, side),
-                upper_of(here),
-                lower_of(here),
-            )
-            terms = [weight_ref[number, k] * pair for number, pair in enumerate(pairs)]
-            base = (1.0 - relax_weight) * here + weight_ref[8, k]
-            out.append(((terms[0] + terms[1]) + (terms[2] + terms[3])) + ((terms[4] + terms[5]) + base))
+        for k in range(16):
+            j, i = k // 4, k % 4
+            west = cells[k - 1] if i > 0 else edges[0][j]
+            east = cells[k + 1] if i < 3 else edges[1][j]
+            south = cells[k - 4] if j > 0 else edges[2][i]
+            north = cells[k + 4] if j < 3 else edges[3][i]
+            out.append(step(cells[k], west, east, south, north, lambda number, k=k: fine_ref[number, k]))
         return out
 
     ring = [(j, i) for j in range(-1, 3) for i in range(-1, 3) if (j in (0, 1)) != (i in (0, 1))]
@@ -436,27 +444,27 @@
         cell = cells[2 * (j % 2) + i % 2]
         return pltpu.roll(cell, shift, 1) if shift else cell
 
-    def relaxed_twice(cells):
-        def step(at, j, i, weights):
-            here = at(j, i)
-            pairs = (at(j, i - 1), at(j, i + 1), at(j - 1, i), at(j + 1, i), upper_of(here), lower_of(here))
-            terms = [weights(number) * pair for number, pair in enumerate(pairs)]
-            base = (1.0 - relax_weight) * here + weights(8)
-            return ((terms[0] + terms[1]) + (terms[2] + terms[3])) + ((terms[4] + terms[5]) + base)
-
+    def relaxed_around(cells):
         old, new = {}, {}
 
-        def at_old(j, i):
+        def at(j, i):
             if (j, i) not in old:
                 old[j, i] = beyond(cells, j, i)
             return old[j, i]
 
-        for q, (j, i) in enumerate(ring):
-            new[j, i] = step(at_old, j, i, lambda number, q=q: ring_ref[number, q])
-        for k in range(4):
-            new[k // 2, k % 2] = step(at_old, k // 2, k % 2, lambda number, k=k: coarse_ref[number, k])
+        for j, i in ring + [(0, 0), (0, 1), (1, 0), (1, 1)]:
+            if (j, i) in ring:
+                weights = lambda number, q=ring.index((j, i)): ring_ref[number, q]
+            else:
+                weights = lambda number, k=2 * j + i: coarse_ref[number, k]
+            new[j, i] = step(at(j, i), at(j, i - 1), at(j, i + 1), at(j - 1, i), at(j + 1, i), weights)
+        return new
+
+    def relaxed_within(new):
         return [
-            step(lambda j, i: new[j, i], k // 2, k % 2, lambda number, k=k: coarse_ref[number, k]) for k in range(4)
+            step(new[j, i], new[j, i - 1], new[j, i + 1], new[j - 1, i], new[j + 1, i],
+                 lambda number, k=2 * j + i: coarse_ref[number, k])
+            for j in range(2) for i in range(2)
         ]
 
     def pair_sums(cells):
@@ -484,8 +492,9 @@
     head = None
     for cycle_no in range(CYCLES):
         for sweep in range(SMOOTH):
-            head = [fine_ref[8, k] for k in range(16)] if head is None else relaxed(head, 4, fine_ref)
-        ahead = relaxed(head, 4, fine_ref)
+            head = [fine_ref[8, k] for k in range(16)] if head is None else relaxed(head, edges_of(head))
+        edges = edges_of(head)
+        ahead = relaxed(head, edges)
         resid = pair_sums([(ahead[k] - head[k]) * fine_ref[6, k] for k in range(16)])
         correction = []
         for k in range(4):
@@ -493,13 +502,27 @@
             coarse_ref[8, k] = correction[k]
         for q, (j, i) in enumerate(ring):
             ring_ref[8, q] = beyond(correction, j, i)
-        for sweep in range((COARSE_SWEEPS - 1) // 2):
-            correction = relaxed_twice(correction)
-        for sweep in range((COARSE_SWEEPS - 1) % 2):
-            correction = relaxed(correction, 2, coarse_ref)
+        sweeps = COARSE_SWEEPS - 1
+        while sweeps > 0:
+            around = relaxed_around(correction)
+            correction = [around[k // 2, k % 2] for k in range(4)]
+            sweeps -= 1
+            if sweeps > 0:
+                correction = relaxed_within(around)
+                around = None
+                sweeps -= 1
+        if around is None:
+            around = {place: beyond(correction, *place) for place in ring}
         head = [head[k] + correction[2 * (k // 8) + (k % 4) // 2] for k in range(16)]
+        edges = (
+            [edges[0][n] + around[n // 2, -1] for n in range(4)],
+            [edges[1][n] + around[n // 2, 2] for n in range(4)],
+            [edges[2][n] + around[-1, n // 2] for n in range(4)],
+            [edges[3][n] + around[2, n // 2] for n in range(4)],
+        )
         for sweep in range(SMOOTH):
-            head = relaxed(head, 4, fine_ref)
+            head = relaxed(head, edges_of(head) if edges is None else edges)
+            edges = None
 
     largest = None
     for k in range(16):

time: 18.4 us -> 18.4 us (level)
  no operation moved by 1% of the time
where the time goes in v7:
time: 18.4 us; the launch traced here: 18.2 us
  starting transfers between devices  7.91 us (43%)
  waiting for transfers between devices  6.08 us (33%)
  Pallas kernels  3.47 us (19%)
  between operations  0.69 us (4%)
    ppermute x4, starting transfers between devices, swapped(): return lax.ppermute(array, 'gx', pairs)  7.91 us
    ppermute x4, waiting for transfers between devices, swapped(): return lax.ppermute(array, 'gx', pairs)  6.08 us
    pallas_call x1, Pallas kernels, local_small(): pl.pallas_call(step_kernel, out_shape=(jax.ShapeDtypeStruct(salt.shape, j...  2.41 us
    pallas_call x1, Pallas kernels, local_small(): pl.pallas_call(pack_kernel, out_shape=(pltpu.VMEM((MAIN + SMALL + COLUMNS...  1.05 us
  transfers between devices with their start and end apart: 4, of which 4 were waited for; matrix products, arithmetic and copies ran while one was open for 0% of the time, Pallas kernels for 0%

profile of v7, /device:TPU:0, one launch (start us, length us, event | category | flops | bytes accessed | tf_op | source)
XLA Modules:
  0.0 18.2 jit_solution(17783892267623126889)
XLA Ops:
  0.6 1.1 %pack.1 = (f32[56,128]{1,0:T(8,128)S(1)}, f32[32,128]{1,0:T(8,128)S(1)}, f32[8,128]{1,0:T(8,128)S(1)}) custom-call(f32[8,8,256]{2,1,0:T(8,128)} %salt_ref.3, s32[8,256]{1,0:T(8,128)} %recharge_ref.3, f32[8,4,32]{2,1,0:T(4,128)} %cond_ref.1, s32[4,32]{1,0:T(4,128)} %codes_ref.1), custom_call_target="tpu_custom_call" | custom-call | tf_op jit(solution)/shard_map/pack/pallas_call | solution.py:633
  1.7 3.5 %collective-permute-start = (f32[56,128]{1,0:T(8,128)S(1)}, f32[56,128]{1,0:T(8,128)S(1)}, u32[]{:S(2)}, u32[]{:S(2)}) collective-permute-start(f32[56,128]{1,0:T(8,128)S(1)} %get-tuple-element.5), channel_id=1, source_target_pairs={{0,9},{1,2},{2,1},{3,10},{4,7},{5,12},{6,15},{7,4},{8,11},{9,0},{1... | collective-permute-start | bytes 86024 | tf_op jit(solution)/shard_map/ppermute | solution.py:648
  5.2 1.6 %collective-permute-done.first_ref = f32[56,128]{1,0:T(8,128)S(1)} collective-permute-done((f32[56,128]{1,0:T(8,128)S(1)}, f32[56,128]{1,0:T(8,128)S(1)}, u32[]{:S(2)}, u32[]{:S(2)}) %collective-permute-start) | collective-permute-done | bytes 28704 | tf_op jit(solution)/shard_map/ppermute | solution.py:648
  6.8 1.9 %collective-permute-start.1 = (f32[72,128]{1,0:T(8,128)S(1)}, f32[72,128]{1,0:T(8,128)S(1)}, u32[]{:S(2)}, u32[]{:S(2)}) collective-permute-start(f32[72,128]{1,0:T(8,128)S(1)} %pad_maximum_fusion), channel_id=1, source_target_pairs={{0,3},{1,8},{2,11},{3,0},{4,13},{5,6},{6,5},{7,14},{8,1},{9,10},{1... | collective-permute-start | bytes 110600 | tf_op jit(solution)/shard_map/ppermute | solution.py:648
  8.7 1.6 %collective-permute-done.1.second_ref = f32[72,128]{1,0:T(8,128)S(1)} collective-permute-done((f32[72,128]{1,0:T(8,128)S(1)}, f32[72,128]{1,0:T(8,128)S(1)}, u32[]{:S(2)}, u32[]{:S(2)}) %collective-permute-start.1) | collective-permute-done | bytes 36896 | tf_op jit(solution)/shard_map/ppermute | solution.py:648
  10.3 1.9 %collective-permute-start.2 = (f32[104,128]{1,0:T(8,128)S(1)}, f32[104,128]{1,0:T(8,128)S(1)}, u32[]{:S(2)}, u32[]{:S(2)}) collective-permute-start(f32[104,128]{1,0:T(8,128)S(1)} %get-tuple-element.8), channel_id=1, source_target_pairs={{0,5},{1,4},{2,7},{3,6},{4,1},{5,0},{6,3},{7,2},{8,13},{9,12},{10,... | collective-permute-start | bytes 159752 | tf_op jit(solution)/shard_map/ppermute | solution.py:648
  12.3 1.9 %collective-permute-done.2 = f32[104,128]{1,0:T(8,128)S(1)} collective-permute-done((f32[104,128]{1,0:T(8,128)S(1)}, f32[104,128]{1,0:T(8,128)S(1)}, u32[]{:S(2)}, u32[]{:S(2)}) %collective-permute-start.2) | collective-permute-done | bytes 53280 | tf_op jit(solution)/shard_map/ppermute | solution.py:648
  14.2 0.0 copy-start
  14.2 0.0 copy-start.1
  14.2 0.6 %collective-permute-start.3 = (f32[208,128]{1,0:T(8,128)S(1)}, f32[208,128]{1,0:T(8,128)S(1)}, u32[]{:S(2)}, u32[]{:S(2)}) collective-permute-start(f32[208,128]{1,0:T(8,128)S(1)} %constant_dynamic-update-slice_fusion.5.near_ref), channel_id=1, source_target_pairs={{0,1},{1,0},{2,3},{3,2},{4,5},{5,4},{6,7},{7,6},{8,9},{9,8},{10,11... | collective-permute-start | bytes 319496 | tf_op jit(solution)/shard_map/ppermute | solution.py:648
  14.8 1.0 %collective-permute-done.3.far_ref = f32[208,128]{1,0:T(8,128)S(1)} collective-permute-done((f32[208,128]{1,0:T(8,128)S(1)}, f32[208,128]{1,0:T(8,128)S(1)}, u32[]{:S(2)}, u32[]{:S(2)}) %collective-permute-start.3) | collective-permute-done | bytes 106528 | tf_op jit(solution)/shard_map/ppermute | solution.py:648
  15.8 0.0 copy-done
  15.8 0.0 copy-done.1
  15.8 2.4 %step.1 = (f32[8,8,256]{2,1,0:T(8,128)}, f32[8,4,32]{2,1,0:T(4,128)}) custom-call(f32[208,128]{1,0:T(8,128)S(1)} %constant_dynamic-update-slice_fusion.5.near_ref, f32[208,128]{1,0:T(8,128)S(1)} %collective-permute-done.3.far_ref, f32[56,128]{1,0:T(8,128)S(1)} %collective-permute-done.first_ref, f32[72,128]{1,0:T(8,128)S(1)} %collective-permute-done.1.second_ref, ...), custom_call_target="tpu_custom_call" | custom-call | tf_op jit(solution)/shard_map/step/pallas_call | solution.py:670
  (13 shorter events, 0.1 us)
Async XLA Ops:
  1.7 5.1 %collective-permute-start = (f32[56,128]{1,0:T(8,128)S(1)}, f32[56,128]{1,0:T(8,128)S(1)}, u32[]{:S(2)}, u32[]{:S(2)}) collective-permute-start(f32[56,128]{1,0:T(8,128)S(1)} %get-tuple-element.5), channel_id=1, source_target_pairs={{0,9},{1,2},{2,1},{3,10},{4,7},{5,12},{6,15},{7,4},{8,11},{9,0},{1... | collective-permute-start | bytes 86024 | tf_op jit(solution)/shard_map/ppermute | solution.py:648
  6.8 3.5 %collective-permute-start.1 = (f32[72,128]{1,0:T(8,128)S(1)}, f32[72,128]{1,0:T(8,128)S(1)}, u32[]{:S(2)}, u32[]{:S(2)}) collective-permute-start(f32[72,128]{1,0:T(8,128)S(1)} %pad_maximum_fusion), channel_id=1, source_target_pairs={{0,3},{1,8},{2,11},{3,0},{4,13},{5,6},{6,5},{7,14},{8,1},{9,10},{1... | collective-permute-start | bytes 110600 | tf_op jit(solution)/shard_map/ppermute | solution.py:648
  10.3 3.8 %collective-permute-start.2 = (f32[104,128]{1,0:T(8,128)S(1)}, f32[104,128]{1,0:T(8,128)S(1)}, u32[]{:S(2)}, u32[]{:S(2)}) collective-permute-start(f32[104,128]{1,0:T(8,128)S(1)} %get-tuple-element.8), channel_id=1, source_target_pairs={{0,5},{1,4},{2,7},{3,6},{4,1},{5,0},{6,3},{7,2},{8,13},{9,12},{10,... | collective-permute-start | bytes 159752 | tf_op jit(solution)/shard_map/ppermute | solution.py:648
  14.2 1.6 %copy-start = (f32[8,8,256]{2,1,0:T(8,128)S(1)}, f32[8,8,256]{2,1,0:T(8,128)}, u32[]{:S(2)}) copy-start(f32[8,8,256]{2,1,0:T(8,128)} %salt_ref.3) | copy-start | bytes 196612
  14.2 1.6 %copy-start.1 = (s32[8,256]{1,0:T(8,128)S(1)}, s32[8,256]{1,0:T(8,128)}, u32[]{:S(2)}) copy-start(s32[8,256]{1,0:T(8,128)} %recharge_ref.3) | copy-start | bytes 24580
  14.2 1.5 %collective-permute-start.3 = (f32[208,128]{1,0:T(8,128)S(1)}, f32[208,128]{1,0:T(8,128)S(1)}, u32[]{:S(2)}, u32[]{:S(2)}) collective-permute-start(f32[208,128]{1,0:T(8,128)S(1)} %constant_dynamic-update-slice_fusion.5.near_ref), channel_id=1, source_target_pairs={{0,1},{1,0},{2,3},{3,2},{4,5},{5,4},{6,7},{7,6},{8,9},{9,8},{10,11... | collective-permute-start | bytes 319496 | tf_op jit(solution)/shard_map/ppermute | solution.py:648

commit v8 on v7

--- a/solution.py
+++ b/solution.py
@@ -238,7 +238,8 @@
 def odd_ones(device):
     return ((device ^ (device >> 1) ^ (device >> 2) ^ (device >> 3)) & 1) == 1
 
-def pack_kernel(salt_ref, recharge_ref, cond_ref, codes_ref, block_ref, inner_ref, relay_ref, flat_ref, turn_ref):
+def pack_kernel(salt_ref, recharge_ref, cond_ref, codes_ref, block_ref, inner_ref, relay_ref, kept_ref, flat_ref, turn_ref):
+    kept_ref[...] = salt_ref[...]
     device = lax.axis_index("gx")
     even = (device & 1) == 0
     for j in range(2):
@@ -311,8 +312,28 @@
 def lower_of(cell):
     return pltpu.roll(cell, 7, 0)
 
+def sides_kernel(salt_ref, side_ref):
+    layer, column = iotas((8, 256))
+    cells = [salt_ref[:, x, :] for x in range(8)]
+    for x in range(8):
+        cell = cells[x]
+        ahead = jnp.where(layer < 7, lower_of(cell), 0.0) - cell
+        half = 0.5 * slope_of(jnp.where(layer > 0, upper_of(ahead), cell), ahead)
+        side_ref[0, x] = cell + half
+        side_ref[1, x] = lower_of(cell - half)
+        ahead = jnp.where(column < 255, pltpu.roll(cell, 255, 1), 0.0) - cell
+        half = 0.5 * slope_of(jnp.where(column > 0, pltpu.roll(ahead, 1, 1), cell), ahead)
+        side_ref[2, x] = cell + half
+        side_ref[3, x] = pltpu.roll(cell - half, 255, 1)
+        side_ref[4, x] = pltpu.roll(cell + half, 1, 1)
+        side_ref[5, x] = cell - half
+        if 0 < x < 7:
+            half = 0.5 * slope_of(cell - cells[x - 1], cells[x + 1] - cell)
+            side_ref[6, x] = cell + half
+            side_ref[7, x] = cell - half
+
 def step_kernel(
-    near_ref, far_ref, first_ref, second_ref, salt_ref, recharge_ref, tendency_ref, head_ref, fine_ref, coarse_ref, ring_ref, wide_ref
+    near_ref, far_ref, first_ref, second_ref, side_ref, salt_ref, recharge_ref, tendency_ref, head_ref, fine_ref, coarse_ref, ring_ref, wide_ref
 ):
     device = lax.axis_index("gx")
     sub, lane = iotas((8, 128))
@@ -582,8 +603,13 @@
         + [salt_ref[:, x, :] for x in range(8)]
         + [jnp.where(even, halo[2 + j], halo[j]) for j in range(2)]
     )
-    diffs = [cells[i + 1] - cells[i] for i in range(11)]
-    halves = [0.5 * slope_of(diffs[i], diffs[i + 1]) for i in range(10)]
+    lower, upper = {}, {}
+    for x in (-1, 0, 7, 8):
+        cell = cells[x + 2]
+        half = 0.5 * slope_of(cell - cells[x + 1], cells[x + 3] - cell)
+        lower[x], upper[x] = cell + half, cell - half
+    for x in range(1, 7):
+        lower[x], upper[x] = side_ref[6, x], side_ref[7, x]
     flux_x = []
     for f in range(9):
         if f % 4 == 0:
@@ -594,7 +620,7 @@
                 face = jnp.where(device == 15, 0.0, face)
         else:
             face = speed_x[1 + f // 4]
-        flux_x.append(face * jnp.where(face > 0, cells[f + 1] + halves[f], cells[f + 2] - halves[f + 1]))
+        flux_x.append(face * jnp.where(face > 0, lower[f - 1], upper[f]))
     faces_z = [jnp.where(layer < 7, 0.5 * (v + pltpu.roll(v, 7, 0)), 0.0) for v in speed_z]
     between = [0.5 * (v + beside) for v, beside in zip(speed_y, beside_y)]
     faces_n = [jnp.where((column & 3) == 3, b, v) for v, b in zip(speed_y, between)]
@@ -602,23 +628,17 @@
     faces_s = [jnp.where((column & 3) == 0, b, v) for v, b in zip(speed_y, between)]
     faces_s = [jnp.where(column > 0, face, 0.0) for face in faces_s]
     for x in range(8):
-        cell = cells[x + 2]
-        ahead = jnp.where(layer < 7, pltpu.roll(cell, 7, 0), 0.0) - cell
-        half = 0.5 * slope_of(jnp.where(layer > 0, pltpu.roll(ahead, 1, 0), cell), ahead)
         face = faces_z[x // 4]
-        flux_z = face * jnp.where(face > 0, cell + half, pltpu.roll(cell - half, 7, 0))
-        change = flux_z - pltpu.roll(flux_z, 1, 0)
+        flux_z = face * jnp.where(face > 0, side_ref[0, x], side_ref[1, x])
+        change = flux_z - upper_of(flux_z)
         change = change + (flux_x[x + 1] - flux_x[x])
-        ahead = jnp.where(column < 255, pltpu.roll(cell, 255, 1), 0.0) - cell
-        half = 0.5 * slope_of(jnp.where(column > 0, pltpu.roll(ahead, 1, 1), cell), ahead)
-        below, above = cell + half, cell - half
         face = faces_n[x // 4]
-        flux_n = face * jnp.where(face > 0, below, pltpu.roll(above, 255, 1))
+        flux_n = face * jnp.where(face > 0, side_ref[2, x], side_ref[3, x])
         face = faces_s[x // 4]
-        flux_s = face * jnp.where(face > 0, pltpu.roll(below, 1, 1), above)
+        flux_s = face * jnp.where(face > 0, side_ref[4, x], side_ref[5, x])
         change = change + (flux_n - flux_s)
         wet = recharge_ref[x : x + 1, :].astype(jnp.float32)
-        dilution = jnp.where(layer == 0, freshening * wet * cell, 0.0)
+        dilution = jnp.where(layer == 0, freshening * wet * cells[x + 2], 0.0)
         tendency_ref[:, x, :] = -step * change - step * dilution
 
     own = 8 * device + ((lane & 31) >> 2)
@@ -630,15 +650,16 @@
 
 def local_small(salt, recharge, conductivity, codes):
     vmem = pl.BlockSpec(memory_space=pltpu.VMEM)
-    block, inner, relay = pl.pallas_call(
+    block, inner, relay, kept = pl.pallas_call(
         pack_kernel,
         out_shape=(
             pltpu.VMEM((MAIN + SMALL + COLUMNS, 128), jnp.float32),
             pltpu.VMEM((COLUMNS, 128), jnp.float32),
             pltpu.VMEM((8, 128), jnp.float32),
+            pltpu.VMEM(salt.shape, jnp.float32),
         ),
         in_specs=[vmem] * 4,
-        out_specs=(vmem,) * 3,
+        out_specs=(vmem,) * 4,
         scratch_shapes=[pltpu.VMEM((2, 64, 128), jnp.float32), pltpu.VMEM((32, 128), jnp.float32)],
         name="pack",
     )(salt, recharge, conductivity, codes)
@@ -667,13 +688,21 @@
         [block[: 4 * MAIN], other[: 4 * MAIN], small(block, 4), small(other, 4), columns(other, 4), inner]
     )
     other = swapped(block, 3)
+    sides = pl.pallas_call(
+        sides_kernel,
+        out_shape=pltpu.VMEM((8, 8, 8, 256), jnp.float32),
+        in_specs=[vmem],
+        out_specs=vmem,
+        cost_estimate=pl.CostEstimate(flops=1 << 20, bytes_accessed=1 << 20, transcendentals=0),
+        name="sides",
+    )(pltpu.with_memory_space_constraint(kept, pltpu.VMEM))
     return pl.pallas_call(
         step_kernel,
         out_shape=(
             jax.ShapeDtypeStruct(salt.shape, jnp.float32),
             jax.ShapeDtypeStruct(conductivity.shape, jnp.float32),
         ),
-        in_specs=[vmem] * 6,
+        in_specs=[vmem] * 7,
         out_specs=(vmem,) * 2,
         scratch_shapes=[
             pltpu.VMEM((15, 16, 8, 128), jnp.float32),
@@ -683,7 +712,7 @@
         ],
         compiler_params=pltpu.CompilerParams(vmem_limit_bytes=16 * 1024 * 1024),
         name="step",
-    )(block, other, first, second, salt, recharge)
+    )(block, other, first, second, sides, kept, recharge)
 
 def local(salt, recharge, conductivity, codes):
     small = (

time: 18.4 us -> 18.3 us (level)
  waiting for transfers between devices: 6.08 us -> 5.73 us
  Pallas kernels: 3.47 us -> 3.74 us
    ppermute x4, waiting for transfers between devices: 6.08 us -> 5.73 us  [swapped(): return lax.ppermute(array, 'gx', pairs)]
    pallas_call x0 -> x1, Pallas kernels: none -> 0.35 us  [local_small(): pl.pallas_call(sides_kernel, out_shape=pltpu.VMEM((8, 8, 8, 256), jnp.flo...]
  transfers between devices with their start and end apart: 4 -> 4, of which waited for: 4 -> 4; matrix products, arithmetic and copies ran while one was open for 0% -> 0% of each run, Pallas kernels for 0% -> 2%
where the time goes in v8:
time: 18.3 us; the launch traced here: 18.1 us
  starting transfers between devices  7.91 us (43%)
  waiting for transfers between devices  5.73 us (31%)
  Pallas kernels  3.74 us (20%)
  between operations  0.68 us (4%)
    ppermute x4, starting transfers between devices, swapped(): return lax.ppermute(array, 'gx', pairs)  7.91 us
    ppermute x4, waiting for transfers between devices, swapped(): return lax.ppermute(array, 'gx', pairs)  5.73 us
    pallas_call x1, Pallas kernels, local_small(): pl.pallas_call(step_kernel, out_shape=(jax.ShapeDtypeStruct(salt.shape, j...  2.33 us
    pallas_call x1, Pallas kernels, local_small(): pl.pallas_call(pack_kernel, out_shape=(pltpu.VMEM((MAIN + SMALL + COLUMNS...  1.06 us
  transfers between devices with their start and end apart: 4, of which 4 were waited for; matrix products, arithmetic and copies ran while one was open for 0% of the time, Pallas kernels for 2%

profile of v8, /device:TPU:0, one launch (start us, length us, event | category | flops | bytes accessed | tf_op | source)
XLA Modules:
  0.0 18.1 jit_solution(16308545699989551869)
XLA Ops:
  0.6 1.1 %pack.1 = (f32[56,128]{1,0:T(8,128)S(1)}, f32[32,128]{1,0:T(8,128)S(1)}, f32[8,128]{1,0:T(8,128)S(1)}, f32[8,8,256]{2,1,0:T(8,128)S(1)}) custom-call(f32[8,8,256]{2,1,0:T(8,128)} %salt_ref.1, s32[8,256]{1,0:T(8,128)} %recharge_ref.3, f32[8,4,32]{2,1,0:T(4,128)} %cond_ref.1, s32[4,32]{1,0:T(4,128)} %codes_ref.1), custom_call_target="tpu_custom_call" | custom-call | tf_op jit(solution)/shard_map/pack/pallas_call | solution.py:653
  1.7 3.5 %collective-permute-start = (f32[56,128]{1,0:T(8,128)S(1)}, f32[56,128]{1,0:T(8,128)S(1)}, u32[]{:S(2)}, u32[]{:S(2)}) collective-permute-start(f32[56,128]{1,0:T(8,128)S(1)} %get-tuple-element.6), channel_id=1, source_target_pairs={{0,9},{1,2},{2,1},{3,10},{4,7},{5,12},{6,15},{7,4},{8,11},{9,0},{1... | collective-permute-start | bytes 86024 | tf_op jit(solution)/shard_map/ppermute | solution.py:669
  5.2 1.6 %collective-permute-done.first_ref = f32[56,128]{1,0:T(8,128)S(1)} collective-permute-done((f32[56,128]{1,0:T(8,128)S(1)}, f32[56,128]{1,0:T(8,128)S(1)}, u32[]{:S(2)}, u32[]{:S(2)}) %collective-permute-start) | collective-permute-done | bytes 28704 | tf_op jit(solution)/shard_map/ppermute | solution.py:669
  6.8 1.9 %collective-permute-start.1 = (f32[72,128]{1,0:T(8,128)S(1)}, f32[72,128]{1,0:T(8,128)S(1)}, u32[]{:S(2)}, u32[]{:S(2)}) collective-permute-start(f32[72,128]{1,0:T(8,128)S(1)} %pad_maximum_fusion), channel_id=1, source_target_pairs={{0,3},{1,8},{2,11},{3,0},{4,13},{5,6},{6,5},{7,14},{8,1},{9,10},{1... | collective-permute-start | bytes 110600 | tf_op jit(solution)/shard_map/ppermute | solution.py:669
  8.7 1.6 %collective-permute-done.1.second_ref = f32[72,128]{1,0:T(8,128)S(1)} collective-permute-done((f32[72,128]{1,0:T(8,128)S(1)}, f32[72,128]{1,0:T(8,128)S(1)}, u32[]{:S(2)}, u32[]{:S(2)}) %collective-permute-start.1) | collective-permute-done | bytes 36896 | tf_op jit(solution)/shard_map/ppermute | solution.py:669
  10.3 1.9 %collective-permute-start.2 = (f32[104,128]{1,0:T(8,128)S(1)}, f32[104,128]{1,0:T(8,128)S(1)}, u32[]{:S(2)}, u32[]{:S(2)}) collective-permute-start(f32[104,128]{1,0:T(8,128)S(1)} %get-tuple-element.10), channel_id=1, source_target_pairs={{0,5},{1,4},{2,7},{3,6},{4,1},{5,0},{6,3},{7,2},{8,13},{9,12},{10,... | collective-permute-start | bytes 159752 | tf_op jit(solution)/shard_map/ppermute | solution.py:669
  12.3 1.9 %collective-permute-done.2 = f32[104,128]{1,0:T(8,128)S(1)} collective-permute-done((f32[104,128]{1,0:T(8,128)S(1)}, f32[104,128]{1,0:T(8,128)S(1)}, u32[]{:S(2)}, u32[]{:S(2)}) %collective-permute-start.2) | collective-permute-done | bytes 53280 | tf_op jit(solution)/shard_map/ppermute | solution.py:669
  14.2 0.6 %collective-permute-start.3 = (f32[208,128]{1,0:T(8,128)S(1)}, f32[208,128]{1,0:T(8,128)S(1)}, u32[]{:S(2)}, u32[]{:S(2)}) collective-permute-start(f32[208,128]{1,0:T(8,128)S(1)} %constant_dynamic-update-slice_fusion.5.near_ref), channel_id=1, source_target_pairs={{0,1},{1,0},{2,3},{3,2},{4,5},{5,4},{6,7},{7,6},{8,9},{9,8},{10,11... | collective-permute-start | bytes 319496 | tf_op jit(solution)/shard_map/ppermute | solution.py:669
  14.8 0.0 copy-start
  14.8 0.3 %sides.1.side_ref = f32[8,8,8,256]{3,2,1,0:T(8,128)S(1)} custom-call(f32[8,8,256]{2,1,0:T(8,128)S(1)} %get-tuple-element.9.salt_ref), custom_call_target="tpu_custom_call" | custom-call | flops 1048576 | bytes 1048576 | tf_op jit(solution)/shard_map/sides/pallas_call | solution.py:691
  15.2 0.6 %collective-permute-done.3.far_ref = f32[208,128]{1,0:T(8,128)S(1)} collective-permute-done((f32[208,128]{1,0:T(8,128)S(1)}, f32[208,128]{1,0:T(8,128)S(1)}, u32[]{:S(2)}, u32[]{:S(2)}) %collective-permute-start.3) | collective-permute-done | bytes 106528 | tf_op jit(solution)/shard_map/ppermute | solution.py:669
  15.8 0.0 copy-done
  15.8 2.3 %step.1 = (f32[8,8,256]{2,1,0:T(8,128)}, f32[8,4,32]{2,1,0:T(4,128)}) custom-call(f32[208,128]{1,0:T(8,128)S(1)} %constant_dynamic-update-slice_fusion.5.near_ref, f32[208,128]{1,0:T(8,128)S(1)} %collective-permute-done.3.far_ref, f32[56,128]{1,0:T(8,128)S(1)} %collective-permute-done.first_ref, f32[72,128]{1,0:T(8,128)S(1)} %collective-permute-done.1.second_ref, ...), custom_call_target="tpu_custom_call" | custom-call | tf_op jit(solution)/shard_map/step/pallas_call | solution.py:699
  (13 shorter events, 0.0 us)
Async XLA Ops:
  1.7 5.1 %collective-permute-start = (f32[56,128]{1,0:T(8,128)S(1)}, f32[56,128]{1,0:T(8,128)S(1)}, u32[]{:S(2)}, u32[]{:S(2)}) collective-permute-start(f32[56,128]{1,0:T(8,128)S(1)} %get-tuple-element.6), channel_id=1, source_target_pairs={{0,9},{1,2},{2,1},{3,10},{4,7},{5,12},{6,15},{7,4},{8,11},{9,0},{1... | collective-permute-start | bytes 86024 | tf_op jit(solution)/shard_map/ppermute | solution.py:669
  6.8 3.5 %collective-permute-start.1 = (f32[72,128]{1,0:T(8,128)S(1)}, f32[72,128]{1,0:T(8,128)S(1)}, u32[]{:S(2)}, u32[]{:S(2)}) collective-permute-start(f32[72,128]{1,0:T(8,128)S(1)} %pad_maximum_fusion), channel_id=1, source_target_pairs={{0,3},{1,8},{2,11},{3,0},{4,13},{5,6},{6,5},{7,14},{8,1},{9,10},{1... | collective-permute-start | bytes 110600 | tf_op jit(solution)/shard_map/ppermute | solution.py:669
  10.3 3.8 %collective-permute-start.2 = (f32[104,128]{1,0:T(8,128)S(1)}, f32[104,128]{1,0:T(8,128)S(1)}, u32[]{:S(2)}, u32[]{:S(2)}) collective-permute-start(f32[104,128]{1,0:T(8,128)S(1)} %get-tuple-element.10), channel_id=1, source_target_pairs={{0,5},{1,4},{2,7},{3,6},{4,1},{5,0},{6,3},{7,2},{8,13},{9,12},{10,... | collective-permute-start | bytes 159752 | tf_op jit(solution)/shard_map/ppermute | solution.py:669
  14.2 1.6 %collective-permute-start.3 = (f32[208,128]{1,0:T(8,128)S(1)}, f32[208,128]{1,0:T(8,128)S(1)}, u32[]{:S(2)}, u32[]{:S(2)}) collective-permute-start(f32[208,128]{1,0:T(8,128)S(1)} %constant_dynamic-update-slice_fusion.5.near_ref), channel_id=1, source_target_pairs={{0,1},{1,0},{2,3},{3,2},{4,5},{5,4},{6,7},{7,6},{8,9},{9,8},{10,11... | collective-permute-start | bytes 319496 | tf_op jit(solution)/shard_map/ppermute | solution.py:669
  14.8 1.0 %copy-start = (s32[8,256]{1,0:T(8,128)S(1)}, s32[8,256]{1,0:T(8,128)}, u32[]{:S(2)}) copy-start(s32[8,256]{1,0:T(8,128)} %recharge_ref.3) | copy-start | bytes 24580

commit v9 on v8

--- a/solution.py
+++ b/solution.py
@@ -238,8 +238,9 @@
 def odd_ones(device):
     return ((device ^ (device >> 1) ^ (device >> 2) ^ (device >> 3)) & 1) == 1
 
-def pack_kernel(salt_ref, recharge_ref, cond_ref, codes_ref, block_ref, inner_ref, relay_ref, kept_ref, flat_ref, turn_ref):
+def pack_kernel(salt_ref, recharge_ref, cond_ref, codes_ref, block_ref, inner_ref, relay_ref, kept_ref, wet_ref, flat_ref, turn_ref):
     kept_ref[...] = salt_ref[...]
+    wet_ref[...] = recharge_ref[...]
     device = lax.axis_index("gx")
     even = (device & 1) == 0
     for j in range(2):
@@ -312,11 +313,13 @@
 def lower_of(cell):
     return pltpu.roll(cell, 7, 0)
 
-def sides_kernel(salt_ref, side_ref):
+def sides_kernel(salt_ref, recharge_ref, side_ref, dilution_ref):
     layer, column = iotas((8, 256))
     cells = [salt_ref[:, x, :] for x in range(8)]
     for x in range(8):
         cell = cells[x]
+        wet = recharge_ref[x : x + 1, :].astype(jnp.float32)
+        dilution_ref[x] = jnp.where(layer == 0, freshening * wet * cell, 0.0)
         ahead = jnp.where(layer < 7, lower_of(cell), 0.0) - cell
         half = 0.5 * slope_of(jnp.where(layer > 0, upper_of(ahead), cell), ahead)
         side_ref[0, x] = cell + half
@@ -333,7 +336,7 @@
             side_ref[7, x] = cell - half
 
 def step_kernel(
-    near_ref, far_ref, first_ref, second_ref, side_ref, salt_ref, recharge_ref, tendency_ref, head_ref, fine_ref, coarse_ref, ring_ref, wide_ref
+    near_ref, far_ref, first_ref, second_ref, side_ref, dilution_ref, salt_ref, tendency_ref, head_ref, fine_ref, coarse_ref, ring_ref, wide_ref
 ):
     device = lax.axis_index("gx")
     sub, lane = iotas((8, 128))
@@ -637,9 +640,7 @@
         face = faces_s[x // 4]
         flux_s = face * jnp.where(face > 0, side_ref[4, x], side_ref[5, x])
         change = change + (flux_n - flux_s)
-        wet = recharge_ref[x : x + 1, :].astype(jnp.float32)
-        dilution = jnp.where(layer == 0, freshening * wet * cells[x + 2], 0.0)
-        tendency_ref[:, x, :] = -step * change - step * dilution
+        tendency_ref[:, x, :] = -step * (change + dilution_ref[x])
 
     own = 8 * device + ((lane & 31) >> 2)
     for j in range(4):
@@ -650,16 +651,17 @@
 
 def local_small(salt, recharge, conductivity, codes):
     vmem = pl.BlockSpec(memory_space=pltpu.VMEM)
-    block, inner, relay, kept = pl.pallas_call(
+    block, inner, relay, kept, wet = pl.pallas_call(
         pack_kernel,
         out_shape=(
             pltpu.VMEM((MAIN + SMALL + COLUMNS, 128), jnp.float32),
             pltpu.VMEM((COLUMNS, 128), jnp.float32),
             pltpu.VMEM((8, 128), jnp.float32),
             pltpu.VMEM(salt.shape, jnp.float32),
+            pltpu.VMEM(recharge.shape, jnp.int32),
         ),
         in_specs=[vmem] * 4,
-        out_specs=(vmem,) * 4,
+        out_specs=(vmem,) * 5,
         scratch_shapes=[pltpu.VMEM((2, 64, 128), jnp.float32), pltpu.VMEM((32, 128), jnp.float32)],
         name="pack",
     )(salt, recharge, conductivity, codes)
@@ -688,14 +690,14 @@
         [block[: 4 * MAIN], other[: 4 * MAIN], small(block, 4), small(other, 4), columns(other, 4), inner]
     )
     other = swapped(block, 3)
-    sides = pl.pallas_call(
+    sides, dilution = pl.pallas_call(
         sides_kernel,
-        out_shape=pltpu.VMEM((8, 8, 8, 256), jnp.float32),
-        in_specs=[vmem],
-        out_specs=vmem,
+        out_shape=(pltpu.VMEM((8, 8, 8, 256), jnp.float32), pltpu.VMEM((8, 8, 256), jnp.float32)),
+        in_specs=[vmem] * 2,
+        out_specs=(vmem,) * 2,
         cost_estimate=pl.CostEstimate(flops=1 << 20, bytes_accessed=1 << 20, transcendentals=0),
         name="sides",
-    )(pltpu.with_memory_space_constraint(kept, pltpu.VMEM))
+    )(*(pltpu.with_memory_space_constraint(array, pltpu.VMEM) for array in (kept, wet)))
     return pl.pallas_call(
         step_kernel,
         out_shape=(
@@ -712,7 +714,7 @@
         ],
         compiler_params=pltpu.CompilerParams(vmem_limit_bytes=16 * 1024 * 1024),
         name="step",
-    )(block, other, first, second, sides, kept, recharge)
+    )(block, other, first, second, sides, dilution, kept)
 
 def local(salt, recharge, conductivity, codes):
     small = (

time: 18.3 us -> 18.3 us (level)
  no operation moved by 1% of the time
where the time goes in v9:
time: 18.3 us; the launch traced here: 18.1 us
  starting transfers between devices  7.91 us (43%)
  waiting for transfers between devices  5.72 us (31%)
  Pallas kernels  3.75 us (20%)
  between operations  0.68 us (4%)
    ppermute x4, starting transfers between devices, swapped(): return lax.ppermute(array, 'gx', pairs)  7.91 us
    ppermute x4, waiting for transfers between devices, swapped(): return lax.ppermute(array, 'gx', pairs)  5.72 us
    pallas_call x1, Pallas kernels, local_small(): pl.pallas_call(step_kernel, out_shape=(jax.ShapeDtypeStruct(salt.shape, j...  2.34 us
    pallas_call x1, Pallas kernels, local_small(): pl.pallas_call(pack_kernel, out_shape=(pltpu.VMEM((MAIN + SMALL + COLUMNS...  1.06 us
  transfers between devices with their start and end apart: 4, of which 4 were waited for; matrix products, arithmetic and copies ran while one was open for 0% of the time, Pallas kernels for 2%

profile of v9, /device:TPU:0, one launch (start us, length us, event | category | flops | bytes accessed | tf_op | source)
XLA Modules:
  0.0 18.1 jit_solution(3701231914189730235)
XLA Ops:
  0.6 1.1 %pack.1 = (f32[56,128]{1,0:T(8,128)S(1)}, f32[32,128]{1,0:T(8,128)S(1)}, f32[8,128]{1,0:T(8,128)S(1)}, f32[8,8,256]{2,1,0:T(8,128)S(1)}, s32[8,256]{1,0:T(8,128)S(1)}) custom-call(f32[8,8,256]{2,1,0:T(8,128)} %salt_ref.1, s32[8,256]{1,0:T(8,128)} %recharge_ref.1, f32[8,4,32]{2,1,0:T(4,128)} %cond_ref.1, s32[4,32]{1,0:T(4,128)} %codes_ref.1), custom_call_target="tpu_custom_call" | custom-call | tf_op jit(solution)/shard_map/pack/pallas_call | solution.py:654
  1.7 3.5 %collective-permute-start = (f32[56,128]{1,0:T(8,128)S(1)}, f32[56,128]{1,0:T(8,128)S(1)}, u32[]{:S(2)}, u32[]{:S(2)}) collective-permute-start(f32[56,128]{1,0:T(8,128)S(1)} %get-tuple-element.9), channel_id=1, source_target_pairs={{0,9},{1,2},{2,1},{3,10},{4,7},{5,12},{6,15},{7,4},{8,11},{9,0},{1... | collective-permute-start | bytes 86024 | tf_op jit(solution)/shard_map/ppermute | solution.py:671
  5.2 1.6 %collective-permute-done.first_ref = f32[56,128]{1,0:T(8,128)S(1)} collective-permute-done((f32[56,128]{1,0:T(8,128)S(1)}, f32[56,128]{1,0:T(8,128)S(1)}, u32[]{:S(2)}, u32[]{:S(2)}) %collective-permute-start) | collective-permute-done | bytes 28704 | tf_op jit(solution)/shard_map/ppermute | solution.py:671
  6.8 1.9 %collective-permute-start.1 = (f32[72,128]{1,0:T(8,128)S(1)}, f32[72,128]{1,0:T(8,128)S(1)}, u32[]{:S(2)}, u32[]{:S(2)}) collective-permute-start(f32[72,128]{1,0:T(8,128)S(1)} %pad_maximum_fusion), channel_id=1, source_target_pairs={{0,3},{1,8},{2,11},{3,0},{4,13},{5,6},{6,5},{7,14},{8,1},{9,10},{1... | collective-permute-start | bytes 110600 | tf_op jit(solution)/shard_map/ppermute | solution.py:671
  8.7 1.6 %collective-permute-done.1.second_ref = f32[72,128]{1,0:T(8,128)S(1)} collective-permute-done((f32[72,128]{1,0:T(8,128)S(1)}, f32[72,128]{1,0:T(8,128)S(1)}, u32[]{:S(2)}, u32[]{:S(2)}) %collective-permute-start.1) | collective-permute-done | bytes 36896 | tf_op jit(solution)/shard_map/ppermute | solution.py:671
  10.3 1.9 %collective-permute-start.2 = (f32[104,128]{1,0:T(8,128)S(1)}, f32[104,128]{1,0:T(8,128)S(1)}, u32[]{:S(2)}, u32[]{:S(2)}) collective-permute-start(f32[104,128]{1,0:T(8,128)S(1)} %get-tuple-element.16), channel_id=1, source_target_pairs={{0,5},{1,4},{2,7},{3,6},{4,1},{5,0},{6,3},{7,2},{8,13},{9,12},{10,... | collective-permute-start | bytes 159752 | tf_op jit(solution)/shard_map/ppermute | solution.py:671
  12.3 1.9 %collective-permute-done.2 = f32[104,128]{1,0:T(8,128)S(1)} collective-permute-done((f32[104,128]{1,0:T(8,128)S(1)}, f32[104,128]{1,0:T(8,128)S(1)}, u32[]{:S(2)}, u32[]{:S(2)}) %collective-permute-start.2) | collective-permute-done | bytes 53280 | tf_op jit(solution)/shard_map/ppermute | solution.py:671
  14.2 0.6 %collective-permute-start.3 = (f32[208,128]{1,0:T(8,128)S(1)}, f32[208,128]{1,0:T(8,128)S(1)}, u32[]{:S(2)}, u32[]{:S(2)}) collective-permute-start(f32[208,128]{1,0:T(8,128)S(1)} %constant_dynamic-update-slice_fusion.5.near_ref), channel_id=1, source_target_pairs={{0,1},{1,0},{2,3},{3,2},{4,5},{5,4},{6,7},{7,6},{8,9},{9,8},{10,11... | collective-permute-start | bytes 319496 | tf_op jit(solution)/shard_map/ppermute | solution.py:671
  14.8 0.4 %sides.1 = (f32[8,8,8,256]{3,2,1,0:T(8,128)S(1)}, f32[8,8,256]{2,1,0:T(8,128)S(1)}) custom-call(f32[8,8,256]{2,1,0:T(8,128)S(1)} %get-tuple-element.12.salt_ref, s32[8,256]{1,0:T(8,128)S(1)} %get-tuple-element.13.recharge_ref), custom_call_target="tpu_custom_call" | custom-call | flops 1048576 | bytes 1048576 | tf_op jit(solution)/shard_map/sides/pallas_call | solution.py:693
  15.2 0.6 %collective-permute-done.3.far_ref = f32[208,128]{1,0:T(8,128)S(1)} collective-permute-done((f32[208,128]{1,0:T(8,128)S(1)}, f32[208,128]{1,0:T(8,128)S(1)}, u32[]{:S(2)}, u32[]{:S(2)}) %collective-permute-start.3) | collective-permute-done | bytes 106528 | tf_op jit(solution)/shard_map/ppermute | solution.py:671
  15.8 2.3 %step.1 = (f32[8,8,256]{2,1,0:T(8,128)}, f32[8,4,32]{2,1,0:T(4,128)}) custom-call(f32[208,128]{1,0:T(8,128)S(1)} %constant_dynamic-update-slice_fusion.5.near_ref, f32[208,128]{1,0:T(8,128)S(1)} %collective-permute-done.3.far_ref, f32[56,128]{1,0:T(8,128)S(1)} %collective-permute-done.first_ref, f32[72,128]{1,0:T(8,128)S(1)} %collective-permute-done.1.second_ref, ...), custom_call_target="tpu_custom_call" | custom-call | tf_op jit(solution)/shard_map/step/pallas_call | solution.py:701
  (13 shorter events, 0.0 us)
Async XLA Ops:
  1.7 5.1 %collective-permute-start = (f32[56,128]{1,0:T(8,128)S(1)}, f32[56,128]{1,0:T(8,128)S(1)}, u32[]{:S(2)}, u32[]{:S(2)}) collective-permute-start(f32[56,128]{1,0:T(8,128)S(1)} %get-tuple-element.9), channel_id=1, source_target_pairs={{0,9},{1,2},{2,1},{3,10},{4,7},{5,12},{6,15},{7,4},{8,11},{9,0},{1... | collective-permute-start | bytes 86024 | tf_op jit(solution)/shard_map/ppermute | solution.py:671
  6.8 3.5 %collective-permute-start.1 = (f32[72,128]{1,0:T(8,128)S(1)}, f32[72,128]{1,0:T(8,128)S(1)}, u32[]{:S(2)}, u32[]{:S(2)}) collective-permute-start(f32[72,128]{1,0:T(8,128)S(1)} %pad_maximum_fusion), channel_id=1, source_target_pairs={{0,3},{1,8},{2,11},{3,0},{4,13},{5,6},{6,5},{7,14},{8,1},{9,10},{1... | collective-permute-start | bytes 110600 | tf_op jit(solution)/shard_map/ppermute | solution.py:671
  10.3 3.8 %collective-permute-start.2 = (f32[104,128]{1,0:T(8,128)S(1)}, f32[104,128]{1,0:T(8,128)S(1)}, u32[]{:S(2)}, u32[]{:S(2)}) collective-permute-start(f32[104,128]{1,0:T(8,128)S(1)} %get-tuple-element.16), channel_id=1, source_target_pairs={{0,5},{1,4},{2,7},{3,6},{4,1},{5,0},{6,3},{7,2},{8,13},{9,12},{10,... | collective-permute-start | bytes 159752 | tf_op jit(solution)/shard_map/ppermute | solution.py:671
  14.2 1.6 %collective-permute-start.3 = (f32[208,128]{1,0:T(8,128)S(1)}, f32[208,128]{1,0:T(8,128)S(1)}, u32[]{:S(2)}, u32[]{:S(2)}) collective-permute-start(f32[208,128]{1,0:T(8,128)S(1)} %constant_dynamic-update-slice_fusion.5.near_ref), channel_id=1, source_target_pairs={{0,1},{1,0},{2,3},{3,2},{4,5},{5,4},{6,7},{7,6},{8,9},{9,8},{10,11... | collective-permute-start | bytes 319496 | tf_op jit(solution)/shard_map/ppermute | solution.py:671

commit v10 on v9

--- a/solution.py
+++ b/solution.py
@@ -432,7 +432,8 @@
             for number, face in enumerate(six):
                 weight_ref[number, k] = weight * face
             weight_ref[6, k] = diag * (1.0 / relax_weight)
-            weight_ref[7, k] = weight
+            if side == 2:
+                weight_ref[7, k] = weight
             weights.append(weight)
         return (face_w, face_e, face_s, face_n, face_d), weights
 
@@ -504,9 +505,7 @@
         pull = faces[4][k] * below
         source = jnp.where(top, recharge_rate * wet_frac[k] + river_head * river[k], 0.0)
         fine_ref[8, k] = weights[k] * (upper_of(pull) - pull + source)
-        fine_ref[9, k] = below
-        for number, face in enumerate(faces):
-            fine_ref[10 + number, k] = face[k]
+        fine_ref[7, k] = below
     coefficients([0.25 * c for c in pair_sums(cond)], pair_sums(penalty), 2, 4.0 * vertical_ratio, coarse_ref)
     for number in range(6):
         cells = [coarse_ref[number, k] for k in range(4)]
@@ -553,10 +552,11 @@
         here = head[k]
         west, east = west_of(head, k, 4) - here, here - east_of(head, k, 4)
         south, north = south_of(head, k, 4) - here, here - north_of(head, k, 4)
-        vel_x = 0.5 * (fine_ref[10, k] * west + fine_ref[11, k] * east)
-        vel_y = 0.5 * (fine_ref[12, k] * south + fine_ref[13, k] * north)
-        flow_d = fine_ref[14, k] * (here - lower_of(here) + fine_ref[9, k])
-        vel_z = 0.5 * (upper_of(flow_d) + flow_d)
+        scale = 0.5 * fine_ref[6, k]
+        vel_x = scale * (fine_ref[0, k] * west + fine_ref[1, k] * east)
+        vel_y = scale * (fine_ref[2, k] * south + fine_ref[3, k] * north)
+        flow_d = scale * fine_ref[5, k] * (here - lower_of(here) + fine_ref[7, k])
+        vel_z = upper_of(flow_d) + flow_d
         wide_ref[0, k] = vel_x
         wide_ref[1, k] = vel_y
         wide_ref[2, k] = vel_z
@@ -707,7 +707,7 @@
         in_specs=[vmem] * 7,
         out_specs=(vmem,) * 2,
         scratch_shapes=[
-            pltpu.VMEM((15, 16, 8, 128), jnp.float32),
+            pltpu.VMEM((9, 16, 8, 128), jnp.float32),
             pltpu.VMEM((9, 4, 8, 128), jnp.float32),
             pltpu.VMEM((9, 8, 8, 128), jnp.float32),
             pltpu.VMEM((3, 16, 8, 128), jnp.float32),

time: 18.3 us -> 18.3 us (level)
  no operation moved by 1% of the time
where the time goes in v10:
time: 18.3 us; the launch traced here: 18.1 us
  starting transfers between devices  7.91 us (43%)
  waiting for transfers between devices  5.72 us (31%)
  Pallas kernels  3.73 us (20%)
  between operations  0.68 us (4%)
    ppermute x4, starting transfers between devices, swapped(): return lax.ppermute(array, 'gx', pairs)  7.91 us
    ppermute x4, waiting for transfers between devices, swapped(): return lax.ppermute(array, 'gx', pairs)  5.72 us
    pallas_call x1, Pallas kernels, local_small(): pl.pallas_call(step_kernel, out_shape=(jax.ShapeDtypeStruct(salt.shape, j...  2.32 us
    pallas_call x1, Pallas kernels, local_small(): pl.pallas_call(pack_kernel, out_shape=(pltpu.VMEM((MAIN + SMALL + COLUMNS...  1.06 us
  transfers between devices with their start and end apart: 4, of which 4 were waited for; matrix products, arithmetic and copies ran while one was open for 0% of the time, Pallas kernels for 2%

profile of v10, /device:TPU:0, one launch (start us, length us, event | category | flops | bytes accessed | tf_op | source)
XLA Modules:
  0.0 18.1 jit_solution(6079479728539760913)
XLA Ops:
  0.6 1.1 %pack.1 = (f32[56,128]{1,0:T(8,128)S(1)}, f32[32,128]{1,0:T(8,128)S(1)}, f32[8,128]{1,0:T(8,128)S(1)}, f32[8,8,256]{2,1,0:T(8,128)S(1)}, s32[8,256]{1,0:T(8,128)S(1)}) custom-call(f32[8,8,256]{2,1,0:T(8,128)} %salt_ref.1, s32[8,256]{1,0:T(8,128)} %recharge_ref.1, f32[8,4,32]{2,1,0:T(4,128)} %cond_ref.1, s32[4,32]{1,0:T(4,128)} %codes_ref.1), custom_call_target="tpu_custom_call" | custom-call | tf_op jit(solution)/shard_map/pack/pallas_call | solution.py:654
  1.7 3.5 %collective-permute-start = (f32[56,128]{1,0:T(8,128)S(1)}, f32[56,128]{1,0:T(8,128)S(1)}, u32[]{:S(2)}, u32[]{:S(2)}) collective-permute-start(f32[56,128]{1,0:T(8,128)S(1)} %get-tuple-element.9), channel_id=1, source_target_pairs={{0,9},{1,2},{2,1},{3,10},{4,7},{5,12},{6,15},{7,4},{8,11},{9,0},{1... | collective-permute-start | bytes 86024 | tf_op jit(solution)/shard_map/ppermute | solution.py:671
  5.2 1.6 %collective-permute-done.first_ref = f32[56,128]{1,0:T(8,128)S(1)} collective-permute-done((f32[56,128]{1,0:T(8,128)S(1)}, f32[56,128]{1,0:T(8,128)S(1)}, u32[]{:S(2)}, u32[]{:S(2)}) %collective-permute-start) | collective-permute-done | bytes 28704 | tf_op jit(solution)/shard_map/ppermute | solution.py:671
  6.8 1.9 %collective-permute-start.1 = (f32[72,128]{1,0:T(8,128)S(1)}, f32[72,128]{1,0:T(8,128)S(1)}, u32[]{:S(2)}, u32[]{:S(2)}) collective-permute-start(f32[72,128]{1,0:T(8,128)S(1)} %pad_maximum_fusion), channel_id=1, source_target_pairs={{0,3},{1,8},{2,11},{3,0},{4,13},{5,6},{6,5},{7,14},{8,1},{9,10},{1... | collective-permute-start | bytes 110600 | tf_op jit(solution)/shard_map/ppermute | solution.py:671
  8.7 1.6 %collective-permute-done.1.second_ref = f32[72,128]{1,0:T(8,128)S(1)} collective-permute-done((f32[72,128]{1,0:T(8,128)S(1)}, f32[72,128]{1,0:T(8,128)S(1)}, u32[]{:S(2)}, u32[]{:S(2)}) %collective-permute-start.1) | collective-permute-done | bytes 36896 | tf_op jit(solution)/shard_map/ppermute | solution.py:671
  10.3 1.9 %collective-permute-start.2 = (f32[104,128]{1,0:T(8,128)S(1)}, f32[104,128]{1,0:T(8,128)S(1)}, u32[]{:S(2)}, u32[]{:S(2)}) collective-permute-start(f32[104,128]{1,0:T(8,128)S(1)} %get-tuple-element.16), channel_id=1, source_target_pairs={{0,5},{1,4},{2,7},{3,6},{4,1},{5,0},{6,3},{7,2},{8,13},{9,12},{10,... | collective-permute-start | bytes 159752 | tf_op jit(solution)/shard_map/ppermute | solution.py:671
  12.3 1.9 %collective-permute-done.2 = f32[104,128]{1,0:T(8,128)S(1)} collective-permute-done((f32[104,128]{1,0:T(8,128)S(1)}, f32[104,128]{1,0:T(8,128)S(1)}, u32[]{:S(2)}, u32[]{:S(2)}) %collective-permute-start.2) | collective-permute-done | bytes 53280 | tf_op jit(solution)/shard_map/ppermute | solution.py:671
  14.2 0.6 %collective-permute-start.3 = (f32[208,128]{1,0:T(8,128)S(1)}, f32[208,128]{1,0:T(8,128)S(1)}, u32[]{:S(2)}, u32[]{:S(2)}) collective-permute-start(f32[208,128]{1,0:T(8,128)S(1)} %constant_dynamic-update-slice_fusion.5.near_ref), channel_id=1, source_target_pairs={{0,1},{1,0},{2,3},{3,2},{4,5},{5,4},{6,7},{7,6},{8,9},{9,8},{10,11... | collective-permute-start | bytes 319496 | tf_op jit(solution)/shard_map/ppermute | solution.py:671
  14.8 0.4 %sides.1 = (f32[8,8,8,256]{3,2,1,0:T(8,128)S(1)}, f32[8,8,256]{2,1,0:T(8,128)S(1)}) custom-call(f32[8,8,256]{2,1,0:T(8,128)S(1)} %get-tuple-element.12.salt_ref, s32[8,256]{1,0:T(8,128)S(1)} %get-tuple-element.13.recharge_ref), custom_call_target="tpu_custom_call" | custom-call | flops 1048576 | bytes 1048576 | tf_op jit(solution)/shard_map/sides/pallas_call | solution.py:693
  15.2 0.6 %collective-permute-done.3.far_ref = f32[208,128]{1,0:T(8,128)S(1)} collective-permute-done((f32[208,128]{1,0:T(8,128)S(1)}, f32[208,128]{1,0:T(8,128)S(1)}, u32[]{:S(2)}, u32[]{:S(2)}) %collective-permute-start.3) | collective-permute-done | bytes 106528 | tf_op jit(solution)/shard_map/ppermute | solution.py:671
  15.8 2.3 %step.1 = (f32[8,8,256]{2,1,0:T(8,128)}, f32[8,4,32]{2,1,0:T(4,128)}) custom-call(f32[208,128]{1,0:T(8,128)S(1)} %constant_dynamic-update-slice_fusion.5.near_ref, f32[208,128]{1,0:T(8,128)S(1)} %collective-permute-done.3.far_ref, f32[56,128]{1,0:T(8,128)S(1)} %collective-permute-done.first_ref, f32[72,128]{1,0:T(8,128)S(1)} %collective-permute-done.1.second_ref, ...), custom_call_target="tpu_custom_call" | custom-call | tf_op jit(solution)/shard_map/step/pallas_call | solution.py:701
  (13 shorter events, 0.0 us)
Async XLA Ops:
  1.7 5.1 %collective-permute-start = (f32[56,128]{1,0:T(8,128)S(1)}, f32[56,128]{1,0:T(8,128)S(1)}, u32[]{:S(2)}, u32[]{:S(2)}) collective-permute-start(f32[56,128]{1,0:T(8,128)S(1)} %get-tuple-element.9), channel_id=1, source_target_pairs={{0,9},{1,2},{2,1},{3,10},{4,7},{5,12},{6,15},{7,4},{8,11},{9,0},{1... | collective-permute-start | bytes 86024 | tf_op jit(solution)/shard_map/ppermute | solution.py:671
  6.8 3.5 %collective-permute-start.1 = (f32[72,128]{1,0:T(8,128)S(1)}, f32[72,128]{1,0:T(8,128)S(1)}, u32[]{:S(2)}, u32[]{:S(2)}) collective-permute-start(f32[72,128]{1,0:T(8,128)S(1)} %pad_maximum_fusion), channel_id=1, source_target_pairs={{0,3},{1,8},{2,11},{3,0},{4,13},{5,6},{6,5},{7,14},{8,1},{9,10},{1... | collective-permute-start | bytes 110600 | tf_op jit(solution)/shard_map/ppermute | solution.py:671
  10.3 3.8 %collective-permute-start.2 = (f32[104,128]{1,0:T(8,128)S(1)}, f32[104,128]{1,0:T(8,128)S(1)}, u32[]{:S(2)}, u32[]{:S(2)}) collective-permute-start(f32[104,128]{1,0:T(8,128)S(1)} %get-tuple-element.16), channel_id=1, source_target_pairs={{0,5},{1,4},{2,7},{3,6},{4,1},{5,0},{6,3},{7,2},{8,13},{9,12},{10,... | collective-permute-start | bytes 159752 | tf_op jit(solution)/shard_map/ppermute | solution.py:671
  14.2 1.6 %collective-permute-start.3 = (f32[208,128]{1,0:T(8,128)S(1)}, f32[208,128]{1,0:T(8,128)S(1)}, u32[]{:S(2)}, u32[]{:S(2)}) collective-permute-start(f32[208,128]{1,0:T(8,128)S(1)} %constant_dynamic-update-slice_fusion.5.near_ref), channel_id=1, source_target_pairs={{0,1},{1,0},{2,3},{3,2},{4,5},{5,4},{6,7},{7,6},{8,9},{9,8},{10,11... | collective-permute-start | bytes 319496 | tf_op jit(solution)/shard_map/ppermute | solution.py:671

commit v11 on v10

--- a/solution.py
+++ b/solution.py
@@ -437,10 +437,10 @@
             weights.append(weight)
         return (face_w, face_e, face_s, face_n, face_d), weights
 
-    def step(here, west, east, south, north, weights):
+    def step(here, west, east, south, north, weights, kept=1.0 - relax_weight):
         pairs = (west, east, south, north, upper_of(here), lower_of(here))
         terms = [weights(number) * pair for number, pair in enumerate(pairs)]
-        base = (1.0 - relax_weight) * here + weights(8)
+        base = kept * here + weights(8)
         return ((terms[0] + terms[1]) + (terms[2] + terms[3])) + ((terms[4] + terms[5]) + base)
 
     def edges_of(cells):
@@ -451,7 +451,7 @@
             [pltpu.roll(cells[i], 120, 1) for i in range(4)],
         )
 
-    def relaxed(cells, edges):
+    def relaxed(cells, edges, kept=1.0 - relax_weight):
         out = []
         for k in range(16):
             j, i = k // 4, k % 4
@@ -459,7 +459,7 @@
             east = cells[k + 1] if i < 3 else edges[1][j]
             south = cells[k - 4] if j > 0 else edges[2][i]
             north = cells[k + 4] if j < 3 else edges[3][i]
-            out.append(step(cells[k], west, east, south, north, lambda number, k=k: fine_ref[number, k]))
+            out.append(step(cells[k], west, east, south, north, lambda number, k=k: fine_ref[number, k], kept))
         return out
 
     ring = [(j, i) for j in range(-1, 3) for i in range(-1, 3) if (j in (0, 1)) != (i in (0, 1))]
@@ -517,8 +517,8 @@
         for sweep in range(SMOOTH):
             head = [fine_ref[8, k] for k in range(16)] if head is None else relaxed(head, edges_of(head))
         edges = edges_of(head)
-        ahead = relaxed(head, edges)
-        resid = pair_sums([(ahead[k] - head[k]) * fine_ref[6, k] for k in range(16)])
+        change = relaxed(head, edges, -relax_weight)
+        resid = pair_sums([change[k] * fine_ref[6, k] for k in range(16)])
         correction = []
         for k in range(4):
             correction.append(coarse_ref[7, k] * resid[k])

time: 18.3 us -> 18.3 us (level)
  no operation moved by 1% of the time
where the time goes in v11:
time: 18.3 us; the launch traced here: 18.1 us
  starting transfers between devices  7.91 us (43%)
  waiting for transfers between devices  5.72 us (31%)
  Pallas kernels  3.73 us (20%)
  between operations  0.68 us (4%)
    ppermute x4, starting transfers between devices, swapped(): return lax.ppermute(array, 'gx', pairs)  7.91 us
    ppermute x4, waiting for transfers between devices, swapped(): return lax.ppermute(array, 'gx', pairs)  5.72 us
    pallas_call x1, Pallas kernels, local_small(): pl.pallas_call(step_kernel, out_shape=(jax.ShapeDtypeStruct(salt.shape, j...  2.32 us
    pallas_call x1, Pallas kernels, local_small(): pl.pallas_call(pack_kernel, out_shape=(pltpu.VMEM((MAIN + SMALL + COLUMNS...  1.06 us
  transfers between devices with their start and end apart: 4, of which 4 were waited for; matrix products, arithmetic and copies ran while one was open for 0% of the time, Pallas kernels for 2%

profile of v11, /device:TPU:0, one launch (start us, length us, event | category | flops | bytes accessed | tf_op | source)
XLA Modules:
  0.0 18.1 jit_solution(13441258689264613285)
XLA Ops:
  0.6 1.1 %pack.1 = (f32[56,128]{1,0:T(8,128)S(1)}, f32[32,128]{1,0:T(8,128)S(1)}, f32[8,128]{1,0:T(8,128)S(1)}, f32[8,8,256]{2,1,0:T(8,128)S(1)}, s32[8,256]{1,0:T(8,128)S(1)}) custom-call(f32[8,8,256]{2,1,0:T(8,128)} %salt_ref.1, s32[8,256]{1,0:T(8,128)} %recharge_ref.1, f32[8,4,32]{2,1,0:T(4,128)} %cond_ref.1, s32[4,32]{1,0:T(4,128)} %codes_ref.1), custom_call_target="tpu_custom_call" | custom-call | tf_op jit(solution)/shard_map/pack/pallas_call | solution.py:654
  1.7 3.5 %collective-permute-start = (f32[56,128]{1,0:T(8,128)S(1)}, f32[56,128]{1,0:T(8,128)S(1)}, u32[]{:S(2)}, u32[]{:S(2)}) collective-permute-start(f32[56,128]{1,0:T(8,128)S(1)} %get-tuple-element.9), channel_id=1, source_target_pairs={{0,9},{1,2},{2,1},{3,10},{4,7},{5,12},{6,15},{7,4},{8,11},{9,0},{1... | collective-permute-start | bytes 86024 | tf_op jit(solution)/shard_map/ppermute | solution.py:671
  5.2 1.6 %collective-permute-done.first_ref = f32[56,128]{1,0:T(8,128)S(1)} collective-permute-done((f32[56,128]{1,0:T(8,128)S(1)}, f32[56,128]{1,0:T(8,128)S(1)}, u32[]{:S(2)}, u32[]{:S(2)}) %collective-permute-start) | collective-permute-done | bytes 28704 | tf_op jit(solution)/shard_map/ppermute | solution.py:671
  6.8 1.9 %collective-permute-start.1 = (f32[72,128]{1,0:T(8,128)S(1)}, f32[72,128]{1,0:T(8,128)S(1)}, u32[]{:S(2)}, u32[]{:S(2)}) collective-permute-start(f32[72,128]{1,0:T(8,128)S(1)} %pad_maximum_fusion), channel_id=1, source_target_pairs={{0,3},{1,8},{2,11},{3,0},{4,13},{5,6},{6,5},{7,14},{8,1},{9,10},{1... | collective-permute-start | bytes 110600 | tf_op jit(solution)/shard_map/ppermute | solution.py:671
  8.7 1.6 %collective-permute-done.1.second_ref = f32[72,128]{1,0:T(8,128)S(1)} collective-permute-done((f32[72,128]{1,0:T(8,128)S(1)}, f32[72,128]{1,0:T(8,128)S(1)}, u32[]{:S(2)}, u32[]{:S(2)}) %collective-permute-start.1) | collective-permute-done | bytes 36896 | tf_op jit(solution)/shard_map/ppermute | solution.py:671
  10.3 1.9 %collective-permute-start.2 = (f32[104,128]{1,0:T(8,128)S(1)}, f32[104,128]{1,0:T(8,128)S(1)}, u32[]{:S(2)}, u32[]{:S(2)}) collective-permute-start(f32[104,128]{1,0:T(8,128)S(1)} %get-tuple-element.16), channel_id=1, source_target_pairs={{0,5},{1,4},{2,7},{3,6},{4,1},{5,0},{6,3},{7,2},{8,13},{9,12},{10,... | collective-permute-start | bytes 159752 | tf_op jit(solution)/shard_map/ppermute | solution.py:671
  12.3 1.9 %collective-permute-done.2 = f32[104,128]{1,0:T(8,128)S(1)} collective-permute-done((f32[104,128]{1,0:T(8,128)S(1)}, f32[104,128]{1,0:T(8,128)S(1)}, u32[]{:S(2)}, u32[]{:S(2)}) %collective-permute-start.2) | collective-permute-done | bytes 53280 | tf_op jit(solution)/shard_map/ppermute | solution.py:671
  14.2 0.6 %collective-permute-start.3 = (f32[208,128]{1,0:T(8,128)S(1)}, f32[208,128]{1,0:T(8,128)S(1)}, u32[]{:S(2)}, u32[]{:S(2)}) collective-permute-start(f32[208,128]{1,0:T(8,128)S(1)} %constant_dynamic-update-slice_fusion.5.near_ref), channel_id=1, source_target_pairs={{0,1},{1,0},{2,3},{3,2},{4,5},{5,4},{6,7},{7,6},{8,9},{9,8},{10,11... | collective-permute-start | bytes 319496 | tf_op jit(solution)/shard_map/ppermute | solution.py:671
  14.8 0.4 %sides.1 = (f32[8,8,8,256]{3,2,1,0:T(8,128)S(1)}, f32[8,8,256]{2,1,0:T(8,128)S(1)}) custom-call(f32[8,8,256]{2,1,0:T(8,128)S(1)} %get-tuple-element.12.salt_ref, s32[8,256]{1,0:T(8,128)S(1)} %get-tuple-element.13.recharge_ref), custom_call_target="tpu_custom_call" | custom-call | flops 1048576 | bytes 1048576 | tf_op jit(solution)/shard_map/sides/pallas_call | solution.py:693
  15.2 0.6 %collective-permute-done.3.far_ref = f32[208,128]{1,0:T(8,128)S(1)} collective-permute-done((f32[208,128]{1,0:T(8,128)S(1)}, f32[208,128]{1,0:T(8,128)S(1)}, u32[]{:S(2)}, u32[]{:S(2)}) %collective-permute-start.3) | collective-permute-done | bytes 106528 | tf_op jit(solution)/shard_map/ppermute | solution.py:671
  15.8 2.3 %step.1 = (f32[8,8,256]{2,1,0:T(8,128)}, f32[8,4,32]{2,1,0:T(4,128)}) custom-call(f32[208,128]{1,0:T(8,128)S(1)} %constant_dynamic-update-slice_fusion.5.near_ref, f32[208,128]{1,0:T(8,128)S(1)} %collective-permute-done.3.far_ref, f32[56,128]{1,0:T(8,128)S(1)} %collective-permute-done.first_ref, f32[72,128]{1,0:T(8,128)S(1)} %collective-permute-done.1.second_ref, ...), custom_call_target="tpu_custom_call" | custom-call | tf_op jit(solution)/shard_map/step/pallas_call | solution.py:701
  (13 shorter events, 0.0 us)
Async XLA Ops:
  1.7 5.1 %collective-permute-start = (f32[56,128]{1,0:T(8,128)S(1)}, f32[56,128]{1,0:T(8,128)S(1)}, u32[]{:S(2)}, u32[]{:S(2)}) collective-permute-start(f32[56,128]{1,0:T(8,128)S(1)} %get-tuple-element.9), channel_id=1, source_target_pairs={{0,9},{1,2},{2,1},{3,10},{4,7},{5,12},{6,15},{7,4},{8,11},{9,0},{1... | collective-permute-start | bytes 86024 | tf_op jit(solution)/shard_map/ppermute | solution.py:671
  6.8 3.5 %collective-permute-start.1 = (f32[72,128]{1,0:T(8,128)S(1)}, f32[72,128]{1,0:T(8,128)S(1)}, u32[]{:S(2)}, u32[]{:S(2)}) collective-permute-start(f32[72,128]{1,0:T(8,128)S(1)} %pad_maximum_fusion), channel_id=1, source_target_pairs={{0,3},{1,8},{2,11},{3,0},{4,13},{5,6},{6,5},{7,14},{8,1},{9,10},{1... | collective-permute-start | bytes 110600 | tf_op jit(solution)/shard_map/ppermute | solution.py:671
  10.3 3.8 %collective-permute-start.2 = (f32[104,128]{1,0:T(8,128)S(1)}, f32[104,128]{1,0:T(8,128)S(1)}, u32[]{:S(2)}, u32[]{:S(2)}) collective-permute-start(f32[104,128]{1,0:T(8,128)S(1)} %get-tuple-element.16), channel_id=1, source_target_pairs={{0,5},{1,4},{2,7},{3,6},{4,1},{5,0},{6,3},{7,2},{8,13},{9,12},{10,... | collective-permute-start | bytes 159752 | tf_op jit(solution)/shard_map/ppermute | solution.py:671
  14.2 1.6 %collective-permute-start.3 = (f32[208,128]{1,0:T(8,128)S(1)}, f32[208,128]{1,0:T(8,128)S(1)}, u32[]{:S(2)}, u32[]{:S(2)}) collective-permute-start(f32[208,128]{1,0:T(8,128)S(1)} %constant_dynamic-update-slice_fusion.5.near_ref), channel_id=1, source_target_pairs={{0,1},{1,0},{2,3},{3,2},{4,5},{5,4},{6,7},{7,6},{8,9},{9,8},{10,11... | collective-permute-start | bytes 319496 | tf_op jit(solution)/shard_map/ppermute | solution.py:671
